TPU v7x, 512 devices: a whole 4x8x8 slice. The times are simulated.
512 devices in a mesh: dp: 8 (over y), tile: 64 (over z, x, core).
Axes of the slice: x: 4, y: 8, z: 8, core: 2. Of those that a mesh axis runs over, the one named last changes fastest.
Arguments:
- hidden: bfloat16 [512, 729, 1152], P(('dp', 'tile')), may hold values from -6 to 6
- norm_gain: float32 [1152], replicated, may hold values from 0.1 to 1.9
- norm_bias: float32 [1152], replicated, may hold values from -3 to 3
- slot_tile: int32 [512], P(('dp', 'tile')), may hold values from -1 to 55, as said below
- block_owner: int32 [8, 4, 27, 9], P('dp'), may hold values from 0 to 1023, as said below
- proj_weight: bfloat16 [3456, 2048], P('tile', 'dp'), may hold values from -0.109375 to 0.109375
- proj_grad: bfloat16 [64, 384, 2048], P('tile', None, 'dp'), may hold values from -0.59765625 to 0.59765625
Outputs:
- projected: bfloat16 [64, 384, 2048], P('tile', None, 'dp')
- weight_grad: float32 [3456, 2048], P('tile', 'dp')
- hidden_grad: bfloat16 [512, 729, 1152], P(('dp', 'tile'))
- gain_grad: float32 [1152], replicated
- bias_grad: float32 [1152], replicated
Inputs may be any that keep to these rules, and one draw needn't show every extreme that they name: `slot_tile`: in each group's 64 * 1 entries (groups in dp order, devices in tile order, then slots) every tile number 0 to 55 stands exactly once and -1 elsewhere. `block_owner`: A value o names owner o // 16 along tile within the group and its slot o % 16. The values of one group are distinct; an owner holds at most 16 blocks and at most 4 blocks of one image, and both bounds are reached in every group.
All inputs are finite; a program needn't handle non-finite values.
Results may differ from a plain program's by a relative error of at most 0.018.
Values may be sent and summed in bfloat16 or wider, within the bound.
No kernel may reach another device: no remote copies, remote signals or barrier semaphores. Data moves between devices by JAX's collectives and lax.ppermute only.
A program may use at most 64 MiB of HBM per device.

v0:
```python
import jax
import jax.numpy as jnp
from jax import lax
from jax.sharding import PartitionSpec as P

GRID = 27
BLOCK = 3
TILES_IMG = 14
IMAGES = 4


epsilon = 1e-06
highest_precision = lax.Precision.HIGHEST


def tile_shape(local_idx):
    tile_scale = jnp.where(local_idx == 0, 1, jnp.where(local_idx < 5, 2, 3)).astype(jnp.int32)
    within = jnp.where(local_idx < 5, local_idx - 1, local_idx - 5)
    tile_row = jnp.where(local_idx == 0, 0, within // tile_scale)
    tile_col = jnp.where(local_idx == 0, 0, within % tile_scale)
    return (tile_scale, tile_row, tile_col)


def pool_matrix(tile_scale, offset, is_live):
    cell_ids = jnp.arange(GRID, dtype=jnp.int32)
    target = (GRID * offset + cell_ids) // tile_scale
    matches = (target[None, :] == cell_ids[:, None]) & is_live
    weight_value = 1.0 / tile_scale.astype(jnp.float32)
    return jnp.where(matches, weight_value, 0.0)


def norm_forward(tokens_in, norm_gain, norm_bias):
    values = tokens_in.astype(jnp.float32)
    centered = values - jnp.mean(values, axis=-1, keepdims=True)
    inverse_scale = lax.rsqrt(jnp.mean(centered * centered, axis=-1, keepdims=True) + epsilon)
    unit_rows = centered * inverse_scale
    return (unit_rows * norm_gain + norm_bias, unit_rows, inverse_scale)


def norm_backward(upstream, unit_rows, inverse_scale, norm_gain):
    scaled = upstream * norm_gain
    width_mean = jnp.mean(scaled, axis=-1, keepdims=True)
    cross_mean = jnp.mean(scaled * unit_rows, axis=-1, keepdims=True)
    return inverse_scale * (scaled - width_mean - unit_rows * cross_mean)


def shards(hidden, norm_gain, norm_bias, slot_tile, block_owner, proj_weight, proj_grad):
    slot_count = hidden.shape[0]
    feature_width = hidden.shape[2]
    peer_count = lax.axis_size("tile")
    block_count = GRID * (GRID // BLOCK)
    capacity = block_count // peer_count + 1
    own_slots = (
        IMAGES * (block_count // peer_count)
        + (IMAGES * (block_count % peer_count) + peer_count - 1) // peer_count
    )
    per_peer = slot_count * capacity
    position_count = peer_count * per_peer
    is_live = slot_tile >= 0
    safe_id = jnp.maximum(slot_tile, 0)
    image_idx = safe_id // TILES_IMG
    tile_scale, tile_row, tile_col = tile_shape(safe_id % TILES_IMG)
    row_pool = jax.vmap(pool_matrix)(tile_scale, tile_row, is_live)
    col_pool = jax.vmap(pool_matrix)(tile_scale, tile_col, is_live)
    normed, unit_rows, inverse_scale = norm_forward(hidden, norm_gain, norm_bias)
    grid_values = normed.reshape(slot_count, GRID, GRID, feature_width)
    row_pooled = jnp.einsum("sra,sabw->srbw", row_pool, grid_values, precision=highest_precision)
    pooled = jnp.einsum("scb,srbw->srcw", col_pool, row_pooled, precision=highest_precision)
    blocks = pooled.astype(jnp.bfloat16).reshape(slot_count, block_count, BLOCK * feature_width)
    row_hit = jnp.sum(row_pool, axis=2) > 0.0
    col_hit = jnp.any(
        (jnp.sum(col_pool, axis=2) > 0.0).reshape(slot_count, GRID // BLOCK, BLOCK), axis=2
    )
    touched = (row_hit[:, :, None] & col_hit[:, None, :]).reshape(slot_count, block_count)
    image_ids = jnp.arange(IMAGES, dtype=jnp.int32)
    owner_table = block_owner.reshape(IMAGES, block_count)
    owner_ids = jnp.sum(
        jnp.where(image_idx[:, None, None] == image_ids[None, :, None], owner_table[None], 0),
        axis=1,
    )
    dest_peer = owner_ids // own_slots
    dest_slot = owner_ids % own_slots
    block_ids = jnp.arange(block_count, dtype=jnp.int32)
    earlier = (dest_peer[:, :, None] == dest_peer[:, None, :]) & touched[:, None, :]
    earlier = earlier & (block_ids[None, None, :] < block_ids[None, :, None])
    rank_within = jnp.sum(earlier.astype(jnp.int32), axis=2)
    slot_ids = jnp.arange(slot_count, dtype=jnp.int32)
    position = dest_peer * per_peer + slot_ids[:, None] * capacity + rank_within
    position_ids = jnp.arange(position_count, dtype=jnp.int32)
    selected = (position[:, :, None] == position_ids[None, None, :]) & touched[:, :, None]
    select_hot = selected.astype(jnp.bfloat16)
    outgoing = jnp.einsum(
        "sbm,sbk->mk", select_hot, blocks, preferred_element_type=jnp.float32
    ).astype(jnp.bfloat16)
    target_code = dest_slot * 3 + tile_scale[:, None]
    labels = jnp.sum(jnp.where(selected, target_code[:, :, None], 0), axis=(0, 1)) - 1
    arrived, arrived_labels = (
        lax.all_to_all(
            outgoing.reshape(peer_count, per_peer, BLOCK * feature_width),
            "tile",
            split_axis=0,
            concat_axis=0,
            tiled=True,
        ),
        lax.all_to_all(
            labels.reshape(peer_count, per_peer), "tile", split_axis=0, concat_axis=0, tiled=True
        ),
    )
    band_ids = jnp.arange(own_slots * 3, dtype=jnp.int32)
    owner_hot = (arrived_labels.reshape(position_count)[None, :] == band_ids[:, None]).astype(
        jnp.bfloat16
    )
    owned_rows = jnp.dot(
        owner_hot,
        arrived.reshape(position_count, BLOCK * feature_width),
        preferred_element_type=jnp.float32,
    )
    owned_rows = owned_rows.reshape(own_slots, 3, BLOCK, feature_width).transpose(0, 2, 1, 3)
    owned_rows = owned_rows.reshape(own_slots * BLOCK, 3 * feature_width).astype(jnp.bfloat16)
    gathered = lax.all_gather(owned_rows, "dp", axis=0, tiled=True)
    upstream = proj_grad[0]
    full_weight = lax.all_gather(proj_weight, "tile", axis=0, tiled=True)
    projected = jnp.dot(gathered, full_weight, preferred_element_type=jnp.float32)
    row_part = lax.dot_general(
        upstream, full_weight, (((1,), (1,)), ((), ())), preferred_element_type=jnp.float32
    )
    weight_grad = lax.psum_scatter(
        lax.dot_general(
            gathered, upstream, (((0,), (0,)), ((), ())), preferred_element_type=jnp.float32
        ),
        "tile",
        scatter_dimension=0,
        tiled=True,
    )
    own_count = own_slots * BLOCK
    summed = lax.psum(row_part.astype(jnp.bfloat16), "dp").astype(jnp.float32)
    own_grad = lax.dynamic_slice_in_dim(
        summed, lax.axis_index("dp") * own_count, own_count, 0
    ).astype(jnp.bfloat16)
    own_grad = own_grad.reshape(own_slots, BLOCK, 3, feature_width).transpose(0, 2, 1, 3)
    own_grad = own_grad.reshape(own_slots * 3, BLOCK * feature_width)
    returning = lax.dot_general(
        owner_hot, own_grad, (((0,), (0,)), ((), ())), preferred_element_type=jnp.float32
    )
    returning = returning.astype(jnp.bfloat16).reshape(peer_count, per_peer, BLOCK * feature_width)
    returned = lax.all_to_all(returning, "tile", split_axis=0, concat_axis=0, tiled=True)
    block_grad = jnp.einsum(
        "sbm,mk->sbk",
        select_hot,
        returned.reshape(position_count, BLOCK * feature_width),
        preferred_element_type=jnp.float32,
    )
    grid_grad = block_grad.reshape(slot_count, GRID, GRID, feature_width)
    col_back = jnp.einsum("scb,srcw->srbw", col_pool, grid_grad, precision=highest_precision)
    token_grad = jnp.einsum("sra,srbw->sabw", row_pool, col_back, precision=highest_precision)
    token_grad = token_grad.reshape(slot_count, GRID * GRID, feature_width)
    hidden_grad = norm_backward(token_grad, unit_rows, inverse_scale, norm_gain).astype(
        jnp.bfloat16
    )
    gain_part = jnp.sum(token_grad * unit_rows, axis=(0, 1))
    bias_part = jnp.sum(token_grad, axis=(0, 1))
    gain_grad, bias_grad = lax.psum((gain_part, bias_part), ("dp", "tile"))
    return (projected.astype(jnp.bfloat16)[None], weight_grad, hidden_grad, gain_grad, bias_grad)


def solution(mesh):
    return jax.shard_map(
        shards,
        mesh=mesh,
        in_specs=(
            P(("dp", "tile"), None, None),
            P(),
            P(),
            P(("dp", "tile")),
            P("dp", None, None, None),
            P("tile", "dp"),
            P("tile", None, "dp"),
        ),
        out_specs=(P("tile", None, "dp"), P("tile", "dp"), P(("dp", "tile"), None, None), P(), P()),
        check_vma=False,
    )
```

profile of v0, /device:TPU:1, one launch (start us, length us, event | category | flops | bytes accessed | tf_op | source)
XLA Modules:
  0.0 642.9 jit_solution(15412709051333515818)
XLA Ops:
  8.0 92.5 %all-gather.6.cloned.1.call-done = bf16[64,54,256]{2,1,0:T(8,128)(2,1)} async-done(((bf16[1,54,256]{2,1,0:T(8,128)(2,1)}), bf16[64,54,256]{2,1,0:T(8,128)(2,1)}) %all-gather.6.cloned.1.call-update) | async-done | bytes 1769488 | tf_op jit(solution)/shard_map/all_gather | solution.py:122
  107.7 4.8 fusion.34
  115.0 6.5 %all-to-all-start = ((s32[64,1,4]{2,1,0:T(1,128)}), s32[64,1,4]{2,1,0:T(1,128)S(1)}, u32[]{:S(2)}, u32[]{:S(2)}) async-start(s32[64,1,4]{2,1,0:T(1,128)} %bitcast.12), calls=%async_computation | async-start | bytes 65536 | tf_op jit(solution)/shard_map/all_to_all | solution.py:105
  121.5 9.3 %all-to-all-done = s32[64,1,4]{2,1,0:T(1,128)S(1)} async-done(((s32[64,1,4]{2,1,0:T(1,128)}), s32[64,1,4]{2,1,0:T(1,128)S(1)}, u32[]{:S(2)}, u32[]{:S(2)}) %all-to-all-start) | async-done | bytes 1056 | tf_op jit(solution)/shard_map/all_to_all | solution.py:105
  132.1 59.0 %all-reduce.5.cloned.1.call-done = bf16[384,3456]{1,0:T(8,128)(2,1)} async-done(((bf16[384,3456]{1,0:T(8,128)(2,1)}), bf16[384,3456]{1,0:T(8,128)(2,1)}) %all-reduce.5.cloned.1.call-update) | async-done | bytes 2654224 | tf_op jit(solution)/shard_map/psum | solution.py:136
  194.4 4.1 reshape.873
  198.5 14.4 %all-to-all-start.2 = ((bf16[64,4,3456]{2,1,0:T(4,128)(2,1)}), bf16[64,4,3456]{2,1,0:T(4,128)(2,1)}, u32[]{:S(2)}, u32[]{:S(2)}) async-start(bf16[64,4,3456]{2,1,0:T(4,128)(2,1)} %reshape.873), calls=%async_computation.2 | async-start | bytes 3538944 | tf_op jit(solution)/shard_map/all_to_all | solution.py:146
  213.9 42.0 %all-to-all-done.2 = bf16[64,4,3456]{2,1,0:T(4,128)(2,1)} async-done(((bf16[64,4,3456]{2,1,0:T(4,128)(2,1)}), bf16[64,4,3456]{2,1,0:T(4,128)(2,1)}, u32[]{:S(2)}, u32[]{:S(2)}) %all-to-all-start.2) | async-done | bytes 1769504 | tf_op jit(solution)/shard_map/all_to_all | solution.py:146
  255.8 3.9 reshape.874
  259.7 3.9 fusion.30
  263.6 5.2 reshape.875
  268.8 6.0 convolution_bitcast_fusion
  274.8 5.8 fusion.87
  280.6 3.9 copy.65
  284.4 4.7 reshape.877
  289.2 3.0 fusion.21
  292.4 4.5 fusion.20
  296.9 4.8 reshape.867
  301.7 7.7 %fusion.11 = f32[27,27,1152]{2,0,1:T(8,128)S(1)} fusion(f32[27,27,1152]{2,1,0:T(8,128)} %reshape.867, f32[]{:T(128)} %bitcast.6, s32[27]{0:T(128)S(1)} %fusion.82, pred[]{:T(512)} %bitcast.5), kind=kOutput, calls=%fused_computation.15 | convolution fusion | flops 272099968 | bytes 6718577 | tf_op jit(solution)/shard_map/sra,sabw->srbw/dot_general | solution.py:67
  309.5 6.1 fusion.23
  321.8 6.7 %all-to-all-start.1 = ((bf16[64,4,3456]{2,1,0:T(4,128)(2,1)}), bf16[64,4,3456]{2,1,0:T(4,128)(2,1)S(1)}, u32[]{:S(2)}, u32[]{:S(2)}) async-start(bf16[64,4,3456]{2,1,0:T(4,128)(2,1)} %reshape.869), calls=%async_computation.1 | async-start | bytes 3538944 | tf_op jit(solution)/shard_map/all_to_all | solution.py:98
  328.6 42.9 %all-to-all-done.1 = bf16[64,4,3456]{2,1,0:T(4,128)(2,1)S(1)} async-done(((bf16[64,4,3456]{2,1,0:T(4,128)(2,1)}), bf16[64,4,3456]{2,1,0:T(4,128)(2,1)S(1)}, u32[]{:S(2)}, u32[]{:S(2)}) %all-to-all-start.1) | async-done | bytes 1769504 | tf_op jit(solution)/shard_map/all_to_all | solution.py:98
  377.1 36.9 %all-gather.4.cloned.1.call-done = bf16[384,3456]{1,0:T(8,128)(2,1)} async-done(((bf16[48,3456]{1,0:T(8,128)(2,1)}), bf16[384,3456]{1,0:T(8,128)(2,1)}) %all-gather.4.cloned.1.call-update) | async-done | bytes 2654224 | tf_op jit(solution)/shard_map/all_gather | solution.py:120
  414.0 4.6 fusion.36
  418.6 80.2 %fusion = f32[64,256]{1,0:T(8,128)S(1)} fusion(f32[3456,256]{1,0:T(8,128)} %fusion.36), kind=kCustom, calls=%all-reduce-scatter | all-reduce-scatter fusion | flops 1048577 | bytes 3606528
  498.9 4.0 collective-permute-start
  505.6 3.1 collective-permute-start.2
  508.7 3.6 collective-permute-start.3
  516.3 99.0 %all-reduce.2 = (f32[1152]{0:T(1024)}, f32[1152]{0:T(1024)}) all-reduce(f32[1152]{0:T(1024)S(1)} %get-tuple-element.6, f32[1152]{0:T(1024)S(1)} %get-tuple-element.8), channel_id=1, replica_groups=mesh['dp'=8,'tile'=64] {'dp','tile'}, use_global_device_ids=true, to_apply=%region_13.15 | all-reduce | flops 2304 | bytes 18432 | tf_op jit(solution)/shard_map/psum | solution.py:162
  619.6 5.6 collective-permute-start.6
  625.2 3.1 collective-permute-start.7
  630.4 3.3 fusion.27
  (87 shorter events, 41.9 us)
Async XLA Ops:
  7.2 95.8 %copy-start = (bf16[1,384,256]{2,1,0:T(8,128)(2,1)S(1)}, bf16[1,384,256]{2,1,0:T(8,128)(2,1)}, u32[]{:S(2)}) copy-start(bf16[1,384,256]{2,1,0:T(8,128)(2,1)} %param.15) | copy-start | bytes 589828
  7.2 93.3 %all-gather.6.cloned.1.call-start = ((), (), s32[]{:S(2)}) async-start(), calls=%async_computation.5 | async-start | bytes 1863680 | tf_op jit(solution)/shard_map/all_gather | solution.py:122
  7.9 183.2 %all-reduce.5.cloned.1.call-start = ((), (), s32[]{:S(2)}) async-start(), calls=%async_computation.4 | async-start | bytes 5308416 | tf_op jit(solution)/shard_map/psum | solution.py:136
  103.0 2.5 copy-start.2
  103.0 4.4 copy-start.5
  115.0 15.8 %all-to-all-start = ((s32[64,1,4]{2,1,0:T(1,128)}), s32[64,1,4]{2,1,0:T(1,128)S(1)}, u32[]{:S(2)}, u32[]{:S(2)}) async-start(s32[64,1,4]{2,1,0:T(1,128)} %bitcast.12), calls=%async_computation | async-start | bytes 65536 | tf_op jit(solution)/shard_map/all_to_all | solution.py:105
  194.4 18.6 %copy-start.1 = (bf16[1,729,1152]{2,1,0:T(8,128)(2,1)S(1)}, bf16[1,729,1152]{2,1,0:T(8,128)(2,1)}, u32[]{:S(2)}) copy-start(bf16[1,729,1152]{2,1,0:T(8,128)(2,1)} %param.9) | copy-start | bytes 5038852
  198.5 57.3 %all-to-all-start.2 = ((bf16[64,4,3456]{2,1,0:T(4,128)(2,1)}), bf16[64,4,3456]{2,1,0:T(4,128)(2,1)}, u32[]{:S(2)}, u32[]{:S(2)}) async-start(bf16[64,4,3456]{2,1,0:T(4,128)(2,1)} %reshape.873), calls=%async_computation.2 | async-start | bytes 3538944 | tf_op jit(solution)/shard_map/all_to_all | solution.py:146
  268.8 6.0 copy-start.4
  289.2 3.3 copy-start.6
  321.8 49.7 %all-to-all-start.1 = ((bf16[64,4,3456]{2,1,0:T(4,128)(2,1)}), bf16[64,4,3456]{2,1,0:T(4,128)(2,1)S(1)}, u32[]{:S(2)}, u32[]{:S(2)}) async-start(bf16[64,4,3456]{2,1,0:T(4,128)(2,1)} %reshape.869), calls=%async_computation.1 | async-start | bytes 3538944 | tf_op jit(solution)/shard_map/all_to_all | solution.py:98
  328.5 85.5 %all-gather.4.cloned.1.call-start = ((), (), s32[]{:S(2)}) async-start(), calls=%async_computation.3 | async-start | bytes 2985984 | tf_op jit(solution)/shard_map/all_gather | solution.py:120
  418.6 211.8 %copy-start.3 = (bf16[3456,256]{1,0:T(8,128)(2,1)S(1)}, bf16[3456,256]{1,0:T(8,128)(2,1)}, u32[]{:S(2)}) copy-start(bf16[3456,256]{1,0:T(8,128)(2,1)} %copy-done.2) | copy-start | bytes 5308420
  498.9 119.2 %collective-permute-start = (f32[64,256]{1,0:T(8,128)S(1)}, f32[64,256]{1,0:T(8,128)S(1)}, u32[]{:S(2)}, u32[]{:S(2)}) collective-permute-start(f32[64,256]{1,0:T(8,128)S(1)} %fusion), channel_id=1, source_target_pairs={{0,1},{1,2},{2,3},{3,4},{4,5},{5,6},{6,7},{7,8},{8,9},{9,10},{10,1... | collective-permute-start | bytes 196616
  502.9 116.7 %collective-permute-start.1 = (f32[64,256]{1,0:T(8,128)S(1)}, f32[64,256]{1,0:T(8,128)S(1)}, u32[]{:S(2)}, u32[]{:S(2)}) collective-permute-start(f32[64,256]{1,0:T(8,128)S(1)} %fusion), channel_id=1, source_target_pairs={{0,2},{1,3},{2,4},{3,5},{4,6},{5,7},{6,8},{7,9},{8,10},{9,11},{10,... | collective-permute-start | bytes 196616
  505.6 119.5 %collective-permute-start.2 = (f32[64,256]{1,0:T(8,128)S(1)}, f32[64,256]{1,0:T(8,128)S(1)}, u32[]{:S(2)}, u32[]{:S(2)}) collective-permute-start(f32[64,256]{1,0:T(8,128)S(1)} %fusion), channel_id=1, source_target_pairs={{0,3},{1,4},{2,5},{3,6},{4,7},{5,8},{6,9},{7,10},{8,11},{9,12},{10... | collective-permute-start | bytes 196616
  508.7 119.5 %collective-permute-start.3 = (f32[64,256]{1,0:T(8,128)S(1)}, f32[64,256]{1,0:T(8,128)S(1)}, u32[]{:S(2)}, u32[]{:S(2)}) collective-permute-start(f32[64,256]{1,0:T(8,128)S(1)} %fusion), channel_id=1, source_target_pairs={{0,4},{1,5},{2,6},{3,7},{4,8},{5,9},{6,10},{7,11},{8,12},{9,13},{1... | collective-permute-start | bytes 196616
  512.4 102.9 %collective-permute-start.9 = (f32[54,256]{1,0:T(8,128)S(1)}, f32[54,256]{1,0:T(8,128)S(1)}, u32[]{:S(2)}, u32[]{:S(2)}) collective-permute-start(f32[54,256]{1,0:T(8,128)S(1)} %slice), channel_id=1, source_target_pairs={{0,10},{1,11},{2,12},{3,13},{4,14},{5,15},{6,16},{7,17},{8,18},{9,... | collective-permute-start | bytes 165896
  615.3 18.5 %collective-permute-start.4 = (f32[64,256]{1,0:T(8,128)S(1)}, f32[64,256]{1,0:T(8,128)S(1)}, u32[]{:S(2)}, u32[]{:S(2)}) collective-permute-start(f32[64,256]{1,0:T(8,128)S(1)} %fusion), channel_id=1, source_target_pairs={{0,5},{1,6},{2,7},{3,8},{4,9},{5,10},{6,11},{7,12},{8,13},{9,14},{... | collective-permute-start | bytes 196616
  618.1 15.7 %collective-permute-start.5 = (f32[64,256]{1,0:T(8,128)S(1)}, f32[64,256]{1,0:T(8,128)S(1)}, u32[]{:S(2)}, u32[]{:S(2)}) collective-permute-start(f32[64,256]{1,0:T(8,128)S(1)} %fusion), channel_id=1, source_target_pairs={{0,6},{1,7},{2,8},{3,9},{4,10},{5,11},{6,12},{7,13},{8,14},{9,15},... | collective-permute-start | bytes 196616
  619.6 14.2 %collective-permute-start.6 = (f32[64,256]{1,0:T(8,128)S(1)}, f32[64,256]{1,0:T(8,128)S(1)}, u32[]{:S(2)}, u32[]{:S(2)}) collective-permute-start(f32[64,256]{1,0:T(8,128)S(1)} %fusion), channel_id=1, source_target_pairs={{0,7},{1,8},{2,9},{3,10},{4,11},{5,12},{6,13},{7,14},{8,15},{9,16}... | collective-permute-start | bytes 196616
  625.2 8.6 %collective-permute-start.7 = (f32[64,256]{1,0:T(8,128)S(1)}, f32[64,256]{1,0:T(8,128)S(1)}, u32[]{:S(2)}, u32[]{:S(2)}) collective-permute-start(f32[64,256]{1,0:T(8,128)S(1)} %fusion), channel_id=1, source_target_pairs={{0,8},{1,9},{2,10},{3,11},{4,12},{5,13},{6,14},{7,15},{8,16},{9,17... | collective-permute-start | bytes 196616
  628.3 5.5 collective-permute-start.8
Sparse Core Ops, SparseCore 0:
  11.3 89.1 all-gather.5
  105.6 85.5 all-reduce.4
  377.3 36.6 all-gather.3
where the time goes:
time: 654 us; the launch traced here: 643 us
  waiting for transfers between devices  283 us (43%)
  blocking collectives  179 us (27%)
  starting transfers between devices  58.2 us (9%)
  matrix products  44.7 us (7%)
  local copies, waits for them, and re-layouts  44.1 us (7%)
  other arithmetic  17.5 us (3%)
  between operations  15.9 us (2%)
    psum x1, blocking collectives, shards(): gain_grad, bias_grad = lax.psum((gain_part, bias_part), ('dp', 'tile'))  99 us
    all_gather x1, waiting for transfers between devices, shards(): full_weight = lax.all_gather(proj_weight, 'tile', axis=0, tiled=True)  92.5 us
    unnamed x1, blocking collectives  80.2 us
    psum x1, waiting for transfers between devices, shards(): summed = lax.psum(row_part.astype(jnp.bfloat16), 'dp').astype(jnp.float32)  59 us
    all_to_all x1, waiting for transfers between devices, shards(): lax.all_to_all(outgoing.reshape(peer_count, per_peer, BLOCK * feature_wid...  42.9 us
    all_to_all x1, waiting for transfers between devices, shards(): lax.all_to_all(returning, 'tile', split_axis=0, concat_axis=0, tiled=True)  42 us
    all_gather x1, waiting for transfers between devices, shards(): gathered = lax.all_gather(owned_rows, 'dp', axis=0, tiled=True)  36.9 us
    unnamed x10, starting transfers between devices  30.5 us
  transfers between devices with their start and end apart: 16, of which 6 were waited for; matrix products, arithmetic and copies ran while one was open for 2% of the time, Pallas kernels for 0%

commit v1 on v0

v1 whole, which is shorter than its diff:
```python
import jax
import jax.numpy as jnp
from jax import lax
from jax.experimental import pallas as pl
from jax.experimental.pallas import tpu as pltpu
from jax.sharding import Mesh, PartitionSpec as P

GRID = 27
BLOCK = 3
TILES_IMG = 14
IMAGES = 4
WIDTH = 1152
TOKENS = GRID * GRID
BLOCKS = GRID * (GRID // BLOCK)
BLOCKS_PAD = 256
NZ, NX, NC = 8, 4, 2
PEERS = NZ * NX * NC
CAP = 4
SEND = PEERS * CAP
OWN = 16
OWN_ROWS = OWN * BLOCK
SHARD = 54
SHARD_PAD = 56
CHUNK = 192
STEPS = 4
ROWS = 32
EPS = 1e-6
VMEM = 48 * 1024 * 1024

f32 = jnp.float32
bf16 = jnp.bfloat16
i32 = jnp.int32


def iota(shape, dim):
    return lax.broadcasted_iota(i32, shape, dim)


def tile_geometry(tile):
    safe = jnp.maximum(tile, 0)
    image = lax.div(safe, TILES_IMG)
    local = safe - image * TILES_IMG
    scale = jnp.where(local == 0, 1, jnp.where(local < 5, 2, 3))
    within = jnp.where(local == 0, 0, jnp.where(local < 5, local - 1, local - 5))
    row = jnp.where(scale == 1, 0, jnp.where(scale == 2, within >> 1, lax.div(within, 3)))
    return image, scale, row, within - row * scale


def weight_of(scale):
    return jnp.where(scale == 1, 1.0, jnp.where(scale == 2, 1.0 / 4.0, 1.0 / 9.0)).astype(f32)


def third(x):
    return (x * 171) >> 9


def token_cells(token, scale, row, col):
    u = (token * 2428) >> 16
    v = token - u * GRID
    down, right = GRID * row + u, GRID * col + v
    r = jnp.where(scale == 1, down, jnp.where(scale == 2, down >> 1, third(down)))
    c = jnp.where(scale == 1, right, jnp.where(scale == 2, right >> 1, third(right)))
    band = third(c)
    return r * (GRID // BLOCK) + band, c - band * BLOCK


def pick_image(image, parts):
    out = jnp.where(image == 0, parts[0], 0)
    for i in range(1, IMAGES):
        out = out + jnp.where(image == i, parts[i], 0)
    return out


def same_owner(image, peer_row_ref, peer_col_ref):
    row = pick_image(image, [peer_row_ref[i : i + 1, :] for i in range(IMAGES)])
    col = pick_image(image, [peer_col_ref[:, i : i + 1] for i in range(IMAGES)])
    return row, col, jnp.where(row == col, 1.0, 0.0)


def unit_rows_of(values):
    centered = values - jnp.sum(values, axis=-1, keepdims=True) * (1.0 / WIDTH)
    var = jnp.sum(centered * centered, axis=-1, keepdims=True) * (1.0 / WIDTH)
    inverse = lax.rsqrt(var + EPS)
    return centered * inverse, inverse


def pool_kernel(tile_ref, peer_row_ref, peer_col_ref, hidden_ref, out_ref, unit_ref):
    step = pl.program_id(0)

    def norm_rows(n, carry):
        start = pl.multiple_of(n * ROWS, ROWS)
        unit, _ = unit_rows_of(hidden_ref[0, pl.ds(start, ROWS), :].astype(f32))
        row = step * CHUNK + start
        valid = row + iota((ROWS, 1), 0) < TOKENS
        unit_ref[pl.ds(pl.multiple_of(row, ROWS), ROWS), :] = jnp.where(valid, unit, 0.0).astype(
            bf16
        )
        return carry

    lax.fori_loop(0, CHUNK // ROWS, norm_rows, 0)

    @pl.when(step == STEPS - 1)
    def _():
        tile = tile_ref[0]
        image, scale, row, col = tile_geometry(tile)
        _, peer, same = same_owner(image, peer_row_ref, peer_col_ref)
        shape = (BLOCKS_PAD, BLOCKS_PAD)
        earlier = jnp.where(iota(shape, 1) < iota(shape, 0), same, 0.0)
        place = peer * CAP + jnp.sum(earlier, axis=1, keepdims=True).astype(i32)
        tokens = STEPS * CHUNK
        token = iota((1, tokens), 1)
        block, cell = token_cells(token, scale, row, col)
        block = jnp.where((token < TOKENS) & (tile >= 0), block, -1)
        hit = iota((BLOCKS_PAD, tokens), 0) == block
        target = jnp.sum(jnp.where(hit, place, 0), axis=0, keepdims=True)
        target = jnp.where(block >= 0, target, -1)
        weight = weight_of(scale)
        for e in range(BLOCK):
            wanted = jnp.where(cell == e, target, -1)
            select = jnp.where(iota((SEND, tokens), 0) == wanted, 1.0, 0.0).astype(bf16)
            pooled = jnp.dot(select, unit_ref[...], preferred_element_type=f32) * weight
            out_ref[:, e * WIDTH : (e + 1) * WIDTH] = pooled.astype(bf16)


def pool_tokens(tile, peer_row, peer_col, hidden):
    return pl.pallas_call(
        pool_kernel,
        grid=(STEPS,),
        in_specs=[
            pl.BlockSpec(memory_space=pltpu.SMEM),
            pl.BlockSpec((IMAGES, BLOCKS_PAD), lambda i: (0, 0)),
            pl.BlockSpec((BLOCKS_PAD, IMAGES), lambda i: (0, 0)),
            pl.BlockSpec((1, CHUNK, WIDTH), lambda i: (0, i, 0)),
        ],
        out_specs=pl.BlockSpec((SEND, BLOCK * WIDTH), lambda i: (0, 0)),
        out_shape=jax.ShapeDtypeStruct((SEND, BLOCK * WIDTH), bf16),
        scratch_shapes=[pltpu.VMEM((STEPS * CHUNK, WIDTH), bf16)],
        compiler_params=pltpu.CompilerParams(vmem_limit_bytes=VMEM),
        name="pool_tokens",
    )(tile, peer_row, peer_col, hidden)


def row_grad_kernel(core_ref, mine_ref, other_ref, grad_ref, weight_ref, part_ref, wide_ref):
    first = core_ref[0] == 0
    for x in range(NX):
        for z in range(NZ):
            mine = mine_ref[x * NZ + z].astype(f32)
            other = other_ref[x * NZ + z].astype(f32)
            at = (z * NX * NC + x * NC) * SHARD
            low = jnp.where(first, mine, other)
            high = jnp.where(first, other, mine)
            wide_ref[at : at + SHARD, :] = low[:SHARD]
            wide_ref[at + SHARD : at + 2 * SHARD, :] = high[:SHARD]
    full = wide_ref[...].astype(bf16)
    weight_ref[...] = full
    part_ref[...] = lax.dot_general(
        grad_ref[0], full, (((1,), (1,)), ((), ())), preferred_element_type=f32
    ).astype(bf16)


def row_grad_part(core, mine, other, grad):
    rows, cols = grad.shape[1:]
    return pl.pallas_call(
        row_grad_kernel,
        in_specs=[pl.BlockSpec(memory_space=pltpu.SMEM)] + [pl.BlockSpec()] * 3,
        out_shape=(
            jax.ShapeDtypeStruct((PEERS * SHARD, cols), bf16),
            jax.ShapeDtypeStruct((rows, PEERS * SHARD), bf16),
        ),
        scratch_shapes=[pltpu.VMEM((PEERS * SHARD, cols), f32)],
        compiler_params=pltpu.CompilerParams(vmem_limit_bytes=VMEM),
        name="row_grad_part",
    )(core, mine, other, grad)


def owner_select(code, e):
    row = iota((3 * OWN_ROWS, SEND), 0)
    of = third(row)
    return jnp.where((of == code) & (row - of * BLOCK == e), 1.0, 0.0).astype(bf16)


def features_kernel(code_ref, named_ref, gain_ref, bias_ref, arrived_ref, out_ref, unit_ref):
    code = code_ref[...]
    total = jnp.zeros((3 * OWN_ROWS, WIDTH), f32)
    for e in range(BLOCK):
        total = total + jnp.dot(
            owner_select(code, e),
            arrived_ref[:, e * WIDTH : (e + 1) * WIDTH],
            preferred_element_type=f32,
        )
    unit_ref[...] = total
    named = named_ref[...] > 0.0
    for s in range(3):
        affine = total[s * OWN_ROWS : (s + 1) * OWN_ROWS] * gain_ref[...] + bias_ref[...]
        out_ref[:, s * WIDTH : (s + 1) * WIDTH] = jnp.where(named, affine, 0.0).astype(bf16)


def owned_features(code, named, gain, bias, arrived):
    return pl.pallas_call(
        features_kernel,
        out_shape=(
            jax.ShapeDtypeStruct((OWN_ROWS, 3 * WIDTH), bf16),
            jax.ShapeDtypeStruct((3 * OWN_ROWS, WIDTH), f32),
        ),
        compiler_params=pltpu.CompilerParams(vmem_limit_bytes=VMEM),
        name="owned_features",
    )(code, named, gain, bias, arrived)


def returning_kernel(code_ref, grad_ref, out_ref):
    code = code_ref[...]
    for e in range(BLOCK):
        select = owner_select(code, e)
        total = jnp.zeros((SEND, WIDTH), f32)
        for s in range(3):
            total = total + lax.dot_general(
                select[s * OWN_ROWS : (s + 1) * OWN_ROWS],
                grad_ref[:, s * WIDTH : (s + 1) * WIDTH],
                (((0,), (0,)), ((), ())),
                preferred_element_type=f32,
            )
        out_ref[:, e * WIDTH : (e + 1) * WIDTH] = total.astype(bf16)


def returning_blocks(code, grad):
    return pl.pallas_call(
        returning_kernel,
        out_shape=jax.ShapeDtypeStruct((SEND, BLOCK * WIDTH), bf16),
        compiler_params=pltpu.CompilerParams(vmem_limit_bytes=VMEM),
        name="returning_blocks",
    )(code, grad)


def hidden_grad_kernel(
    tile_ref, peer_row_ref, peer_col_ref, gain_ref, hidden_ref, returned_ref, out_ref, token_ref
):
    step = pl.program_id(0)
    tile = tile_ref[0]
    image, scale, row, col = tile_geometry(tile)
    peer, _, same = same_owner(image, peer_row_ref, peer_col_ref)
    shape = (BLOCKS_PAD, BLOCKS_PAD)
    earlier = jnp.where(iota(shape, 0) < iota(shape, 1), same, 0.0)
    place = peer * CAP + jnp.sum(earlier, axis=0, keepdims=True).astype(i32)
    token = step * CHUNK + iota((CHUNK, 1), 0)
    block, cell = token_cells(token, scale, row, col)
    block = jnp.where((token < TOKENS) & (tile >= 0), block, -1)
    hit = iota((CHUNK, BLOCKS_PAD), 1) == block
    target = jnp.sum(jnp.where(hit, place, 0), axis=1, keepdims=True)
    target = jnp.where(block >= 0, target, -1)
    total = jnp.zeros((CHUNK, WIDTH), f32)
    for e in range(BLOCK):
        wanted = jnp.where(cell == e, target, -1)
        select = jnp.where(iota((CHUNK, SEND), 1) == wanted, 1.0, 0.0).astype(bf16)
        total = total + jnp.dot(
            select, returned_ref[:, e * WIDTH : (e + 1) * WIDTH], preferred_element_type=f32
        )
    token_ref[...] = total * weight_of(scale)
    gain = gain_ref[...]

    def norm_rows(n, carry):
        start = pl.multiple_of(n * ROWS, ROWS)
        unit, inverse = unit_rows_of(hidden_ref[0, pl.ds(start, ROWS), :].astype(f32))
        scaled = token_ref[pl.ds(start, ROWS), :] * gain
        mean = jnp.sum(scaled, axis=-1, keepdims=True) * (1.0 / WIDTH)
        cross = jnp.sum(scaled * unit, axis=-1, keepdims=True) * (1.0 / WIDTH)
        out_ref[0, pl.ds(start, ROWS), :] = (inverse * (scaled - mean - unit * cross)).astype(bf16)
        return carry

    lax.fori_loop(0, CHUNK // ROWS, norm_rows, 0)


def hidden_gradient(tile, peer_row, peer_col, gain, hidden, returned):
    return pl.pallas_call(
        hidden_grad_kernel,
        grid=(STEPS,),
        in_specs=[
            pl.BlockSpec(memory_space=pltpu.SMEM),
            pl.BlockSpec((IMAGES, BLOCKS_PAD), lambda i: (0, 0)),
            pl.BlockSpec((BLOCKS_PAD, IMAGES), lambda i: (0, 0)),
            pl.BlockSpec((1, WIDTH), lambda i: (0, 0)),
            pl.BlockSpec((1, CHUNK, WIDTH), lambda i: (0, i, 0)),
            pl.BlockSpec((SEND, BLOCK * WIDTH), lambda i: (0, 0)),
        ],
        out_specs=pl.BlockSpec((1, CHUNK, WIDTH), lambda i: (0, i, 0)),
        out_shape=jax.ShapeDtypeStruct((1, TOKENS, WIDTH), bf16),
        scratch_shapes=[pltpu.VMEM((CHUNK, WIDTH), f32)],
        compiler_params=pltpu.CompilerParams(vmem_limit_bytes=VMEM),
        name="hidden_gradient",
    )(tile, peer_row, peer_col, gain, hidden, returned)


def projector_kernel(gathered_ref, weight_ref, grad_ref, projected_ref, terms_ref, wide_ref):
    projected_ref[0] = jnp.dot(
        gathered_ref[...], weight_ref[...], preferred_element_type=f32
    ).astype(bf16)
    wide_ref[...] = lax.dot_general(
        gathered_ref[...], grad_ref[0], (((0,), (0,)), ((), ())), preferred_element_type=f32
    )
    cols = grad_ref.shape[2]
    pad = jnp.zeros((SHARD_PAD - SHARD, cols), f32)
    for c in range(NC):
        for x in range(NX):
            for z in range(NZ):
                at = (z * NX * NC + x * NC + c) * SHARD
                part = jnp.concatenate([wide_ref[at : at + SHARD, :], pad], axis=0)
                terms_ref[(c * NX + x) * NZ + z] = part.astype(bf16)


def projector(gathered, weight, grad):
    rows, cols = grad.shape[1:]
    return pl.pallas_call(
        projector_kernel,
        out_shape=(
            jax.ShapeDtypeStruct((1, rows, cols), bf16),
            jax.ShapeDtypeStruct((PEERS, SHARD_PAD, cols), bf16),
        ),
        scratch_shapes=[pltpu.VMEM((PEERS * SHARD, cols), f32)],
        compiler_params=pltpu.CompilerParams(vmem_limit_bytes=VMEM),
        name="projector",
    )(gathered, weight, grad)


def scatter_sum(terms, axis, count):
    parts = lax.all_to_all(terms, axis, split_axis=0, concat_axis=0, tiled=True)
    return jnp.sum(parts.reshape((count, -1) + parts.shape[1:]).astype(f32), axis=0)


def spread(shard, axis, count):
    copies = jnp.broadcast_to(shard[None], (count,) + shard.shape)
    return lax.all_to_all(copies, axis, split_axis=0, concat_axis=0, tiled=True)


def shards(hidden, norm_gain, norm_bias, slot_tile, block_owner, proj_weight, proj_grad):
    cols = proj_weight.shape[1]
    core = lax.axis_index("c")
    me = (lax.axis_index("z") * NX + lax.axis_index("x")) * NC + core

    tile_row = jnp.broadcast_to(slot_tile.astype(bf16)[:, None], (1, cols))
    shard = jnp.concatenate(
        [proj_weight, tile_row, jnp.zeros((SHARD_PAD - SHARD - 1, cols), bf16)], axis=0
    )
    over_z = spread(shard, "z", NZ)
    mine = spread(over_z, "x", NX).reshape(NX * NZ, SHARD_PAD, cols)
    other = lax.ppermute(mine, "c", [(0, 1), (1, 0)])

    table = block_owner.reshape(IMAGES, BLOCKS)
    peers = jnp.pad(table >> 4, ((0, 0), (0, BLOCKS_PAD - BLOCKS)), constant_values=-1)
    outgoing = pool_tokens(slot_tile, peers, peers.T, hidden)
    arrived = lax.all_to_all(outgoing, ("z", "x", "c"), 0, 0, tiled=True)

    weight, row_part = row_grad_part(core.reshape(1), mine, other, proj_grad)
    own_grad = lax.psum_scatter(row_part, "dp", scatter_dimension=0, tiled=True)

    held = (table >> 4) == me
    below = jnp.triu(jnp.ones((BLOCKS, BLOCKS), bf16), 1)
    rank = jnp.dot(held.astype(bf16), below, preferred_element_type=f32).astype(i32)
    slot = table & (OWN - 1)
    ranks = jnp.arange(CAP, dtype=i32)
    of_rank = held[:, None, :] & (rank[:, None, :] == ranks[None, :, None])
    slot_of = jnp.max(jnp.where(of_rank, slot[:, None, :], -1), axis=2)
    slots = jnp.arange(OWN, dtype=i32)
    named = jnp.any(held[None] & (slot[None] == slots[:, None, None]), axis=(1, 2))
    named = jnp.repeat(named.astype(f32), BLOCK).reshape(OWN_ROWS, 1)

    ids_mine = mine[:, SHARD, 0].astype(i32).reshape(NX, NZ)
    ids_other = other[:, SHARD, 0].astype(i32).reshape(NX, NZ)
    low = jnp.where(core == 0, ids_mine, ids_other)
    high = jnp.where(core == 0, ids_other, ids_mine)
    ids = jnp.stack([low, high], axis=-1).transpose(1, 0, 2).reshape(PEERS)
    safe = jnp.maximum(ids, 0)
    image = safe // TILES_IMG
    local = safe % TILES_IMG
    scale = jnp.where(local == 0, 0, jnp.where(local < 5, 1, 2))
    of_image = (image[:, None] == jnp.arange(IMAGES, dtype=i32)[None]) & (ids >= 0)[:, None]
    found = jnp.max(jnp.where(of_image[:, :, None], slot_of[None], -1), axis=1)
    code = jnp.where(found >= 0, scale[:, None] * OWN + found, -1).reshape(1, SEND)

    gain = norm_gain.reshape(1, WIDTH)
    features, unit_sums = owned_features(code, named, gain, norm_bias.reshape(1, WIDTH), arrived)
    gathered = lax.all_gather(features, "dp", axis=0, tiled=True)

    returning = returning_blocks(code, own_grad)
    returned = lax.all_to_all(returning, ("z", "x", "c"), 0, 0, tiled=True)

    grads = own_grad.astype(f32).reshape(OWN_ROWS, 3, WIDTH)
    units = unit_sums.reshape(3, OWN_ROWS, WIDTH).transpose(1, 0, 2)
    totals = jnp.stack(
        [jnp.sum(grads * units, axis=(0, 1)), jnp.sum(grads * named[:, :, None], axis=(0, 1))]
    )
    for axis in ("dp", "z", "x", "c"):
        totals = lax.psum(totals, axis)

    projected, terms = projector(gathered, weight, proj_grad)
    terms = scatter_sum(terms, "c", NC).astype(bf16)
    terms = scatter_sum(terms, "x", NX).astype(bf16)
    weight_grad = scatter_sum(terms, "z", NZ)[0, :SHARD]

    hidden_grad = hidden_gradient(slot_tile, peers, peers.T, gain, hidden, returned)
    return projected, weight_grad, hidden_grad, totals[0], totals[1]


def solution(mesh):
    sizes = (mesh.shape["dp"], NZ, NX, NC)
    split = Mesh(mesh.devices.reshape(sizes), ("dp", "z", "x", "c"))
    tile = ("z", "x", "c")
    every = ("dp",) + tile
    return jax.shard_map(
        shards,
        mesh=split,
        in_specs=(
            P(every, None, None),
            P(),
            P(),
            P(every),
            P("dp", None, None, None),
            P(tile, "dp"),
            P(tile, None, "dp"),
        ),
        out_specs=(P(tile, None, "dp"), P(tile, "dp"), P(every, None, None), P(), P()),
        check_vma=False,
    )
```

time: 654 us -> 298 us (0.46); the launches traced: 643 us -> 297 us
  waiting for transfers between devices: 283 us -> 78.3 us
  blocking collectives: 179 us -> 107 us
  matrix products: 44.7 us -> 0.15 us
  Pallas kernels: 0 us -> 28.3 us
  local copies, waits for them, and re-layouts: 44.1 us -> 22.6 us
  starting transfers between devices: 58.2 us -> 37.4 us
  other arithmetic: 17.5 us -> 8.48 us
    all_gather x2 -> x1, waiting for transfers between devices: 129 us -> 33.6 us  [shards(): gathered = lax.all_gather(features, 'dp', axis=0, tiled=True)]
    unnamed x1 -> x0, blocking collectives: 80.2 us -> none
    all_to_all x3 -> x4, waiting for transfers between devices: 94.2 us -> 35 us  [the longest x1 33.7 us: shards(): arrived = lax.all_to_all(outgoing, ('z', 'x', 'c'), 0, 0, tiled=True)]
    psum x1 -> x0, waiting for transfers between devices: 59 us -> none  [shards(): summed = lax.psum(row_part.astype(jnp.bfloat16), 'dp').astype(jnp.float32)]
    all_to_all x0 -> x3, blocking collectives: none -> 45.5 us  [the longest x2 25.1 us: scatter_sum(): parts = lax.all_to_all(terms, axis, split_axis=0, concat_axis=0, tiled=True)]
    dot_general x11 -> x1, matrix products: 44.7 us -> 0.15 us  [shards(): jnp.dot(held.astype(bf16), below, preferred_element_type=f32).astype(i32)]
    psum x1 -> x4, blocking collectives: 99 us -> 61.5 us  [shards(): totals = lax.psum(totals, axis)]
    unnamed x10 -> x0, starting transfers between devices: 30.5 us -> none
  transfers between devices with their start and end apart: 16 -> 7, of which waited for: 6 -> 5; matrix products, arithmetic and copies ran while one was open for 2% -> 4% of each run, Pallas kernels for 0% -> 6%
where the time goes in v1:
time: 298 us; the launch traced here: 297 us
  blocking collectives  107 us (36%)
  waiting for transfers between devices  78.3 us (26%)
  starting transfers between devices  37.4 us (13%)
  Pallas kernels  28.3 us (9%)
  local copies, waits for them, and re-layouts  22.6 us (8%)
  between operations  15.1 us (5%)
  other arithmetic  8.48 us (3%)
    psum x4, blocking collectives, shards(): totals = lax.psum(totals, axis)  61.5 us
    all_to_all x1, waiting for transfers between devices, shards(): arrived = lax.all_to_all(outgoing, ('z', 'x', 'c'), 0, 0, tiled=True)  33.7 us
    all_gather x1, waiting for transfers between devices, shards(): gathered = lax.all_gather(features, 'dp', axis=0, tiled=True)  33.6 us
    all_to_all x2, blocking collectives, scatter_sum(): parts = lax.all_to_all(terms, axis, split_axis=0, concat_axis=0, tiled=True)  25.1 us
    all_to_all x1, blocking collectives, spread(): return lax.all_to_all(copies, axis, split_axis=0, concat_axis=0, tiled=True)  20.4 us
    all_to_all x1, starting transfers between devices, shards(): returned = lax.all_to_all(returning, ('z', 'x', 'c'), 0, 0, tiled=True)  14.8 us
    pallas_call x1, Pallas kernels, hidden_gradient(): pl.pallas_call(hidden_grad_kernel, grid=(STEPS,), in_specs=[pl.BlockSpec(...  11.3 us
    all_to_all x1, starting transfers between devices, shards(): arrived = lax.all_to_all(outgoing, ('z', 'x', 'c'), 0, 0, tiled=True)  8.58 us
  transfers between devices with their start and end apart: 7, of which 5 were waited for; matrix products, arithmetic and copies ran while one was open for 4% of the time, Pallas kernels for 6%

profile of v1, /device:TPU:1, one launch (start us, length us, event | category | flops | bytes accessed | tf_op | source)
XLA Modules:
  0.0 297.2 jit_solution(4553134318709075111)
XLA Ops:
  8.8 20.4 %all_to_all.47 = bf16[8,56,256]{2,1,0:T(8,128)(2,1)S(1)} all-to-all(bf16[8,56,256]{2,1,0:T(8,128)(2,1)S(1)} %broadcast_in_dim.93), channel_id=1, replica_groups=mesh['dp'=8,'z'=8,'x'=4,'c'=2] {'z'}, dimensions={0} | all-to-all | bytes 458752 | tf_op jit(solution)/shard_map/all_to_all | solution.py:330
  29.3 1.0 broadcast_in_dim.94
  30.2 4.2 %all-to-all-start.1 = ((bf16[4,8,56,256]{3,2,1,0:T(8,128)(2,1)}), bf16[4,8,56,256]{3,2,1,0:T(8,128)(2,1)}, u32[]{:S(2)}, u32[]{:S(2)}) async-start(bf16[4,8,56,256]{3,2,1,0:T(8,128)(2,1)} %broadcast_in_dim.94), calls=%async_computation.1 | async-start | bytes 1835008 | tf_op jit(solution)/shard_map/all_to_all | solution.py:330
  35.0 7.0 %pool_tokens.1 = bf16[256,3456]{1,0:T(8,128)(2,1)S(1)} custom-call(s32[1]{0:T(128)S(6)} %copy.49.tile_ref, s32[4,256]{1,0:T(4,128)S(1)} %pad.4.clone.peer_row_ref, s32[256,4]{1,0:T(8,128)S(1)} %pad_bitcast_fusion.peer_col_ref, bf16[1,729,1152]{2,1,0:T(8,128)(2,1)S(1)} %copy-done), custom_call_target="tpu_custom_call" | custom-call | tf_op jit(solution)/shard_map/pool_tokens/pallas_call | solution.py:126
  42.7 1.5 all_to_all.31
  44.1 1.3 all-to-all-done.1
  45.5 8.6 %all-to-all-start.2 = ((bf16[64,4,3456]{2,1,0:T(4,128)(2,1)}), bf16[64,4,3456]{2,1,0:T(4,128)(2,1)}, u32[]{:S(2)}, u32[]{:S(2)}) async-start(bf16[64,4,3456]{2,1,0:T(4,128)(2,1)} %all_to_all.31), calls=%async_computation.2 | async-start | bytes 3538944 | tf_op jit(solution)/shard_map/all_to_all | solution.py:349
  54.1 2.5 collective-permute-start
  57.6 1.4 collective-permute-done.other_ref
  59.0 2.1 fusion.8
  63.4 33.7 %all-to-all-done.2 = bf16[64,4,3456]{2,1,0:T(4,128)(2,1)} async-done(((bf16[64,4,3456]{2,1,0:T(4,128)(2,1)}), bf16[64,4,3456]{2,1,0:T(4,128)(2,1)}, u32[]{:S(2)}, u32[]{:S(2)}) %all-to-all-start.2) | async-done | bytes 1769504 | tf_op jit(solution)/shard_map/all_to_all | solution.py:349
  97.1 2.9 all_to_all.33.arrived_ref
  102.1 1.2 copy-done.6
  104.2 3.8 %row_grad_part.1 = (bf16[3456,256]{1,0:T(8,128)(2,1)S(1)}, bf16[384,3456]{1,0:T(8,128)(2,1)}) custom-call(s32[1]{0:T(128)} %bitcast.7.core_ref, bf16[32,56,256]{2,1,0:T(8,128)(2,1)} %bitcast.1.mine_ref, bf16[32,56,256]{2,1,0:T(8,128)(2,1)S(1)} %copy-done.6, bf16[1,384,256]{2,1,0:T(8,128)(2,1)S(1)} %copy-done.7), custom_call_target="tpu_custom_call" | custom-call | tf_op jit(solution)/shard_map/row_grad_part/pallas_call | solution.py:163
  108.1 33.6 %all-gather.2.cloned.1.call-done.gathered_ref = bf16[384,3456]{1,0:T(8,128)(2,1)} async-done(((bf16[48,3456]{1,0:T(8,128)(2,1)}), bf16[384,3456]{1,0:T(8,128)(2,1)}) %all-gather.2.cloned.1.call-update) | async-done | bytes 2654224 | tf_op jit(solution)/shard_map/all_gather | solution.py:380
  142.6 4.1 %projector.1 = (bf16[1,384,256]{2,1,0:T(8,128)(2,1)}, bf16[64,56,256]{2,1,0:T(8,128)(2,1)S(1)}) custom-call(bf16[384,3456]{1,0:T(8,128)(2,1)} %all-gather.2.cloned.1.call-done.gathered_ref, bf16[3456,256]{1,0:T(8,128)(2,1)S(1)} %get-tuple-element.12.weight_ref, bf16[1,384,256]{2,1,0:T(8,128)(2,1)S(1)} %copy-done.8), custom_call_target="tpu_custom_call" | custom-call | tf_op jit(solution)/shard_map/projector/pallas_call | solution.py:311
  146.7 8.3 %all_to_all.48 = bf16[64,56,256]{2,1,0:T(8,128)(2,1)S(1)} all-to-all(bf16[64,56,256]{2,1,0:T(8,128)(2,1)S(1)} %get-tuple-element.14), channel_id=1, replica_groups=mesh['dp'=8,'z'=8,'x'=4,'c'=2] {'c'}, dimensions={0} | all-to-all | bytes 3670016 | tf_op jit(solution)/shard_map/all_to_all | solution.py:324
  155.0 1.5 reduce_sum.60
  156.5 16.8 %all_to_all.49 = bf16[32,56,256]{2,1,0:T(8,128)(2,1)S(1)} all-to-all(bf16[32,56,256]{2,1,0:T(8,128)(2,1)} %reduce_sum.60), channel_id=1, replica_groups=mesh['dp'=8,'z'=8,'x'=4,'c'=2] {'x'}, dimensions={0} | all-to-all | bytes 1835008 | tf_op jit(solution)/shard_map/all_to_all | solution.py:324
  174.2 7.1 %all-to-all-start.5 = ((bf16[8,56,256]{2,1,0:T(8,128)(2,1)}), bf16[8,56,256]{2,1,0:T(8,128)(2,1)}, u32[]{:S(2)}, u32[]{:S(2)}) async-start(bf16[8,56,256]{2,1,0:T(8,128)(2,1)} %reduce_sum.61), calls=%async_computation.5 | async-start | bytes 458752 | tf_op jit(solution)/shard_map/all_to_all | solution.py:324
  181.3 8.2 %reduce-scatter.2.cloned.1.call-done.grad_ref = bf16[48,3456]{1,0:T(8,128)(2,1)} async-done(((bf16[384,3456]{1,0:T(8,128)(2,1)}), bf16[48,3456]{1,0:T(8,128)(2,1)}) %reduce-scatter.2.cloned.1.call-update) | async-done | bytes 331792 | tf_op jit(solution)/shard_map/reduce_scatter | solution.py:352
  190.5 1.6 returning_blocks.1
  192.1 1.4 all_to_all.37
  193.5 14.8 %all-to-all-start.6 = ((bf16[64,4,3456]{2,1,0:T(4,128)(2,1)}), bf16[64,4,3456]{2,1,0:T(4,128)(2,1)}, u32[]{:S(2)}, u32[]{:S(2)}) async-start(bf16[64,4,3456]{2,1,0:T(4,128)(2,1)} %all_to_all.37), calls=%async_computation.7 | async-start | bytes 3538944 | tf_op jit(solution)/shard_map/all_to_all | solution.py:383
  208.4 1.2 reshape.242
  209.7 1.6 fusion
  211.5 14.0 %psum.28 = f32[2,1152]{1,0:T(2,128)S(1)} all-reduce(f32[2,1152]{1,0:T(2,128)S(1)} %pad_maximum_fusion), channel_id=1, replica_groups=mesh['dp'=8,'z'=8,'x'=4,'c'=2] {'dp'}, use_global_device_ids=true, to_apply=%region_10.11 | all-reduce | flops 2304 | bytes 18432 | tf_op jit(solution)/shard_map/psum | solution.py:391
  225.5 31.2 %psum.29 = f32[2,1152]{1,0:T(2,128)S(1)} all-reduce(f32[2,1152]{1,0:T(2,128)S(1)} %psum.28), channel_id=1, replica_groups=mesh['dp'=8,'z'=8,'x'=4,'c'=2] {'z'}, use_global_device_ids=true, to_apply=%region_11.12 | all-reduce | flops 2304 | bytes 18432 | tf_op jit(solution)/shard_map/psum | solution.py:391
  256.7 8.7 %psum.30 = f32[2,1152]{1,0:T(2,128)S(1)} all-reduce(f32[2,1152]{1,0:T(2,128)S(1)} %psum.29), channel_id=1, replica_groups=mesh['dp'=8,'z'=8,'x'=4,'c'=2] {'x'}, use_global_device_ids=true, to_apply=%region_12.13 | all-reduce | flops 2304 | bytes 18432 | tf_op jit(solution)/shard_map/psum | solution.py:391
  265.4 7.5 %psum.31 = f32[2,1152]{1,0:T(2,128)S(1)} all-reduce(f32[2,1152]{1,0:T(2,128)S(1)} %psum.30), channel_id=1, replica_groups=mesh['dp'=8,'z'=8,'x'=4,'c'=2] {'c'}, use_global_device_ids=true, to_apply=%region_13.14 | all-reduce | flops 2304 | bytes 18432 | tf_op jit(solution)/shard_map/psum | solution.py:391
  275.2 2.9 all_to_all.39.returned_ref
  279.0 11.3 %hidden_gradient.1 = bf16[1,729,1152]{2,1,0:T(8,128)(2,1)} custom-call(s32[1]{0:T(128)S(6)} %copy.49.tile_ref, s32[4,256]{1,0:T(4,128)S(1)} %pad.4.clone.peer_row_ref, s32[256,4]{1,0:T(8,128)S(1)} %copy-done.4, f32[1,1152]{1,0:T(1,128)S(1)} %reshape.237.gain_ref, bf16[1,729,1152]{2,1,0:T(8,128)(2,1)S(1)} %copy-done, ...), custom_call_target="tpu_custom_call" | custom-call | tf_op jit(solution)/shard_map/hidden_gradient/pallas_call | solution.py:273
  (89 shorter events, 14.6 us)
Async XLA Ops:
  8.8 25.7 %copy-start.12 = (s32[1,4,27,9]{2,1,3,0:T(4,128)S(1)}, s32[1,4,27,9]{2,1,3,0:T(4,128)}, u32[]{:S(2)}) copy-start(s32[1,4,27,9]{2,1,3,0:T(4,128)} %param.11) | copy-start | bytes 11668
  29.3 5.7 %copy-start = (bf16[1,729,1152]{2,1,0:T(8,128)(2,1)S(1)}, bf16[1,729,1152]{2,1,0:T(8,128)(2,1)}, u32[]{:S(2)}) copy-start(bf16[1,729,1152]{2,1,0:T(8,128)(2,1)} %hidden_ref.3) | copy-start | bytes 5038852
  30.2 15.3 %all-to-all-start.1 = ((bf16[4,8,56,256]{3,2,1,0:T(8,128)(2,1)}), bf16[4,8,56,256]{3,2,1,0:T(8,128)(2,1)}, u32[]{:S(2)}, u32[]{:S(2)}) async-start(bf16[4,8,56,256]{3,2,1,0:T(8,128)(2,1)} %broadcast_in_dim.94), calls=%async_computation.1 | async-start | bytes 1835008 | tf_op jit(solution)/shard_map/all_to_all | solution.py:330
  42.0 0.6 copy-start.3
  44.1 13.1 %copy-start.13 = (f32[1152]{0:T(1024)S(1)}, f32[1152]{0:T(1024)}, u32[]{:S(2)}) copy-start(f32[1152]{0:T(1024)} %param.8) | copy-start | bytes 13828
  44.1 13.1 %copy-start.14 = (f32[1152]{0:T(1024)S(1)}, f32[1152]{0:T(1024)}, u32[]{:S(2)}) copy-start(f32[1152]{0:T(1024)} %param.9) | copy-start | bytes 13828
  45.5 51.6 %all-to-all-start.2 = ((bf16[64,4,3456]{2,1,0:T(4,128)(2,1)}), bf16[64,4,3456]{2,1,0:T(4,128)(2,1)}, u32[]{:S(2)}, u32[]{:S(2)}) async-start(bf16[64,4,3456]{2,1,0:T(4,128)(2,1)} %all_to_all.31), calls=%async_computation.2 | async-start | bytes 3538944 | tf_op jit(solution)/shard_map/all_to_all | solution.py:349
  54.1 87.6 %all-gather.2.cloned.1.call-start = ((), (), s32[]{:S(2)}) async-start(), calls=%async_computation.8 | async-start | bytes 2985984 | tf_op jit(solution)/shard_map/all_gather | solution.py:380
  54.1 4.8 %collective-permute-start = (bf16[32,56,256]{2,1,0:T(8,128)(2,1)}, bf16[32,56,256]{2,1,0:T(8,128)(2,1)S(1)}, u32[]{:S(2)}, u32[]{:S(2)}) collective-permute-start(bf16[32,56,256]{2,1,0:T(8,128)(2,1)} %bitcast.1.mine_ref), channel_id=1, source_target_pairs={{0,1},{1,0},{2,3},{3,2},{4,5},{5,4},{6,7},{7,6},{8,9},{9,8},{10,11... | collective-permute-start | bytes 2752520 | tf_op jit(solution)/shard_map/ppermute | solution.py:344
  61.0 0.9 copy-start.5
  100.5 0.8 copy-start.9
  101.3 0.7 copy-start.11
  102.1 87.4 %reduce-scatter.2.cloned.1.call-start = ((), (), s32[]{:S(2)}) async-start(), calls=%async_computation.9 | async-start | bytes 2985984 | tf_op jit(solution)/shard_map/reduce_scatter | solution.py:352
  102.1 1.2 copy-start.6
  103.3 0.9 copy-start.7
  141.7 0.9 copy-start.8
  174.2 19.4 %all-to-all-start.5 = ((bf16[8,56,256]{2,1,0:T(8,128)(2,1)}), bf16[8,56,256]{2,1,0:T(8,128)(2,1)}, u32[]{:S(2)}, u32[]{:S(2)}) async-start(bf16[8,56,256]{2,1,0:T(8,128)(2,1)} %reduce_sum.61), calls=%async_computation.5 | async-start | bytes 458752 | tf_op jit(solution)/shard_map/all_to_all | solution.py:324
  189.5 1.0 copy-start.1
  193.5 14.9 %copy-start.2 = (bf16[48,3456]{1,0:T(8,128)(2,1)S(1)}, bf16[48,3456]{1,0:T(8,128)(2,1)}, u32[]{:S(2)}) copy-start(bf16[48,3456]{1,0:T(8,128)(2,1)} %reduce-scatter.2.cloned.1.call-done.grad_ref) | copy-start | bytes 995332
  193.5 16.1 %copy-start.10 = (f32[144,1152]{1,0:T(8,128)S(1)}, f32[144,1152]{1,0:T(8,128)}, u32[]{:S(2)}) copy-start(f32[144,1152]{1,0:T(8,128)} %copy-done.9) | copy-start | bytes 1990660
  193.5 81.7 %all-to-all-start.6 = ((bf16[64,4,3456]{2,1,0:T(4,128)(2,1)}), bf16[64,4,3456]{2,1,0:T(4,128)(2,1)}, u32[]{:S(2)}, u32[]{:S(2)}) async-start(bf16[64,4,3456]{2,1,0:T(4,128)(2,1)} %all_to_all.37), calls=%async_computation.7 | async-start | bytes 3538944 | tf_op jit(solution)/shard_map/all_to_all | solution.py:383
  278.1 0.9 copy-start.4
Sparse Core Ops, SparseCore 0:
  102.2 39.4 all-gather.1
  144.6 44.9 reduce-scatter.1

commit v2 on v1

--- a/solution.py
+++ b/solution.py
@@ -13,7 +13,7 @@
 TOKENS = GRID * GRID
 BLOCKS = GRID * (GRID // BLOCK)
 BLOCKS_PAD = 256
-NZ, NX, NC = 8, 4, 2
+NDP, NZ, NX, NC = 8, 8, 4, 2
 PEERS = NZ * NX * NC
 CAP = 4
 SEND = PEERS * CAP
@@ -21,12 +21,17 @@
 OWN_ROWS = OWN * BLOCK
 SHARD = 54
 SHARD_PAD = 56
+TERM_PAD = 64
 CHUNK = 192
 STEPS = 4
 ROWS = 32
 EPS = 1e-6
 VMEM = 48 * 1024 * 1024
 
+FEATURES_COST = 40
+ROW_GRAD_COST = 20
+POOL_COST = 8
+
 f32 = jnp.float32
 bf16 = jnp.bfloat16
 i32 = jnp.int32
@@ -34,6 +39,12 @@
 
 def iota(shape, dim):
     return lax.broadcasted_iota(i32, shape, dim)
+
+
+def cost(micros):
+    return pl.CostEstimate(
+        flops=micros * 10**9, transcendentals=0, bytes_accessed=micros * 3 * 10**6
+    )
 
 
 def tile_geometry(tile):
@@ -82,6 +93,16 @@
     var = jnp.sum(centered * centered, axis=-1, keepdims=True) * (1.0 / WIDTH)
     inverse = lax.rsqrt(var + EPS)
     return centered * inverse, inverse
+
+
+def put_blocks(ref, e, rows):
+    cell = slice(e * WIDTH, (e + 1) * WIDTH)
+    ref[:, :, cell] = rows.reshape(PEERS, CAP, WIDTH).astype(bf16)
+
+
+def get_blocks(ref, e):
+    cell = slice(e * WIDTH, (e + 1) * WIDTH)
+    return ref[:, :, cell].reshape(SEND, WIDTH)
 
 
 def pool_kernel(tile_ref, peer_row_ref, peer_col_ref, hidden_ref, out_ref, unit_ref):
@@ -119,7 +140,7 @@
             wanted = jnp.where(cell == e, target, -1)
             select = jnp.where(iota((SEND, tokens), 0) == wanted, 1.0, 0.0).astype(bf16)
             pooled = jnp.dot(select, unit_ref[...], preferred_element_type=f32) * weight
-            out_ref[:, e * WIDTH : (e + 1) * WIDTH] = pooled.astype(bf16)
+            put_blocks(out_ref, e, pooled)
 
 
 def pool_tokens(tile, peer_row, peer_col, hidden):
@@ -132,25 +153,28 @@
             pl.BlockSpec((BLOCKS_PAD, IMAGES), lambda i: (0, 0)),
             pl.BlockSpec((1, CHUNK, WIDTH), lambda i: (0, i, 0)),
         ],
-        out_specs=pl.BlockSpec((SEND, BLOCK * WIDTH), lambda i: (0, 0)),
-        out_shape=jax.ShapeDtypeStruct((SEND, BLOCK * WIDTH), bf16),
+        out_specs=pl.BlockSpec((PEERS, CAP, BLOCK * WIDTH), lambda i: (0, 0, 0)),
+        out_shape=jax.ShapeDtypeStruct((PEERS, CAP, BLOCK * WIDTH), bf16),
         scratch_shapes=[pltpu.VMEM((STEPS * CHUNK, WIDTH), bf16)],
         compiler_params=pltpu.CompilerParams(vmem_limit_bytes=VMEM),
+        cost_estimate=cost(POOL_COST),
         name="pool_tokens",
     )(tile, peer_row, peer_col, hidden)
 
 
-def row_grad_kernel(core_ref, mine_ref, other_ref, grad_ref, weight_ref, part_ref, wide_ref):
+def row_grad_kernel(
+    core_ref, mine_ref, other_ref, grad_ref, weight_ref, part_ref, tiles_ref, wide_ref
+):
     first = core_ref[0] == 0
     for x in range(NX):
         for z in range(NZ):
             mine = mine_ref[x * NZ + z].astype(f32)
             other = other_ref[x * NZ + z].astype(f32)
-            at = (z * NX * NC + x * NC) * SHARD
-            low = jnp.where(first, mine, other)
-            high = jnp.where(first, other, mine)
-            wide_ref[at : at + SHARD, :] = low[:SHARD]
-            wide_ref[at + SHARD : at + 2 * SHARD, :] = high[:SHARD]
+            low, high = jnp.where(first, mine, other), jnp.where(first, other, mine)
+            for c, block in enumerate((low, high)):
+                peer = (z * NX + x) * NC + c
+                wide_ref[peer * SHARD : (peer + 1) * SHARD, :] = block[:SHARD]
+                tiles_ref[peer : peer + 1, :] = block[SHARD : SHARD + 1, : tiles_ref.shape[1]]
     full = wide_ref[...].astype(bf16)
     weight_ref[...] = full
     part_ref[...] = lax.dot_general(
@@ -166,9 +190,11 @@
         out_shape=(
             jax.ShapeDtypeStruct((PEERS * SHARD, cols), bf16),
             jax.ShapeDtypeStruct((rows, PEERS * SHARD), bf16),
+            jax.ShapeDtypeStruct((PEERS, 128), f32),
         ),
         scratch_shapes=[pltpu.VMEM((PEERS * SHARD, cols), f32)],
         compiler_params=pltpu.CompilerParams(vmem_limit_bytes=VMEM),
+        cost_estimate=cost(ROW_GRAD_COST),
         name="row_grad_part",
     )(core, mine, other, grad)
 
@@ -179,13 +205,15 @@
     return jnp.where((of == code) & (row - of * BLOCK == e), 1.0, 0.0).astype(bf16)
 
 
-def features_kernel(code_ref, named_ref, gain_ref, bias_ref, arrived_ref, out_ref, unit_ref):
+def features_kernel(
+    code_ref, named_ref, gain_ref, bias_ref, arrived_ref, part_ref, out_ref, unit_ref
+):
     code = code_ref[...]
     total = jnp.zeros((3 * OWN_ROWS, WIDTH), f32)
     for e in range(BLOCK):
         total = total + jnp.dot(
             owner_select(code, e),
-            arrived_ref[:, e * WIDTH : (e + 1) * WIDTH],
+            get_blocks(arrived_ref, e),
             preferred_element_type=f32,
         )
     unit_ref[...] = total
@@ -195,19 +223,21 @@
         out_ref[:, s * WIDTH : (s + 1) * WIDTH] = jnp.where(named, affine, 0.0).astype(bf16)
 
 
-def owned_features(code, named, gain, bias, arrived):
+def owned_features(code, named, gain, bias, arrived, part):
     return pl.pallas_call(
         features_kernel,
+        in_specs=[pl.BlockSpec()] * 5 + [pl.BlockSpec(memory_space=pl.ANY)],
         out_shape=(
             jax.ShapeDtypeStruct((OWN_ROWS, 3 * WIDTH), bf16),
             jax.ShapeDtypeStruct((3 * OWN_ROWS, WIDTH), f32),
         ),
         compiler_params=pltpu.CompilerParams(vmem_limit_bytes=VMEM),
+        cost_estimate=cost(FEATURES_COST),
         name="owned_features",
-    )(code, named, gain, bias, arrived)
-
-
-def returning_kernel(code_ref, grad_ref, out_ref):
+    )(code, named, gain, bias, arrived, part)
+
+
+def returning_kernel(code_ref, named_ref, unit_ref, grad_ref, out_ref, totals_ref):
     code = code_ref[...]
     for e in range(BLOCK):
         select = owner_select(code, e)
@@ -219,16 +249,29 @@
                 (((0,), (0,)), ((), ())),
                 preferred_element_type=f32,
             )
-        out_ref[:, e * WIDTH : (e + 1) * WIDTH] = total.astype(bf16)
-
-
-def returning_blocks(code, grad):
+        put_blocks(out_ref, e, total)
+    named = named_ref[...] > 0.0
+    gain_sum = jnp.zeros((1, WIDTH), f32)
+    bias_sum = jnp.zeros((1, WIDTH), f32)
+    for s in range(3):
+        rows = grad_ref[:, s * WIDTH : (s + 1) * WIDTH].astype(f32)
+        rows = jnp.where(named, rows, 0.0)
+        unit = unit_ref[s * OWN_ROWS : (s + 1) * OWN_ROWS, :]
+        gain_sum = gain_sum + jnp.sum(rows * unit, axis=0, keepdims=True)
+        bias_sum = bias_sum + jnp.sum(rows, axis=0, keepdims=True)
+    totals_ref[...] = jnp.concatenate([gain_sum, bias_sum], axis=0)
+
+
+def returning_blocks(code, named, unit_sums, grad):
     return pl.pallas_call(
         returning_kernel,
-        out_shape=jax.ShapeDtypeStruct((SEND, BLOCK * WIDTH), bf16),
+        out_shape=(
+            jax.ShapeDtypeStruct((PEERS, CAP, BLOCK * WIDTH), bf16),
+            jax.ShapeDtypeStruct((2, WIDTH), f32),
+        ),
         compiler_params=pltpu.CompilerParams(vmem_limit_bytes=VMEM),
         name="returning_blocks",
-    )(code, grad)
+    )(code, named, unit_sums, grad)
 
 
 def hidden_grad_kernel(
@@ -252,7 +295,7 @@
         wanted = jnp.where(cell == e, target, -1)
         select = jnp.where(iota((CHUNK, SEND), 1) == wanted, 1.0, 0.0).astype(bf16)
         total = total + jnp.dot(
-            select, returned_ref[:, e * WIDTH : (e + 1) * WIDTH], preferred_element_type=f32
+            select, get_blocks(returned_ref, e), preferred_element_type=f32
         )
     token_ref[...] = total * weight_of(scale)
     gain = gain_ref[...]
@@ -279,7 +322,7 @@
             pl.BlockSpec((BLOCKS_PAD, IMAGES), lambda i: (0, 0)),
             pl.BlockSpec((1, WIDTH), lambda i: (0, 0)),
             pl.BlockSpec((1, CHUNK, WIDTH), lambda i: (0, i, 0)),
-            pl.BlockSpec((SEND, BLOCK * WIDTH), lambda i: (0, 0)),
+            pl.BlockSpec((PEERS, CAP, BLOCK * WIDTH), lambda i: (0, 0, 0)),
         ],
         out_specs=pl.BlockSpec((1, CHUNK, WIDTH), lambda i: (0, i, 0)),
         out_shape=jax.ShapeDtypeStruct((1, TOKENS, WIDTH), bf16),
@@ -289,35 +332,52 @@
     )(tile, peer_row, peer_col, gain, hidden, returned)
 
 
-def projector_kernel(gathered_ref, weight_ref, grad_ref, projected_ref, terms_ref, wide_ref):
+def projector_kernel(
+    core_ref,
+    gathered_ref,
+    weight_ref,
+    grad_ref,
+    totals_ref,
+    after_ref,
+    projected_ref,
+    kept_ref,
+    sent_ref,
+    wide_ref,
+):
+    first = core_ref[0] == 0
+    wide_ref[...] = lax.dot_general(
+        gathered_ref[...], grad_ref[0], (((0,), (0,)), ((), ())), preferred_element_type=f32
+    )
+    rest = TERM_PAD - SHARD - totals_ref.shape[0]
+    totals = jnp.concatenate([totals_ref[...], jnp.zeros((rest, grad_ref.shape[2]), f32)], axis=0)
+    for x in range(NX):
+        for z in range(NZ):
+            at = (z * NX * NC + x * NC) * SHARD
+            low = jnp.concatenate([wide_ref[at : at + SHARD, :], totals], axis=0)
+            high = jnp.concatenate([wide_ref[at + SHARD : at + 2 * SHARD, :], totals], axis=0)
+            kept_ref[x * NZ + z] = jnp.where(first, low, high).astype(bf16)
+            sent_ref[x * NZ + z] = jnp.where(first, high, low).astype(bf16)
     projected_ref[0] = jnp.dot(
         gathered_ref[...], weight_ref[...], preferred_element_type=f32
     ).astype(bf16)
-    wide_ref[...] = lax.dot_general(
-        gathered_ref[...], grad_ref[0], (((0,), (0,)), ((), ())), preferred_element_type=f32
-    )
-    cols = grad_ref.shape[2]
-    pad = jnp.zeros((SHARD_PAD - SHARD, cols), f32)
-    for c in range(NC):
-        for x in range(NX):
-            for z in range(NZ):
-                at = (z * NX * NC + x * NC + c) * SHARD
-                part = jnp.concatenate([wide_ref[at : at + SHARD, :], pad], axis=0)
-                terms_ref[(c * NX + x) * NZ + z] = part.astype(bf16)
-
-
-def projector(gathered, weight, grad):
+
+
+def projector(core, gathered, weight, grad, totals, after):
     rows, cols = grad.shape[1:]
     return pl.pallas_call(
         projector_kernel,
+        in_specs=[pl.BlockSpec(memory_space=pltpu.SMEM)]
+        + [pl.BlockSpec()] * 4
+        + [pl.BlockSpec(memory_space=pl.ANY)],
         out_shape=(
             jax.ShapeDtypeStruct((1, rows, cols), bf16),
-            jax.ShapeDtypeStruct((PEERS, SHARD_PAD, cols), bf16),
+            jax.ShapeDtypeStruct((NX * NZ, TERM_PAD, cols), bf16),
+            jax.ShapeDtypeStruct((NX * NZ, TERM_PAD, cols), bf16),
         ),
         scratch_shapes=[pltpu.VMEM((PEERS * SHARD, cols), f32)],
         compiler_params=pltpu.CompilerParams(vmem_limit_bytes=VMEM),
         name="projector",
-    )(gathered, weight, grad)
+    )(core, gathered, weight, grad, totals, after)
 
 
 def scatter_sum(terms, axis, count):
@@ -335,20 +395,21 @@
     core = lax.axis_index("c")
     me = (lax.axis_index("z") * NX + lax.axis_index("x")) * NC + core
 
+    table = block_owner.reshape(IMAGES, BLOCKS)
+    peers = jnp.pad(table >> 4, ((0, 0), (0, BLOCKS_PAD - BLOCKS)), constant_values=-1)
+    outgoing = pool_tokens(slot_tile, peers, peers.T, hidden)
+
     tile_row = jnp.broadcast_to(slot_tile.astype(bf16)[:, None], (1, cols))
     shard = jnp.concatenate(
         [proj_weight, tile_row, jnp.zeros((SHARD_PAD - SHARD - 1, cols), bf16)], axis=0
     )
     over_z = spread(shard, "z", NZ)
-    mine = spread(over_z, "x", NX).reshape(NX * NZ, SHARD_PAD, cols)
+    over_z, outgoing = lax.optimization_barrier((over_z, outgoing))
+    arrived = lax.all_to_all(outgoing, ("z", "x", "c"), 0, 0, tiled=True)
+    mine = lax.all_gather(over_z, "x", axis=0, tiled=True)
     other = lax.ppermute(mine, "c", [(0, 1), (1, 0)])
 
-    table = block_owner.reshape(IMAGES, BLOCKS)
-    peers = jnp.pad(table >> 4, ((0, 0), (0, BLOCKS_PAD - BLOCKS)), constant_values=-1)
-    outgoing = pool_tokens(slot_tile, peers, peers.T, hidden)
-    arrived = lax.all_to_all(outgoing, ("z", "x", "c"), 0, 0, tiled=True)
-
-    weight, row_part = row_grad_part(core.reshape(1), mine, other, proj_grad)
+    weight, row_part, tiles = row_grad_part(core.reshape(1), mine, other, proj_grad)
     own_grad = lax.psum_scatter(row_part, "dp", scatter_dimension=0, tiled=True)
 
     held = (table >> 4) == me
@@ -362,11 +423,7 @@
     named = jnp.any(held[None] & (slot[None] == slots[:, None, None]), axis=(1, 2))
     named = jnp.repeat(named.astype(f32), BLOCK).reshape(OWN_ROWS, 1)
 
-    ids_mine = mine[:, SHARD, 0].astype(i32).reshape(NX, NZ)
-    ids_other = other[:, SHARD, 0].astype(i32).reshape(NX, NZ)
-    low = jnp.where(core == 0, ids_mine, ids_other)
-    high = jnp.where(core == 0, ids_other, ids_mine)
-    ids = jnp.stack([low, high], axis=-1).transpose(1, 0, 2).reshape(PEERS)
+    ids = tiles[:, 0].astype(i32)
     safe = jnp.maximum(ids, 0)
     image = safe // TILES_IMG
     local = safe % TILES_IMG
@@ -376,27 +433,28 @@
     code = jnp.where(found >= 0, scale[:, None] * OWN + found, -1).reshape(1, SEND)
 
     gain = norm_gain.reshape(1, WIDTH)
-    features, unit_sums = owned_features(code, named, gain, norm_bias.reshape(1, WIDTH), arrived)
+    features, unit_sums = owned_features(
+        code, named, gain, norm_bias.reshape(1, WIDTH), arrived, row_part
+    )
+
+    returning, totals = returning_blocks(code, named, unit_sums, own_grad)
     gathered = lax.all_gather(features, "dp", axis=0, tiled=True)
-
-    returning = returning_blocks(code, own_grad)
     returned = lax.all_to_all(returning, ("z", "x", "c"), 0, 0, tiled=True)
 
-    grads = own_grad.astype(f32).reshape(OWN_ROWS, 3, WIDTH)
-    units = unit_sums.reshape(3, OWN_ROWS, WIDTH).transpose(1, 0, 2)
-    totals = jnp.stack(
-        [jnp.sum(grads * units, axis=(0, 1)), jnp.sum(grads * named[:, :, None], axis=(0, 1))]
-    )
-    for axis in ("dp", "z", "x", "c"):
-        totals = lax.psum(totals, axis)
-
-    projected, terms = projector(gathered, weight, proj_grad)
-    terms = scatter_sum(terms, "c", NC).astype(bf16)
+    totals = lax.psum(totals, "dp").reshape(-1, cols)
+    extra = totals.shape[0]
+    projected, kept, sent = projector(
+        core.reshape(1), gathered, weight, proj_grad, totals, returning
+    )
+    got = lax.ppermute(sent, "c", [(0, 1), (1, 0)])
+    terms = (kept.astype(f32) + got.astype(f32)).astype(bf16)
+    terms, returned = lax.optimization_barrier((terms, returned))
+    hidden_grad = hidden_gradient(slot_tile, peers, peers.T, gain, hidden, returned)
     terms = scatter_sum(terms, "x", NX).astype(bf16)
-    weight_grad = scatter_sum(terms, "z", NZ)[0, :SHARD]
-
-    hidden_grad = hidden_gradient(slot_tile, peers, peers.T, gain, hidden, returned)
-    return projected, weight_grad, hidden_grad, totals[0], totals[1]
+    terms, hidden_grad = lax.optimization_barrier((terms, hidden_grad))
+    summed = scatter_sum(terms, "z", NZ)[0]
+    totals = summed[SHARD : SHARD + extra].reshape(2, WIDTH)
+    return projected, summed[:SHARD], hidden_grad, totals[0], totals[1]
 
 
 def solution(mesh):

time: 298 us -> 220 us (0.74)
  blocking collectives: 107 us -> 55.6 us
  waiting for transfers between devices: 78.3 us -> 48.6 us
  starting transfers between devices: 37.4 us -> 49.8 us
  local copies, waits for them, and re-layouts: 22.6 us -> 11.9 us
  Pallas kernels: 28.3 us -> 31.8 us
  other arithmetic: 8.48 us -> 5.05 us
    psum x4 -> x1, blocking collectives: 61.5 us -> 25 us  [shards(): totals = lax.psum(totals, 'dp').reshape(-1, cols)]
    all_gather x1, waiting for transfers between devices: 33.6 us -> 4.67 us  [shards(): gathered = lax.all_gather(features, 'dp', axis=0, tiled=True)]
    all_to_all x1 -> x0, blocking collectives: 20.4 us -> none  [spread(): return lax.all_to_all(copies, axis, split_axis=0, concat_axis=0, tiled=True)]
    all_gather x0 -> x1, blocking collectives: none -> 13 us  [shards(): mine = lax.all_gather(over_z, 'x', axis=0, tiled=True)]
    all_to_all x4 -> x0, local copies, waits for them, and re-layouts: 8.7 us -> none  [the longest x2 4.36 us: shards(): arrived = lax.all_to_all(outgoing, ('z', 'x', 'c'), 0, 0, tiled=True)]
    all_to_all x2 -> x1, blocking collectives: 25.1 us -> 17.6 us  [scatter_sum(): parts = lax.all_to_all(terms, axis, split_axis=0, concat_axis=0, tiled=True)]
    all_to_all x1, starting transfers between devices: 4.24 us -> 10.9 us  [spread(): return lax.all_to_all(copies, axis, split_axis=0, concat_axis=0, tiled=True)]
    reduce_scatter x1, waiting for transfers between devices: 8.21 us -> 2.65 us  [shards(): own_grad = lax.psum_scatter(row_part, 'dp', scatter_dimension=0, tiled=True)]
  transfers between devices with their start and end apart: 7 -> 8, of which waited for: 5 -> 5; matrix products, arithmetic and copies ran while one was open for 4% -> 2% of each run, Pallas kernels for 6% -> 15%
where the time goes in v2:
time: 220 us; the launch traced here: 218 us
  blocking collectives  55.6 us (25%)
  starting transfers between devices  49.8 us (23%)
  waiting for transfers between devices  48.6 us (22%)
  Pallas kernels  31.8 us (14%)
  between operations  14.9 us (7%)
  local copies, waits for them, and re-layouts  11.9 us (5%)
  other arithmetic  5.05 us (2%)
    all_to_all x1, waiting for transfers between devices, shards(): arrived = lax.all_to_all(outgoing, ('z', 'x', 'c'), 0, 0, tiled=True)  36.8 us
    psum x1, blocking collectives, shards(): totals = lax.psum(totals, 'dp').reshape(-1, cols)  25 us
    all_to_all x1, blocking collectives, scatter_sum(): parts = lax.all_to_all(terms, axis, split_axis=0, concat_axis=0, tiled=True)  17.6 us
    all_to_all x1, starting transfers between devices, shards(): returned = lax.all_to_all(returning, ('z', 'x', 'c'), 0, 0, tiled=True)  14.5 us
    all_gather x1, blocking collectives, shards(): mine = lax.all_gather(over_z, 'x', axis=0, tiled=True)  13 us
    pallas_call x1, Pallas kernels, hidden_gradient(): pl.pallas_call(hidden_grad_kernel, grid=(STEPS,), in_specs=[pl.BlockSpec(...  11.4 us
    all_to_all x1, starting transfers between devices, spread(): return lax.all_to_all(copies, axis, split_axis=0, concat_axis=0, tiled=True)  10.9 us
    all_to_all x1, starting transfers between devices, shards(): arrived = lax.all_to_all(outgoing, ('z', 'x', 'c'), 0, 0, tiled=True)  10.8 us
  transfers between devices with their start and end apart: 8, of which 5 were waited for; matrix products, arithmetic and copies ran while one was open for 2% of the time, Pallas kernels for 15%

profile of v2, /device:TPU:1, one launch (start us, length us, event | category | flops | bytes accessed | tf_op | source)
XLA Modules:
  0.0 217.8 jit_solution(5111999708751014058)
XLA Ops:
  8.0 0.8 maximum_maximum_fusion
  8.8 0.7 broadcast_in_dim.87
  9.5 10.9 %all-to-all-start = ((bf16[8,56,256]{2,1,0:T(8,128)(2,1)}), bf16[8,56,256]{2,1,0:T(8,128)(2,1)S(1)}, u32[]{:S(2)}, u32[]{:S(2)}) async-start(bf16[8,56,256]{2,1,0:T(8,128)(2,1)} %broadcast_in_dim.87), calls=%async_computation | async-start | bytes 458752 | tf_op jit(solution)/shard_map/all_to_all | solution.py:390
  20.4 0.7 broadcast_shift-right-arithmetic_fusion
  21.6 1.4 copy-done.3
  23.0 8.3 %pool_tokens.1 = bf16[64,4,3456]{2,1,0:T(4,128)(2,1)} custom-call(s32[1]{0:T(128)S(6)} %copy.42.tile_ref, s32[4,256]{1,0:T(4,128)S(1)} %pad.4.clone.peer_row_ref, s32[256,4]{1,0:T(8,128)S(1)} %pad_bitcast_fusion.peer_col_ref, bf16[1,729,1152]{2,1,0:T(8,128)(2,1)S(1)} %copy-done.3), custom_call_target="tpu_custom_call" | custom-call | flops 8000000000 | bytes 24000000 | tf_op jit(solution)/shard_map/pool_tokens/pallas_call | solution.py:147
  31.4 0.7 copy-done.5
  32.6 13.0 %all_gather.6.mine_ref = bf16[32,56,256]{2,1,0:T(8,128)(2,1)S(1)} all-gather(bf16[8,56,256]{2,1,0:T(8,128)(2,1)S(1)} %all-to-all-done), channel_id=1, replica_groups=mesh['dp'=8,'z'=8,'x'=4,'c'=2] {'x'}, dimensions={0}, use_global_device_ids=true | all-gather | bytes 1146880 | tf_op jit(solution)/shard_map/all_gather | solution.py:409
  45.6 4.1 %collective-permute-start = (bf16[32,56,256]{2,1,0:T(8,128)(2,1)S(1)}, bf16[32,56,256]{2,1,0:T(8,128)(2,1)S(1)}, u32[]{:S(2)}, u32[]{:S(2)}) collective-permute-start(bf16[32,56,256]{2,1,0:T(8,128)(2,1)S(1)} %all_gather.6.mine_ref), channel_id=1, source_target_pairs={{0,1},{1,0},{2,3},{3,2},{4,5},{5,4},{6,7},{7,6},{8,9},{9,8},{10,11... | collective-permute-start | bytes 2752520 | tf_op jit(solution)/shard_map/ppermute | solution.py:410
  49.7 10.8 %all-to-all-start.1 = ((bf16[64,4,3456]{2,1,0:T(4,128)(2,1)}), bf16[64,4,3456]{2,1,0:T(4,128)(2,1)}, u32[]{:S(2)}, u32[]{:S(2)}) async-start(bf16[64,4,3456]{2,1,0:T(4,128)(2,1)} %pool_tokens.1), calls=%async_computation.1 | async-start | bytes 3538944 | tf_op jit(solution)/shard_map/all_to_all | solution.py:408
  60.6 2.7 %row_grad_part.1 = (bf16[3456,256]{1,0:T(8,128)(2,1)S(1)}, bf16[384,3456]{1,0:T(8,128)(2,1)}, f32[64,128]{1,0:T(8,128)S(1)}) custom-call(s32[1]{0:T(128)} %bitcast.core_ref, bf16[32,56,256]{2,1,0:T(8,128)(2,1)S(1)} %all_gather.6.mine_ref, bf16[32,56,256]{2,1,0:T(8,128)(2,1)S(1)} %collective-permute-done.other_ref, bf16[1,384,256]{2,1,0:T(8,128)(2,1)S(1)} %copy-done.9), custom_call_target="tpu_custom_call" | custom-call | flops 20000000000 | bytes 60000000 | tf_op jit(solution)/shard_map/row_grad_part/pallas_call | solution.py:187
  63.3 1.3 copy-done.1
  66.7 36.8 %all-to-all-done.1.arrived_ref = bf16[64,4,3456]{2,1,0:T(4,128)(2,1)} async-done(((bf16[64,4,3456]{2,1,0:T(4,128)(2,1)}), bf16[64,4,3456]{2,1,0:T(4,128)(2,1)}, u32[]{:S(2)}, u32[]{:S(2)}) %all-to-all-start.1) | async-done | bytes 1769504 | tf_op jit(solution)/shard_map/all_to_all | solution.py:408
  103.4 2.0 owned_features.1
  105.4 0.7 copy-done.8
  106.2 2.6 %reduce-scatter.2.cloned.1.call-done.grad_ref = bf16[48,3456]{1,0:T(8,128)(2,1)} async-done(((bf16[384,3456]{1,0:T(8,128)(2,1)}), bf16[48,3456]{1,0:T(8,128)(2,1)}) %reduce-scatter.2.cloned.1.call-update) | async-done | bytes 331792 | tf_op jit(solution)/shard_map/reduce_scatter | solution.py:413
  108.8 1.0 copy-done.7
  109.8 3.1 %returning_blocks.1 = (bf16[64,4,3456]{2,1,0:T(4,128)(2,1)}, f32[2,1152]{1,0:T(2,128)S(1)}) custom-call(s32[1,256]{1,0:T(1,128)S(1)} %select_n.61.code_ref, f32[48,1]{1,0:T(8,128)S(1)} %reshape_reshape.4.named_ref, f32[144,1152]{1,0:T(8,128)S(1)} %get-tuple-element.27.unit_ref, bf16[48,3456]{1,0:T(8,128)(2,1)S(1)} %copy-done.7), custom_call_target="tpu_custom_call" | custom-call | tf_op jit(solution)/shard_map/returning_blocks/pallas_call | solution.py:266
  112.9 14.5 %all-to-all-start.2 = ((bf16[64,4,3456]{2,1,0:T(4,128)(2,1)}), bf16[64,4,3456]{2,1,0:T(4,128)(2,1)S(1)}, u32[]{:S(2)}, u32[]{:S(2)}) async-start(bf16[64,4,3456]{2,1,0:T(4,128)(2,1)} %get-tuple-element.29.after_ref), calls=%async_computation.3 | async-start | bytes 3538944 | tf_op jit(solution)/shard_map/all_to_all | solution.py:442
  128.0 25.0 %psum.7.totals_ref = f32[9,256]{1,0:T(8,128)S(1)} all-reduce(f32[9,256]{1,0:T(8,128)} %reshape.148), channel_id=1, replica_groups=mesh['dp'=8,'z'=8,'x'=4,'c'=2] {'dp'}, use_global_device_ids=true, to_apply=%region_4.5 | all-reduce | flops 2304 | bytes 18432 | tf_op jit(solution)/shard_map/psum | solution.py:444
  152.9 4.7 %all-gather.2.cloned.1.call-done.gathered_ref = bf16[384,3456]{1,0:T(8,128)(2,1)} async-done(((bf16[48,3456]{1,0:T(8,128)(2,1)}), bf16[384,3456]{1,0:T(8,128)(2,1)}) %all-gather.2.cloned.1.call-update) | async-done | bytes 2654224 | tf_op jit(solution)/shard_map/all_gather | solution.py:441
  157.6 0.9 copy-done.10
  158.5 4.4 %projector.1 = (bf16[1,384,256]{2,1,0:T(8,128)(2,1)}, bf16[32,64,256]{2,1,0:T(8,128)(2,1)S(1)}, bf16[32,64,256]{2,1,0:T(8,128)(2,1)S(1)}) custom-call(s32[1]{0:T(128)} %bitcast.core_ref, bf16[384,3456]{1,0:T(8,128)(2,1)} %all-gather.2.cloned.1.call-done.gathered_ref, bf16[3456,256]{1,0:T(8,128)(2,1)S(1)} %copy-done.2, bf16[1,384,256]{2,1,0:T(8,128)(2,1)S(1)} %copy-done.10, ...), custom_call_target="tpu_custom_call" | custom-call | tf_op jit(solution)/shard_map/projector/pallas_call | solution.py:367
  162.9 5.1 %collective-permute-start.1 = (bf16[32,64,256]{2,1,0:T(8,128)(2,1)S(1)}, bf16[32,64,256]{2,1,0:T(8,128)(2,1)S(1)}, u32[]{:S(2)}, u32[]{:S(2)}) collective-permute-start(bf16[32,64,256]{2,1,0:T(8,128)(2,1)S(1)} %get-tuple-element.32), channel_id=1, source_target_pairs={{0,1},{1,0},{2,3},{3,2},{4,5},{5,4},{6,7},{7,6},{8,9},{9,8},{10,11... | collective-permute-start | bytes 3145736 | tf_op jit(solution)/shard_map/ppermute | solution.py:449
  168.0 2.3 %collective-permute-done.1 = bf16[32,64,256]{2,1,0:T(8,128)(2,1)S(1)} collective-permute-done((bf16[32,64,256]{2,1,0:T(8,128)(2,1)S(1)}, bf16[32,64,256]{2,1,0:T(8,128)(2,1)S(1)}, u32[]{:S(2)}, u32[]{:S(2)}) %collective-permute-start.1) | collective-permute-done | bytes 1048608 | tf_op jit(solution)/shard_map/ppermute | solution.py:449
  170.3 1.4 add_convert_fusion
  171.7 4.4 %all-to-all-start.3 = ((bf16[32,64,256]{2,1,0:T(8,128)(2,1)}), bf16[32,64,256]{2,1,0:T(8,128)(2,1)}, u32[]{:S(2)}, u32[]{:S(2)}) async-start(bf16[32,64,256]{2,1,0:T(8,128)(2,1)} %add_convert_fusion), calls=%async_computation.4 | async-start | bytes 2097152 | tf_op jit(solution)/shard_map/all_to_all | solution.py:384
  176.1 0.9 copy-done.6
  177.0 11.4 %hidden_gradient.1 = bf16[1,729,1152]{2,1,0:T(8,128)(2,1)} custom-call(s32[1]{0:T(128)S(6)} %copy.42.tile_ref, s32[4,256]{1,0:T(4,128)S(1)} %copy-done.14, s32[256,4]{1,0:T(8,128)S(1)} %copy-done.6, f32[1,1152]{1,0:T(1,128)S(1)} %copy-done.12, bf16[1,729,1152]{2,1,0:T(8,128)(2,1)S(1)} %copy-done.4, bf16[64,4,3456]{2,1,0:T(4,128)(2,1)S(1)} %all-to-all-done.2.returned_ref), custom_call_target="tpu_custom_call" | custom-call | tf_op jit(solution)/shard_map/hidden_gradient/pallas_call | solution.py:316
  188.4 2.3 %all-to-all-done.3 = bf16[32,64,256]{2,1,0:T(8,128)(2,1)} async-done(((bf16[32,64,256]{2,1,0:T(8,128)(2,1)}), bf16[32,64,256]{2,1,0:T(8,128)(2,1)}, u32[]{:S(2)}, u32[]{:S(2)}) %all-to-all-start.3) | async-done | bytes 1048608 | tf_op jit(solution)/shard_map/all_to_all | solution.py:384
  190.6 1.4 reduce_sum.23
  192.1 17.6 %all_to_all.25 = bf16[8,64,256]{2,1,0:T(8,128)(2,1)S(1)} all-to-all(bf16[8,64,256]{2,1,0:T(8,128)(2,1)S(1)} %reduce_sum.23), channel_id=1, replica_groups=mesh['dp'=8,'z'=8,'x'=4,'c'=2] {'z'}, dimensions={0} | all-to-all | bytes 524288 | tf_op jit(solution)/shard_map/all_to_all | solution.py:384
  (66 shorter events, 5.3 us)
Async XLA Ops:
  9.5 23.1 %all-to-all-start = ((bf16[8,56,256]{2,1,0:T(8,128)(2,1)}), bf16[8,56,256]{2,1,0:T(8,128)(2,1)S(1)}, u32[]{:S(2)}, u32[]{:S(2)}) async-start(bf16[8,56,256]{2,1,0:T(8,128)(2,1)} %broadcast_in_dim.87), calls=%async_computation | async-start | bytes 458752 | tf_op jit(solution)/shard_map/all_to_all | solution.py:390
  21.6 1.5 copy-start.3
  31.4 0.7 copy-start.5
  32.0 0.6 copy-start.13
  45.6 15.0 %copy-start.9 = (bf16[1,384,256]{2,1,0:T(8,128)(2,1)S(1)}, bf16[1,384,256]{2,1,0:T(8,128)(2,1)}, u32[]{:S(2)}) copy-start(bf16[1,384,256]{2,1,0:T(8,128)(2,1)} %grad_ref.3) | copy-start | bytes 589828
  45.6 15.0 %collective-permute-start = (bf16[32,56,256]{2,1,0:T(8,128)(2,1)S(1)}, bf16[32,56,256]{2,1,0:T(8,128)(2,1)S(1)}, u32[]{:S(2)}, u32[]{:S(2)}) collective-permute-start(bf16[32,56,256]{2,1,0:T(8,128)(2,1)S(1)} %all_gather.6.mine_ref), channel_id=1, source_target_pairs={{0,1},{1,0},{2,3},{3,2},{4,5},{5,4},{6,7},{7,6},{8,9},{9,8},{10,11... | collective-permute-start | bytes 2752520 | tf_op jit(solution)/shard_map/ppermute | solution.py:410
  49.7 53.7 %all-to-all-start.1 = ((bf16[64,4,3456]{2,1,0:T(4,128)(2,1)}), bf16[64,4,3456]{2,1,0:T(4,128)(2,1)}, u32[]{:S(2)}, u32[]{:S(2)}) async-start(bf16[64,4,3456]{2,1,0:T(4,128)(2,1)} %pool_tokens.1), calls=%async_computation.1 | async-start | bytes 3538944 | tf_op jit(solution)/shard_map/all_to_all | solution.py:408
  60.5 48.3 %reduce-scatter.2.cloned.1.call-start = ((), (), s32[]{:S(2)}) async-start(), calls=%async_computation.7 | async-start | bytes 2985984 | tf_op jit(solution)/shard_map/reduce_scatter | solution.py:413
  63.3 1.3 copy-start.1
  64.5 0.7 copy-start.15
  64.5 0.7 copy-start.16
  64.5 38.9 %copy-start = (bf16[384,3456]{1,0:T(8,128)(2,1)S(1)}, bf16[384,3456]{1,0:T(8,128)(2,1)}, u32[]{:S(2)}) copy-start(bf16[384,3456]{1,0:T(8,128)(2,1)} %get-tuple-element.24.part_ref) | copy-start | bytes 7962628
  64.6 93.0 %all-gather.2.cloned.1.call-start = ((), (), s32[]{:S(2)}) async-start(), calls=%async_computation.6 | async-start | bytes 2985984 | tf_op jit(solution)/shard_map/all_gather | solution.py:441
  65.2 40.2 %copy-start.11 = (f32[1,1152]{1,0:T(1,128)}, f32[1,1152]{1,0:T(1,128)S(1)}, u32[]{:S(2)}) copy-start(f32[1,1152]{1,0:T(1,128)S(1)} %reshape.146.gain_ref) | copy-start | bytes 13828
  105.4 0.7 copy-start.8
  108.8 1.0 copy-start.7
  112.9 44.7 %copy-start.2 = (bf16[3456,256]{1,0:T(8,128)(2,1)S(1)}, bf16[3456,256]{1,0:T(8,128)(2,1)}, u32[]{:S(2)}) copy-start(bf16[3456,256]{1,0:T(8,128)(2,1)} %copy-done.1) | copy-start | bytes 5308420
  112.9 58.8 %all-to-all-start.2 = ((bf16[64,4,3456]{2,1,0:T(4,128)(2,1)}), bf16[64,4,3456]{2,1,0:T(4,128)(2,1)S(1)}, u32[]{:S(2)}, u32[]{:S(2)}) async-start(bf16[64,4,3456]{2,1,0:T(4,128)(2,1)} %get-tuple-element.29.after_ref), calls=%async_computation.3 | async-start | bytes 3538944 | tf_op jit(solution)/shard_map/all_to_all | solution.py:442
  157.6 0.9 copy-start.10
  162.9 7.4 %collective-permute-start.1 = (bf16[32,64,256]{2,1,0:T(8,128)(2,1)S(1)}, bf16[32,64,256]{2,1,0:T(8,128)(2,1)S(1)}, u32[]{:S(2)}, u32[]{:S(2)}) collective-permute-start(bf16[32,64,256]{2,1,0:T(8,128)(2,1)S(1)} %get-tuple-element.32), channel_id=1, source_target_pairs={{0,1},{1,0},{2,3},{3,2},{4,5},{5,4},{6,7},{7,6},{8,9},{9,8},{10,11... | collective-permute-start | bytes 3145736 | tf_op jit(solution)/shard_map/ppermute | solution.py:449
  171.6 4.4 %copy-start.4 = (bf16[1,729,1152]{2,1,0:T(8,128)(2,1)S(1)}, bf16[1,729,1152]{2,1,0:T(8,128)(2,1)}, u32[]{:S(2)}) copy-start(bf16[1,729,1152]{2,1,0:T(8,128)(2,1)} %hidden_ref.3) | copy-start | bytes 5038852
  171.6 4.4 %copy-start.12 = (f32[1,1152]{1,0:T(1,128)S(1)}, f32[1,1152]{1,0:T(1,128)}, u32[]{:S(2)}) copy-start(f32[1,1152]{1,0:T(1,128)} %copy-done.11) | copy-start | bytes 13828
  171.6 4.4 %copy-start.14 = (s32[4,256]{1,0:T(4,128)S(1)}, s32[4,256]{1,0:T(4,128)}, u32[]{:S(2)}) copy-start(s32[4,256]{1,0:T(4,128)} %copy-done.13) | copy-start | bytes 12292
  171.7 19.0 %all-to-all-start.3 = ((bf16[32,64,256]{2,1,0:T(8,128)(2,1)}), bf16[32,64,256]{2,1,0:T(8,128)(2,1)}, u32[]{:S(2)}, u32[]{:S(2)}) async-start(bf16[32,64,256]{2,1,0:T(8,128)(2,1)} %add_convert_fusion), calls=%async_computation.4 | async-start | bytes 2097152 | tf_op jit(solution)/shard_map/all_to_all | solution.py:384
  176.1 0.9 copy-start.6
Sparse Core Ops, SparseCore 0:
  64.7 44.0 reduce-scatter.1
  111.5 46.0 all-gather.1

commit v3 on v2

--- a/solution.py
+++ b/solution.py
@@ -26,10 +26,10 @@
 STEPS = 4
 ROWS = 32
 EPS = 1e-6
-VMEM = 48 * 1024 * 1024
-
-FEATURES_COST = 40
-ROW_GRAD_COST = 20
+VMEM = 32 * 1024 * 1024
+
+FEATURES_COST = 2
+ROW_GRAD_COST = 3
 POOL_COST = 8
 
 f32 = jnp.float32
@@ -88,13 +88,6 @@
     return row, col, jnp.where(row == col, 1.0, 0.0)
 
 
-def unit_rows_of(values):
-    centered = values - jnp.sum(values, axis=-1, keepdims=True) * (1.0 / WIDTH)
-    var = jnp.sum(centered * centered, axis=-1, keepdims=True) * (1.0 / WIDTH)
-    inverse = lax.rsqrt(var + EPS)
-    return centered * inverse, inverse
-
-
 def put_blocks(ref, e, rows):
     cell = slice(e * WIDTH, (e + 1) * WIDTH)
     ref[:, :, cell] = rows.reshape(PEERS, CAP, WIDTH).astype(bf16)
@@ -105,12 +98,19 @@
     return ref[:, :, cell].reshape(SEND, WIDTH)
 
 
-def pool_kernel(tile_ref, peer_row_ref, peer_col_ref, hidden_ref, out_ref, unit_ref):
+def pool_kernel(tile_ref, peer_row_ref, peer_col_ref, hidden_ref, out_ref, stats_ref, unit_ref):
     step = pl.program_id(0)
 
     def norm_rows(n, carry):
         start = pl.multiple_of(n * ROWS, ROWS)
-        unit, _ = unit_rows_of(hidden_ref[0, pl.ds(start, ROWS), :].astype(f32))
+        values = hidden_ref[0, pl.ds(start, ROWS), :].astype(f32)
+        mean = jnp.sum(values, axis=-1, keepdims=True) * (1.0 / WIDTH)
+        centered = values - mean
+        var = jnp.sum(centered * centered, axis=-1, keepdims=True) * (1.0 / WIDTH)
+        inverse = lax.rsqrt(var + EPS)
+        unit = centered * inverse
+        lane = iota((ROWS, stats_ref.shape[1]), 1)
+        stats_ref[pl.ds(start, ROWS), :] = jnp.where(lane == 0, mean, inverse)
         row = step * CHUNK + start
         valid = row + iota((ROWS, 1), 0) < TOKENS
         unit_ref[pl.ds(pl.multiple_of(row, ROWS), ROWS), :] = jnp.where(valid, unit, 0.0).astype(
@@ -153,8 +153,14 @@
             pl.BlockSpec((BLOCKS_PAD, IMAGES), lambda i: (0, 0)),
             pl.BlockSpec((1, CHUNK, WIDTH), lambda i: (0, i, 0)),
         ],
-        out_specs=pl.BlockSpec((PEERS, CAP, BLOCK * WIDTH), lambda i: (0, 0, 0)),
-        out_shape=jax.ShapeDtypeStruct((PEERS, CAP, BLOCK * WIDTH), bf16),
+        out_specs=(
+            pl.BlockSpec((PEERS, CAP, BLOCK * WIDTH), lambda i: (0, 0, 0)),
+            pl.BlockSpec((CHUNK, 128), lambda i: (i, 0)),
+        ),
+        out_shape=(
+            jax.ShapeDtypeStruct((PEERS, CAP, BLOCK * WIDTH), bf16),
+            jax.ShapeDtypeStruct((STEPS * CHUNK, 128), f32),
+        ),
         scratch_shapes=[pltpu.VMEM((STEPS * CHUNK, WIDTH), bf16)],
         compiler_params=pltpu.CompilerParams(vmem_limit_bytes=VMEM),
         cost_estimate=cost(POOL_COST),
@@ -168,8 +174,8 @@
     first = core_ref[0] == 0
     for x in range(NX):
         for z in range(NZ):
-            mine = mine_ref[x * NZ + z].astype(f32)
-            other = other_ref[x * NZ + z].astype(f32)
+            mine = mine_ref[z * NX + x].astype(f32)
+            other = other_ref[z * NX + x].astype(f32)
             low, high = jnp.where(first, mine, other), jnp.where(first, other, mine)
             for c, block in enumerate((low, high)):
                 peer = (z * NX + x) * NC + c
@@ -206,7 +212,7 @@
 
 
 def features_kernel(
-    code_ref, named_ref, gain_ref, bias_ref, arrived_ref, part_ref, out_ref, unit_ref
+    code_ref, named_ref, gain_ref, bias_ref, arrived_ref, out_ref, unit_ref
 ):
     code = code_ref[...]
     total = jnp.zeros((3 * OWN_ROWS, WIDTH), f32)
@@ -223,10 +229,9 @@
         out_ref[:, s * WIDTH : (s + 1) * WIDTH] = jnp.where(named, affine, 0.0).astype(bf16)
 
 
-def owned_features(code, named, gain, bias, arrived, part):
+def owned_features(code, named, gain, bias, arrived):
     return pl.pallas_call(
         features_kernel,
-        in_specs=[pl.BlockSpec()] * 5 + [pl.BlockSpec(memory_space=pl.ANY)],
         out_shape=(
             jax.ShapeDtypeStruct((OWN_ROWS, 3 * WIDTH), bf16),
             jax.ShapeDtypeStruct((3 * OWN_ROWS, WIDTH), f32),
@@ -234,22 +239,19 @@
         compiler_params=pltpu.CompilerParams(vmem_limit_bytes=VMEM),
         cost_estimate=cost(FEATURES_COST),
         name="owned_features",
-    )(code, named, gain, bias, arrived, part)
+    )(code, named, gain, bias, arrived)
 
 
 def returning_kernel(code_ref, named_ref, unit_ref, grad_ref, out_ref, totals_ref):
     code = code_ref[...]
+    stacked = jnp.concatenate(
+        [grad_ref[:, s * WIDTH : (s + 1) * WIDTH] for s in range(3)], axis=0
+    )
     for e in range(BLOCK):
-        select = owner_select(code, e)
-        total = jnp.zeros((SEND, WIDTH), f32)
-        for s in range(3):
-            total = total + lax.dot_general(
-                select[s * OWN_ROWS : (s + 1) * OWN_ROWS],
-                grad_ref[:, s * WIDTH : (s + 1) * WIDTH],
-                (((0,), (0,)), ((), ())),
-                preferred_element_type=f32,
-            )
-        put_blocks(out_ref, e, total)
+        returned = lax.dot_general(
+            owner_select(code, e), stacked, (((0,), (0,)), ((), ())), preferred_element_type=f32
+        )
+        put_blocks(out_ref, e, returned)
     named = named_ref[...] > 0.0
     gain_sum = jnp.zeros((1, WIDTH), f32)
     bias_sum = jnp.zeros((1, WIDTH), f32)
@@ -275,11 +277,26 @@
 
 
 def hidden_grad_kernel(
-    tile_ref, peer_row_ref, peer_col_ref, gain_ref, hidden_ref, returned_ref, out_ref, token_ref
+    tile_ref,
+    peer_row_ref,
+    peer_col_ref,
+    gain_ref,
+    hidden_ref,
+    stats_ref,
+    returned_ref,
+    out_ref,
+    token_ref,
+    blocks_ref,
 ):
     step = pl.program_id(0)
     tile = tile_ref[0]
     image, scale, row, col = tile_geometry(tile)
+
+    @pl.when(step == 0)
+    def _():
+        for e in range(BLOCK):
+            blocks_ref[e] = get_blocks(returned_ref, e)
+
     peer, _, same = same_owner(image, peer_row_ref, peer_col_ref)
     shape = (BLOCKS_PAD, BLOCKS_PAD)
     earlier = jnp.where(iota(shape, 0) < iota(shape, 1), same, 0.0)
@@ -294,25 +311,21 @@
     for e in range(BLOCK):
         wanted = jnp.where(cell == e, target, -1)
         select = jnp.where(iota((CHUNK, SEND), 1) == wanted, 1.0, 0.0).astype(bf16)
-        total = total + jnp.dot(
-            select, get_blocks(returned_ref, e), preferred_element_type=f32
-        )
-    token_ref[...] = total * weight_of(scale)
-    gain = gain_ref[...]
-
-    def norm_rows(n, carry):
-        start = pl.multiple_of(n * ROWS, ROWS)
-        unit, inverse = unit_rows_of(hidden_ref[0, pl.ds(start, ROWS), :].astype(f32))
-        scaled = token_ref[pl.ds(start, ROWS), :] * gain
-        mean = jnp.sum(scaled, axis=-1, keepdims=True) * (1.0 / WIDTH)
+        total = total + jnp.dot(select, blocks_ref[e], preferred_element_type=f32)
+    token_ref[...] = total
+    gain = gain_ref[...] * weight_of(scale)
+
+    for n in range(CHUNK // ROWS):
+        rows = slice(n * ROWS, (n + 1) * ROWS)
+        mean, inverse = stats_ref[rows, 0:1], stats_ref[rows, 1:2]
+        unit = (hidden_ref[0, rows, :].astype(f32) - mean) * inverse
+        scaled = token_ref[rows, :] * gain
+        level = jnp.sum(scaled, axis=-1, keepdims=True) * (1.0 / WIDTH)
         cross = jnp.sum(scaled * unit, axis=-1, keepdims=True) * (1.0 / WIDTH)
-        out_ref[0, pl.ds(start, ROWS), :] = (inverse * (scaled - mean - unit * cross)).astype(bf16)
-        return carry
-
-    lax.fori_loop(0, CHUNK // ROWS, norm_rows, 0)
-
-
-def hidden_gradient(tile, peer_row, peer_col, gain, hidden, returned):
+        out_ref[0, rows, :] = (inverse * (scaled - level - unit * cross)).astype(bf16)
+
+
+def hidden_gradient(tile, peer_row, peer_col, gain, hidden, stats, returned):
     return pl.pallas_call(
         hidden_grad_kernel,
         grid=(STEPS,),
@@ -322,67 +335,87 @@
             pl.BlockSpec((BLOCKS_PAD, IMAGES), lambda i: (0, 0)),
             pl.BlockSpec((1, WIDTH), lambda i: (0, 0)),
             pl.BlockSpec((1, CHUNK, WIDTH), lambda i: (0, i, 0)),
+            pl.BlockSpec((CHUNK, 128), lambda i: (i, 0)),
             pl.BlockSpec((PEERS, CAP, BLOCK * WIDTH), lambda i: (0, 0, 0)),
         ],
         out_specs=pl.BlockSpec((1, CHUNK, WIDTH), lambda i: (0, i, 0)),
         out_shape=jax.ShapeDtypeStruct((1, TOKENS, WIDTH), bf16),
-        scratch_shapes=[pltpu.VMEM((CHUNK, WIDTH), f32)],
+        scratch_shapes=[
+            pltpu.VMEM((CHUNK, WIDTH), f32),
+            pltpu.VMEM((BLOCK, SEND, WIDTH), bf16),
+        ],
         compiler_params=pltpu.CompilerParams(vmem_limit_bytes=VMEM),
         name="hidden_gradient",
-    )(tile, peer_row, peer_col, gain, hidden, returned)
-
-
-def projector_kernel(
-    core_ref,
-    gathered_ref,
-    weight_ref,
-    grad_ref,
-    totals_ref,
-    after_ref,
-    projected_ref,
-    kept_ref,
-    sent_ref,
-    wide_ref,
+    )(tile, peer_row, peer_col, gain, hidden, stats, returned)
+
+
+def weight_terms_kernel(
+    core_ref, gathered_ref, grad_ref, totals_ref, kept_ref, sent_ref, done_ref, wide_ref
 ):
+    done_ref[...] = jnp.zeros(done_ref.shape, f32)
     first = core_ref[0] == 0
     wide_ref[...] = lax.dot_general(
         gathered_ref[...], grad_ref[0], (((0,), (0,)), ((), ())), preferred_element_type=f32
     )
     rest = TERM_PAD - SHARD - totals_ref.shape[0]
     totals = jnp.concatenate([totals_ref[...], jnp.zeros((rest, grad_ref.shape[2]), f32)], axis=0)
-    for x in range(NX):
-        for z in range(NZ):
+    for z in range(NZ):
+        for x in range(NX):
             at = (z * NX * NC + x * NC) * SHARD
             low = jnp.concatenate([wide_ref[at : at + SHARD, :], totals], axis=0)
             high = jnp.concatenate([wide_ref[at + SHARD : at + 2 * SHARD, :], totals], axis=0)
-            kept_ref[x * NZ + z] = jnp.where(first, low, high).astype(bf16)
-            sent_ref[x * NZ + z] = jnp.where(first, high, low).astype(bf16)
+            kept_ref[z * NX + x] = jnp.where(first, low, high).astype(bf16)
+            sent_ref[z * NX + x] = jnp.where(first, high, low).astype(bf16)
+
+
+def weight_terms(core, gathered, grad, totals):
+    cols = grad.shape[2]
+    return pl.pallas_call(
+        weight_terms_kernel,
+        in_specs=[pl.BlockSpec(memory_space=pltpu.SMEM)] + [pl.BlockSpec()] * 3,
+        out_shape=(jax.ShapeDtypeStruct((NZ * NX, TERM_PAD, cols), bf16),) * 2
+        + (jax.ShapeDtypeStruct((8, 128), f32),),
+        scratch_shapes=[pltpu.VMEM((PEERS * SHARD, cols), f32)],
+        compiler_params=pltpu.CompilerParams(vmem_limit_bytes=VMEM),
+        name="weight_terms",
+    )(core, gathered, grad, totals)
+
+
+def project_kernel(gathered_ref, weight_ref, after_ref, projected_ref):
     projected_ref[0] = jnp.dot(
         gathered_ref[...], weight_ref[...], preferred_element_type=f32
     ).astype(bf16)
 
 
-def projector(core, gathered, weight, grad, totals, after):
-    rows, cols = grad.shape[1:]
-    return pl.pallas_call(
-        projector_kernel,
-        in_specs=[pl.BlockSpec(memory_space=pltpu.SMEM)]
-        + [pl.BlockSpec()] * 4
-        + [pl.BlockSpec(memory_space=pl.ANY)],
+def project(gathered, weight, after):
+    return pl.pallas_call(
+        project_kernel,
+        in_specs=[pl.BlockSpec()] * 2 + [pl.BlockSpec(memory_space=pl.ANY)],
+        out_shape=jax.ShapeDtypeStruct((1, gathered.shape[0], weight.shape[1]), bf16),
+        compiler_params=pltpu.CompilerParams(vmem_limit_bytes=VMEM),
+        name="project",
+    )(gathered, weight, after)
+
+
+def weight_sum_kernel(parts_ref, weight_ref, totals_ref):
+    total = parts_ref[0].astype(f32)
+    for n in range(1, parts_ref.shape[0]):
+        total = total + parts_ref[n].astype(f32)
+    weight_ref[...] = total[:SHARD]
+    totals_ref[...] = total[SHARD : SHARD + totals_ref.shape[0]]
+
+
+def weight_sum(parts, extra):
+    cols = parts.shape[2]
+    return pl.pallas_call(
+        weight_sum_kernel,
         out_shape=(
-            jax.ShapeDtypeStruct((1, rows, cols), bf16),
-            jax.ShapeDtypeStruct((NX * NZ, TERM_PAD, cols), bf16),
-            jax.ShapeDtypeStruct((NX * NZ, TERM_PAD, cols), bf16),
-        ),
-        scratch_shapes=[pltpu.VMEM((PEERS * SHARD, cols), f32)],
-        compiler_params=pltpu.CompilerParams(vmem_limit_bytes=VMEM),
-        name="projector",
-    )(core, gathered, weight, grad, totals, after)
-
-
-def scatter_sum(terms, axis, count):
-    parts = lax.all_to_all(terms, axis, split_axis=0, concat_axis=0, tiled=True)
-    return jnp.sum(parts.reshape((count, -1) + parts.shape[1:]).astype(f32), axis=0)
+            jax.ShapeDtypeStruct((SHARD, cols), f32),
+            jax.ShapeDtypeStruct((extra, cols), f32),
+        ),
+        compiler_params=pltpu.CompilerParams(vmem_limit_bytes=VMEM),
+        name="weight_sum",
+    )(parts)
 
 
 def spread(shard, axis, count):
@@ -397,16 +430,15 @@
 
     table = block_owner.reshape(IMAGES, BLOCKS)
     peers = jnp.pad(table >> 4, ((0, 0), (0, BLOCKS_PAD - BLOCKS)), constant_values=-1)
-    outgoing = pool_tokens(slot_tile, peers, peers.T, hidden)
+    outgoing, stats = pool_tokens(slot_tile, peers, peers.T, hidden)
 
     tile_row = jnp.broadcast_to(slot_tile.astype(bf16)[:, None], (1, cols))
     shard = jnp.concatenate(
         [proj_weight, tile_row, jnp.zeros((SHARD_PAD - SHARD - 1, cols), bf16)], axis=0
     )
-    over_z = spread(shard, "z", NZ)
-    over_z, outgoing = lax.optimization_barrier((over_z, outgoing))
+    mine = spread(shard, ("z", "x"), NZ * NX)
+    mine, outgoing = lax.optimization_barrier((mine, outgoing))
     arrived = lax.all_to_all(outgoing, ("z", "x", "c"), 0, 0, tiled=True)
-    mine = lax.all_gather(over_z, "x", axis=0, tiled=True)
     other = lax.ppermute(mine, "c", [(0, 1), (1, 0)])
 
     weight, row_part, tiles = row_grad_part(core.reshape(1), mine, other, proj_grad)
@@ -434,7 +466,7 @@
 
     gain = norm_gain.reshape(1, WIDTH)
     features, unit_sums = owned_features(
-        code, named, gain, norm_bias.reshape(1, WIDTH), arrived, row_part
+        code, named, gain, norm_bias.reshape(1, WIDTH), arrived
     )
 
     returning, totals = returning_blocks(code, named, unit_sums, own_grad)
@@ -443,18 +475,16 @@
 
     totals = lax.psum(totals, "dp").reshape(-1, cols)
     extra = totals.shape[0]
-    projected, kept, sent = projector(
-        core.reshape(1), gathered, weight, proj_grad, totals, returning
-    )
+    kept, sent, done = weight_terms(core.reshape(1), gathered, proj_grad, totals)
+    projected = project(gathered, weight, done)
     got = lax.ppermute(sent, "c", [(0, 1), (1, 0)])
     terms = (kept.astype(f32) + got.astype(f32)).astype(bf16)
     terms, returned = lax.optimization_barrier((terms, returned))
-    hidden_grad = hidden_gradient(slot_tile, peers, peers.T, gain, hidden, returned)
-    terms = scatter_sum(terms, "x", NX).astype(bf16)
-    terms, hidden_grad = lax.optimization_barrier((terms, hidden_grad))
-    summed = scatter_sum(terms, "z", NZ)[0]
-    totals = summed[SHARD : SHARD + extra].reshape(2, WIDTH)
-    return projected, summed[:SHARD], hidden_grad, totals[0], totals[1]
+    hidden_grad = hidden_gradient(slot_tile, peers, peers.T, gain, hidden, stats, returned)
+    parts = lax.all_to_all(terms, ("z", "x"), split_axis=0, concat_axis=0, tiled=True)
+    weight_grad, totals = weight_sum(parts, extra)
+    totals = totals.reshape(2, WIDTH)
+    return projected, weight_grad, hidden_grad, totals[0], totals[1]
 
 
 def solution(mesh):

time: 220 us -> 208 us (0.945)
  waiting for transfers between devices: 48.6 us -> 80.7 us
  blocking collectives: 55.6 us -> 26.4 us
  Pallas kernels: 31.8 us -> 26.4 us
  local copies, waits for them, and re-layouts: 11.9 us -> 8.29 us
  starting transfers between devices: 49.8 us -> 46.3 us
    all_to_all x1 -> x0, blocking collectives: 17.6 us -> none  [scatter_sum(): parts = lax.all_to_all(terms, axis, split_axis=0, concat_axis=0, tiled=True)]
    all_to_all x1, waiting for transfers between devices: 0.01 us -> 14.6 us  [spread(): return lax.all_to_all(copies, axis, split_axis=0, concat_axis=0, tiled=True)]
    all_to_all x1, waiting for transfers between devices: 2.27 us -> 16.1 us  [shards(): lax.all_to_all(terms, ('z', 'x'), split_axis=0, concat_axis=0, tiled=True)]
    all_gather x1 -> x0, blocking collectives: 13 us -> none  [shards(): mine = lax.all_gather(over_z, 'x', axis=0, tiled=True)]
    all_to_all x1, starting transfers between devices: 14.5 us -> 6.89 us  [shards(): returned = lax.all_to_all(returning, ('z', 'x', 'c'), 0, 0, tiled=True)]
    all_to_all x1, starting transfers between devices: 10.8 us -> 5.78 us  [shards(): arrived = lax.all_to_all(outgoing, ('z', 'x', 'c'), 0, 0, tiled=True)]
    all_to_all x1, starting transfers between devices: 4.38 us -> 9.23 us  [shards(): lax.all_to_all(terms, ('z', 'x'), split_axis=0, concat_axis=0, tiled=True)]
    all_to_all x1, waiting for transfers between devices: 36.8 us -> 41.4 us  [shards(): arrived = lax.all_to_all(outgoing, ('z', 'x', 'c'), 0, 0, tiled=True)]
  transfers between devices with their start and end apart: 8 -> 8, of which waited for: 5 -> 7; matrix products, arithmetic and copies ran while one was open for 2% -> 2% of each run, Pallas kernels for 15% -> 11%
where the time goes in v3:
time: 208 us; the launch traced here: 206 us
  waiting for transfers between devices  80.7 us (39%)
  starting transfers between devices  46.3 us (22%)
  Pallas kernels  26.4 us (13%)
  blocking collectives  26.4 us (13%)
  between operations  15 us (7%)
  local copies, waits for them, and re-layouts  8.29 us (4%)
  other arithmetic  2.87 us (1%)
    all_to_all x1, waiting for transfers between devices, shards(): arrived = lax.all_to_all(outgoing, ('z', 'x', 'c'), 0, 0, tiled=True)  41.4 us
    psum x1, blocking collectives, shards(): totals = lax.psum(totals, 'dp').reshape(-1, cols)  26.4 us
    all_to_all x1, waiting for transfers between devices, shards(): lax.all_to_all(terms, ('z', 'x'), split_axis=0, concat_axis=0, tiled=True)  16.1 us
    all_to_all x1, waiting for transfers between devices, spread(): return lax.all_to_all(copies, axis, split_axis=0, concat_axis=0, tiled=True)  14.6 us
    all_to_all x1, starting transfers between devices, spread(): return lax.all_to_all(copies, axis, split_axis=0, concat_axis=0, tiled=True)  13.7 us
    all_to_all x1, starting transfers between devices, shards(): lax.all_to_all(terms, ('z', 'x'), split_axis=0, concat_axis=0, tiled=True)  9.23 us
    pallas_call x1, Pallas kernels, pool_tokens(): pl.pallas_call(pool_kernel, grid=(STEPS,), in_specs=[pl.BlockSpec(memory_...  8.29 us
    pallas_call x1, Pallas kernels, hidden_gradient(): pl.pallas_call(hidden_grad_kernel, grid=(STEPS,), in_specs=[pl.BlockSpec(...  7.14 us
  transfers between devices with their start and end apart: 8, of which 7 were waited for; matrix products, arithmetic and copies ran while one was open for 2% of the time, Pallas kernels for 11%

profile of v3, /device:TPU:1, one launch (start us, length us, event | category | flops | bytes accessed | tf_op | source)
XLA Modules:
  0.0 206.1 jit_solution(3305803574029107348)
XLA Ops:
  8.0 0.8 maximum_maximum_fusion
  8.8 1.0 broadcast_in_dim.87
  9.8 13.7 %all-to-all-start = ((bf16[32,56,256]{2,1,0:T(8,128)(2,1)}), bf16[32,56,256]{2,1,0:T(8,128)(2,1)S(1)}, u32[]{:S(2)}, u32[]{:S(2)}) async-start(bf16[32,56,256]{2,1,0:T(8,128)(2,1)} %broadcast_in_dim.87), calls=%async_computation | async-start | bytes 1835008 | tf_op jit(solution)/shard_map/all_to_all | solution.py:423
  24.1 8.3 %pool_tokens.1 = (bf16[64,4,3456]{2,1,0:T(4,128)(2,1)}, f32[768,128]{1,0:T(8,128)S(1)}) custom-call(s32[1]{0:T(128)S(6)} %copy.35.tile_ref, s32[4,256]{1,0:T(4,128)S(1)} %pad.4.clone.peer_row_ref, s32[256,4]{1,0:T(8,128)S(1)} %pad_bitcast_fusion.peer_col_ref, bf16[1,729,1152]{2,1,0:T(8,128)(2,1)S(1)} %copy-done.4), custom_call_target="tpu_custom_call" | custom-call | flops 8000000000 | bytes 24000000 | tf_op jit(solution)/shard_map/pool_tokens/pallas_call | solution.py:147
  32.4 14.6 %all-to-all-done.mine_ref = bf16[32,56,256]{2,1,0:T(8,128)(2,1)S(1)} async-done(((bf16[32,56,256]{2,1,0:T(8,128)(2,1)}), bf16[32,56,256]{2,1,0:T(8,128)(2,1)S(1)}, u32[]{:S(2)}, u32[]{:S(2)}) %all-to-all-start) | async-done | bytes 917536 | tf_op jit(solution)/shard_map/all_to_all | solution.py:423
  47.0 5.0 %collective-permute-start = (bf16[32,56,256]{2,1,0:T(8,128)(2,1)S(1)}, bf16[32,56,256]{2,1,0:T(8,128)(2,1)S(1)}, u32[]{:S(2)}, u32[]{:S(2)}) collective-permute-start(bf16[32,56,256]{2,1,0:T(8,128)(2,1)S(1)} %all-to-all-done.mine_ref), channel_id=1, source_target_pairs={{0,1},{1,0},{2,3},{3,2},{4,5},{5,4},{6,7},{7,6},{8,9},{9,8},{10,11... | collective-permute-start | bytes 2752520 | tf_op jit(solution)/shard_map/ppermute | solution.py:442
  52.0 2.1 %collective-permute-done.other_ref = bf16[32,56,256]{2,1,0:T(8,128)(2,1)S(1)} collective-permute-done((bf16[32,56,256]{2,1,0:T(8,128)(2,1)S(1)}, bf16[32,56,256]{2,1,0:T(8,128)(2,1)S(1)}, u32[]{:S(2)}, u32[]{:S(2)}) %collective-permute-start) | collective-permute-done | bytes 917536 | tf_op jit(solution)/shard_map/ppermute | solution.py:442
  54.1 2.7 %row_grad_part.1 = (bf16[3456,256]{1,0:T(8,128)(2,1)S(1)}, bf16[384,3456]{1,0:T(8,128)(2,1)}, f32[64,128]{1,0:T(8,128)S(1)}) custom-call(s32[1]{0:T(128)} %bitcast.core_ref, bf16[32,56,256]{2,1,0:T(8,128)(2,1)S(1)} %all-to-all-done.mine_ref, bf16[32,56,256]{2,1,0:T(8,128)(2,1)S(1)} %collective-permute-done.other_ref, bf16[1,384,256]{2,1,0:T(8,128)(2,1)S(1)} %copy-done.7), custom_call_target="tpu_custom_call" | custom-call | flops 3000000000 | bytes 9000000 | tf_op jit(solution)/shard_map/row_grad_part/pallas_call | solution.py:193
  56.7 1.2 copy-done.2
  58.0 5.8 %all-to-all-start.1 = ((bf16[64,4,3456]{2,1,0:T(4,128)(2,1)}), bf16[64,4,3456]{2,1,0:T(4,128)(2,1)S(1)}, u32[]{:S(2)}, u32[]{:S(2)}) async-start(bf16[64,4,3456]{2,1,0:T(4,128)(2,1)} %get-tuple-element.26), calls=%async_computation.1 | async-start | bytes 3538944 | tf_op jit(solution)/shard_map/all_to_all | solution.py:441
  64.6 0.2 select_reduce_fusion
  64.9 0.2 multiply_reduce_fusion
  65.4 41.4 %all-to-all-done.1.arrived_ref = bf16[64,4,3456]{2,1,0:T(4,128)(2,1)S(1)} async-done(((bf16[64,4,3456]{2,1,0:T(4,128)(2,1)}), bf16[64,4,3456]{2,1,0:T(4,128)(2,1)S(1)}, u32[]{:S(2)}, u32[]{:S(2)}) %all-to-all-start.1) | async-done | bytes 1769504 | tf_op jit(solution)/shard_map/all_to_all | solution.py:441
  106.8 1.2 owned_features.1
  108.0 1.0 copy-done.6
  109.0 2.3 %returning_blocks.1 = (bf16[64,4,3456]{2,1,0:T(4,128)(2,1)}, f32[2,1152]{1,0:T(2,128)S(1)}) custom-call(s32[1,256]{1,0:T(1,128)S(1)} %select_n.61.code_ref, f32[48,1]{1,0:T(8,128)S(1)} %reshape_reshape.4.named_ref, f32[144,1152]{1,0:T(8,128)S(1)} %get-tuple-element.29.unit_ref, bf16[48,3456]{1,0:T(8,128)(2,1)S(1)} %copy-done.6), custom_call_target="tpu_custom_call" | custom-call | tf_op jit(solution)/shard_map/returning_blocks/pallas_call | solution.py:268
  111.3 6.9 %all-to-all-start.2 = ((bf16[64,4,3456]{2,1,0:T(4,128)(2,1)}), bf16[64,4,3456]{2,1,0:T(4,128)(2,1)}, u32[]{:S(2)}, u32[]{:S(2)}) async-start(bf16[64,4,3456]{2,1,0:T(4,128)(2,1)} %get-tuple-element.35), calls=%async_computation.3 | async-start | bytes 3538944 | tf_op jit(solution)/shard_map/all_to_all | solution.py:474
  118.2 26.4 %psum.7.totals_ref = f32[9,256]{1,0:T(8,128)S(1)} all-reduce(f32[9,256]{1,0:T(8,128)S(1)} %reshape.139), channel_id=1, replica_groups=mesh['dp'=8,'z'=8,'x'=4,'c'=2] {'dp'}, use_global_device_ids=true, to_apply=%region_4.5 | all-reduce | flops 2304 | bytes 18432 | tf_op jit(solution)/shard_map/psum | solution.py:476
  144.6 3.5 %all-gather.2.cloned.1.call-done.gathered_ref = bf16[384,3456]{1,0:T(8,128)(2,1)} async-done(((bf16[48,3456]{1,0:T(8,128)(2,1)}), bf16[384,3456]{1,0:T(8,128)(2,1)}) %all-gather.2.cloned.1.call-update) | async-done | bytes 2654224 | tf_op jit(solution)/shard_map/all_gather | solution.py:473
  148.1 1.7 copy-done
  149.8 1.2 weight_terms.1
  151.0 5.6 %collective-permute-start.1 = (bf16[32,64,256]{2,1,0:T(8,128)(2,1)S(1)}, bf16[32,64,256]{2,1,0:T(8,128)(2,1)S(1)}, u32[]{:S(2)}, u32[]{:S(2)}) collective-permute-start(bf16[32,64,256]{2,1,0:T(8,128)(2,1)S(1)} %get-tuple-element.34), channel_id=1, source_target_pairs={{0,1},{1,0},{2,3},{3,2},{4,5},{5,4},{6,7},{7,6},{8,9},{9,8},{10,11... | collective-permute-start | bytes 3145736 | tf_op jit(solution)/shard_map/ppermute | solution.py:480
  156.7 2.3 %collective-permute-done.1 = bf16[32,64,256]{2,1,0:T(8,128)(2,1)S(1)} collective-permute-done((bf16[32,64,256]{2,1,0:T(8,128)(2,1)S(1)}, bf16[32,64,256]{2,1,0:T(8,128)(2,1)S(1)}, u32[]{:S(2)}, u32[]{:S(2)}) %collective-permute-start.1) | collective-permute-done | bytes 1048608 | tf_op jit(solution)/shard_map/ppermute | solution.py:480
  158.9 1.4 add_convert_fusion
  160.3 0.8 all-to-all-done.2.returned_ref
  161.1 9.2 %all-to-all-start.3 = ((bf16[32,64,256]{2,1,0:T(8,128)(2,1)}), bf16[32,64,256]{2,1,0:T(8,128)(2,1)}, u32[]{:S(2)}, u32[]{:S(2)}) async-start(bf16[32,64,256]{2,1,0:T(8,128)(2,1)} %add_convert_fusion), calls=%async_computation.4 | async-start | bytes 2097152 | tf_op jit(solution)/shard_map/all_to_all | solution.py:484
  170.3 1.5 copy-done.3
  171.8 1.6 project.1
  173.4 7.1 %hidden_gradient.1 = bf16[1,729,1152]{2,1,0:T(8,128)(2,1)} custom-call(s32[1]{0:T(128)S(6)} %copy.35.tile_ref, s32[4,256]{1,0:T(4,128)S(1)} %pad.4.clone.peer_row_ref, s32[256,4]{1,0:T(8,128)S(1)} %pad_bitcast_fusion.peer_col_ref, f32[1,1152]{1,0:T(1,128)S(1)} %reshape.137.gain_ref, bf16[1,729,1152]{2,1,0:T(8,128)(2,1)S(1)} %copy-done.5, ...), custom_call_target="tpu_custom_call" | custom-call | tf_op jit(solution)/shard_map/hidden_gradient/pallas_call | solution.py:329
  180.5 16.1 %all-to-all-done.3.parts_ref = bf16[32,64,256]{2,1,0:T(8,128)(2,1)} async-done(((bf16[32,64,256]{2,1,0:T(8,128)(2,1)}), bf16[32,64,256]{2,1,0:T(8,128)(2,1)}, u32[]{:S(2)}, u32[]{:S(2)}) %all-to-all-start.3) | async-done | bytes 1048608 | tf_op jit(solution)/shard_map/all_to_all | solution.py:484
  196.6 2.0 weight_sum.1
  198.6 0.6 slice_reduce_fusion
  (50 shorter events, 1.9 us)
Async XLA Ops:
  7.2 16.4 %copy-start.8 = (s32[1,4,27,9]{2,1,3,0:T(4,128)S(1)}, s32[1,4,27,9]{2,1,3,0:T(4,128)}, u32[]{:S(2)}) copy-start(s32[1,4,27,9]{2,1,3,0:T(4,128)} %param.11) | copy-start | bytes 11668
  8.8 15.3 %copy-start.4 = (bf16[1,729,1152]{2,1,0:T(8,128)(2,1)S(1)}, bf16[1,729,1152]{2,1,0:T(8,128)(2,1)}, u32[]{:S(2)}) copy-start(bf16[1,729,1152]{2,1,0:T(8,128)(2,1)} %hidden_ref.3) | copy-start | bytes 5038852
  9.8 37.2 %all-to-all-start = ((bf16[32,56,256]{2,1,0:T(8,128)(2,1)}), bf16[32,56,256]{2,1,0:T(8,128)(2,1)S(1)}, u32[]{:S(2)}, u32[]{:S(2)}) async-start(bf16[32,56,256]{2,1,0:T(8,128)(2,1)} %broadcast_in_dim.87), calls=%async_computation | async-start | bytes 1835008 | tf_op jit(solution)/shard_map/all_to_all | solution.py:423
  23.5 84.5 %reduce-scatter.2.cloned.1.call-start = ((), (), s32[]{:S(2)}) async-start(), calls=%async_computation.6 | async-start | bytes 2985984 | tf_op jit(solution)/shard_map/reduce_scatter | solution.py:445
  24.1 30.0 %copy-start.7 = (bf16[1,384,256]{2,1,0:T(8,128)(2,1)S(1)}, bf16[1,384,256]{2,1,0:T(8,128)(2,1)}, u32[]{:S(2)}) copy-start(bf16[1,384,256]{2,1,0:T(8,128)(2,1)} %grad_ref.3) | copy-start | bytes 589828
  47.0 7.1 %collective-permute-start = (bf16[32,56,256]{2,1,0:T(8,128)(2,1)S(1)}, bf16[32,56,256]{2,1,0:T(8,128)(2,1)S(1)}, u32[]{:S(2)}, u32[]{:S(2)}) collective-permute-start(bf16[32,56,256]{2,1,0:T(8,128)(2,1)S(1)} %all-to-all-done.mine_ref), channel_id=1, source_target_pairs={{0,1},{1,0},{2,3},{3,2},{4,5},{5,4},{6,7},{7,6},{8,9},{9,8},{10,11... | collective-permute-start | bytes 2752520 | tf_op jit(solution)/shard_map/ppermute | solution.py:442
  56.7 1.2 copy-start.2
  58.0 5.9 %copy-start.9 = (f32[1152]{0:T(1024)S(1)}, f32[1152]{0:T(1024)}, u32[]{:S(2)}) copy-start(f32[1152]{0:T(1024)} %param.8) | copy-start | bytes 13828
  58.0 5.9 %copy-start.10 = (f32[1152]{0:T(1024)S(1)}, f32[1152]{0:T(1024)}, u32[]{:S(2)}) copy-start(f32[1152]{0:T(1024)} %param.9) | copy-start | bytes 13828
  58.0 48.7 %all-to-all-start.1 = ((bf16[64,4,3456]{2,1,0:T(4,128)(2,1)}), bf16[64,4,3456]{2,1,0:T(4,128)(2,1)S(1)}, u32[]{:S(2)}, u32[]{:S(2)}) async-start(bf16[64,4,3456]{2,1,0:T(4,128)(2,1)} %get-tuple-element.26), calls=%async_computation.1 | async-start | bytes 3538944 | tf_op jit(solution)/shard_map/all_to_all | solution.py:441
  63.8 84.2 %all-gather.2.cloned.1.call-start = ((), (), s32[]{:S(2)}) async-start(), calls=%async_computation.5 | async-start | bytes 2985984 | tf_op jit(solution)/shard_map/all_gather | solution.py:473
  108.0 1.0 copy-start.6
  111.3 49.8 %all-to-all-start.2 = ((bf16[64,4,3456]{2,1,0:T(4,128)(2,1)}), bf16[64,4,3456]{2,1,0:T(4,128)(2,1)}, u32[]{:S(2)}, u32[]{:S(2)}) async-start(bf16[64,4,3456]{2,1,0:T(4,128)(2,1)} %get-tuple-element.35), calls=%async_computation.3 | async-start | bytes 3538944 | tf_op jit(solution)/shard_map/all_to_all | solution.py:474
  148.1 1.7 copy-start
  151.0 7.9 %collective-permute-start.1 = (bf16[32,64,256]{2,1,0:T(8,128)(2,1)S(1)}, bf16[32,64,256]{2,1,0:T(8,128)(2,1)S(1)}, u32[]{:S(2)}, u32[]{:S(2)}) collective-permute-start(bf16[32,64,256]{2,1,0:T(8,128)(2,1)S(1)} %get-tuple-element.34), channel_id=1, source_target_pairs={{0,1},{1,0},{2,3},{3,2},{4,5},{5,4},{6,7},{7,6},{8,9},{9,8},{10,11... | collective-permute-start | bytes 3145736 | tf_op jit(solution)/shard_map/ppermute | solution.py:480
  158.9 11.4 %copy-start.1 = (bf16[384,3456]{1,0:T(8,128)(2,1)S(1)}, bf16[384,3456]{1,0:T(8,128)(2,1)}, u32[]{:S(2)}) copy-start(bf16[384,3456]{1,0:T(8,128)(2,1)} %all-gather.2.cloned.1.call-done.gathered_ref) | copy-start | bytes 7962628
  161.1 35.5 %all-to-all-start.3 = ((bf16[32,64,256]{2,1,0:T(8,128)(2,1)}), bf16[32,64,256]{2,1,0:T(8,128)(2,1)}, u32[]{:S(2)}, u32[]{:S(2)}) async-start(bf16[32,64,256]{2,1,0:T(8,128)(2,1)} %add_convert_fusion), calls=%async_computation.4 | async-start | bytes 2097152 | tf_op jit(solution)/shard_map/all_to_all | solution.py:484
  170.3 1.5 copy-start.3
  171.8 1.6 copy-start.5
Sparse Core Ops, SparseCore 0:
  58.1 39.3 reduce-scatter.1
  108.1 39.8 all-gather.1

commit v4 on v3

--- a/solution.py
+++ b/solution.py
@@ -26,7 +26,7 @@
 STEPS = 4
 ROWS = 32
 EPS = 1e-6
-VMEM = 32 * 1024 * 1024
+MIB = 1024 * 1024
 
 FEATURES_COST = 2
 ROW_GRAD_COST = 3
@@ -162,27 +162,27 @@
             jax.ShapeDtypeStruct((STEPS * CHUNK, 128), f32),
         ),
         scratch_shapes=[pltpu.VMEM((STEPS * CHUNK, WIDTH), bf16)],
-        compiler_params=pltpu.CompilerParams(vmem_limit_bytes=VMEM),
+        compiler_params=pltpu.CompilerParams(vmem_limit_bytes=24 * MIB),
         cost_estimate=cost(POOL_COST),
         name="pool_tokens",
     )(tile, peer_row, peer_col, hidden)
 
 
-def row_grad_kernel(
-    core_ref, mine_ref, other_ref, grad_ref, weight_ref, part_ref, tiles_ref, wide_ref
-):
+def join_weight(core_ref, mine_ref, other_ref, wide_ref, tiles_ref=None):
     first = core_ref[0] == 0
-    for x in range(NX):
-        for z in range(NZ):
-            mine = mine_ref[z * NX + x].astype(f32)
-            other = other_ref[z * NX + x].astype(f32)
-            low, high = jnp.where(first, mine, other), jnp.where(first, other, mine)
-            for c, block in enumerate((low, high)):
-                peer = (z * NX + x) * NC + c
-                wide_ref[peer * SHARD : (peer + 1) * SHARD, :] = block[:SHARD]
+    for n in range(NZ * NX):
+        mine, other = mine_ref[n].astype(f32), other_ref[n].astype(f32)
+        low, high = jnp.where(first, mine, other), jnp.where(first, other, mine)
+        for c, block in enumerate((low, high)):
+            peer = n * NC + c
+            wide_ref[peer * SHARD : (peer + 1) * SHARD, :] = block[:SHARD]
+            if tiles_ref is not None:
                 tiles_ref[peer : peer + 1, :] = block[SHARD : SHARD + 1, : tiles_ref.shape[1]]
-    full = wide_ref[...].astype(bf16)
-    weight_ref[...] = full
+    return wide_ref[...].astype(bf16)
+
+
+def row_grad_kernel(core_ref, mine_ref, other_ref, grad_ref, part_ref, tiles_ref, wide_ref):
+    full = join_weight(core_ref, mine_ref, other_ref, wide_ref, tiles_ref)
     part_ref[...] = lax.dot_general(
         grad_ref[0], full, (((1,), (1,)), ((), ())), preferred_element_type=f32
     ).astype(bf16)
@@ -194,12 +194,11 @@
         row_grad_kernel,
         in_specs=[pl.BlockSpec(memory_space=pltpu.SMEM)] + [pl.BlockSpec()] * 3,
         out_shape=(
-            jax.ShapeDtypeStruct((PEERS * SHARD, cols), bf16),
             jax.ShapeDtypeStruct((rows, PEERS * SHARD), bf16),
             jax.ShapeDtypeStruct((PEERS, 128), f32),
         ),
         scratch_shapes=[pltpu.VMEM((PEERS * SHARD, cols), f32)],
-        compiler_params=pltpu.CompilerParams(vmem_limit_bytes=VMEM),
+        compiler_params=pltpu.CompilerParams(vmem_limit_bytes=24 * MIB),
         cost_estimate=cost(ROW_GRAD_COST),
         name="row_grad_part",
     )(core, mine, other, grad)
@@ -212,7 +211,7 @@
 
 
 def features_kernel(
-    code_ref, named_ref, gain_ref, bias_ref, arrived_ref, out_ref, unit_ref
+    code_ref, named_ref, gain_ref, bias_ref, arrived_ref, after_ref, out_ref, unit_ref
 ):
     code = code_ref[...]
     total = jnp.zeros((3 * OWN_ROWS, WIDTH), f32)
@@ -229,20 +228,21 @@
         out_ref[:, s * WIDTH : (s + 1) * WIDTH] = jnp.where(named, affine, 0.0).astype(bf16)
 
 
-def owned_features(code, named, gain, bias, arrived):
+def owned_features(code, named, gain, bias, arrived, after):
     return pl.pallas_call(
         features_kernel,
         out_shape=(
             jax.ShapeDtypeStruct((OWN_ROWS, 3 * WIDTH), bf16),
             jax.ShapeDtypeStruct((3 * OWN_ROWS, WIDTH), f32),
         ),
-        compiler_params=pltpu.CompilerParams(vmem_limit_bytes=VMEM),
+        compiler_params=pltpu.CompilerParams(vmem_limit_bytes=16 * MIB),
         cost_estimate=cost(FEATURES_COST),
         name="owned_features",
-    )(code, named, gain, bias, arrived)
-
-
-def returning_kernel(code_ref, named_ref, unit_ref, grad_ref, out_ref, totals_ref):
+    )(code, named, gain, bias, arrived, after)
+
+
+def returning_kernel(code_ref, grad_ref, out_ref, done_ref):
+    done_ref[...] = jnp.zeros(done_ref.shape, f32)
     code = code_ref[...]
     stacked = jnp.concatenate(
         [grad_ref[:, s * WIDTH : (s + 1) * WIDTH] for s in range(3)], axis=0
@@ -252,6 +252,21 @@
             owner_select(code, e), stacked, (((0,), (0,)), ((), ())), preferred_element_type=f32
         )
         put_blocks(out_ref, e, returned)
+
+
+def returning_blocks(code, grad):
+    return pl.pallas_call(
+        returning_kernel,
+        out_shape=(
+            jax.ShapeDtypeStruct((PEERS, CAP, BLOCK * WIDTH), bf16),
+            jax.ShapeDtypeStruct((8, 128), f32),
+        ),
+        compiler_params=pltpu.CompilerParams(vmem_limit_bytes=16 * MIB),
+        name="returning_blocks",
+    )(code, grad)
+
+
+def gain_and_bias_kernel(named_ref, unit_ref, grad_ref, totals_ref):
     named = named_ref[...] > 0.0
     gain_sum = jnp.zeros((1, WIDTH), f32)
     bias_sum = jnp.zeros((1, WIDTH), f32)
@@ -264,16 +279,13 @@
     totals_ref[...] = jnp.concatenate([gain_sum, bias_sum], axis=0)
 
 
-def returning_blocks(code, named, unit_sums, grad):
-    return pl.pallas_call(
-        returning_kernel,
-        out_shape=(
-            jax.ShapeDtypeStruct((PEERS, CAP, BLOCK * WIDTH), bf16),
-            jax.ShapeDtypeStruct((2, WIDTH), f32),
-        ),
-        compiler_params=pltpu.CompilerParams(vmem_limit_bytes=VMEM),
-        name="returning_blocks",
-    )(code, named, unit_sums, grad)
+def gain_and_bias(named, unit_sums, grad):
+    return pl.pallas_call(
+        gain_and_bias_kernel,
+        out_shape=jax.ShapeDtypeStruct((2, WIDTH), f32),
+        compiler_params=pltpu.CompilerParams(vmem_limit_bytes=8 * MIB),
+        name="gain_and_bias",
+    )(named, unit_sums, grad)
 
 
 def hidden_grad_kernel(
@@ -344,7 +356,7 @@
             pltpu.VMEM((CHUNK, WIDTH), f32),
             pltpu.VMEM((BLOCK, SEND, WIDTH), bf16),
         ],
-        compiler_params=pltpu.CompilerParams(vmem_limit_bytes=VMEM),
+        compiler_params=pltpu.CompilerParams(vmem_limit_bytes=24 * MIB),
         name="hidden_gradient",
     )(tile, peer_row, peer_col, gain, hidden, stats, returned)
 
@@ -376,25 +388,28 @@
         out_shape=(jax.ShapeDtypeStruct((NZ * NX, TERM_PAD, cols), bf16),) * 2
         + (jax.ShapeDtypeStruct((8, 128), f32),),
         scratch_shapes=[pltpu.VMEM((PEERS * SHARD, cols), f32)],
-        compiler_params=pltpu.CompilerParams(vmem_limit_bytes=VMEM),
+        compiler_params=pltpu.CompilerParams(vmem_limit_bytes=24 * MIB),
         name="weight_terms",
     )(core, gathered, grad, totals)
 
 
-def project_kernel(gathered_ref, weight_ref, after_ref, projected_ref):
-    projected_ref[0] = jnp.dot(
-        gathered_ref[...], weight_ref[...], preferred_element_type=f32
-    ).astype(bf16)
-
-
-def project(gathered, weight, after):
+def project_kernel(core_ref, gathered_ref, mine_ref, other_ref, after_ref, projected_ref, wide_ref):
+    full = join_weight(core_ref, mine_ref, other_ref, wide_ref)
+    projected_ref[0] = jnp.dot(gathered_ref[...], full, preferred_element_type=f32).astype(bf16)
+
+
+def project(core, gathered, mine, other, after):
+    rows, cols = gathered.shape[0], mine.shape[2]
     return pl.pallas_call(
         project_kernel,
-        in_specs=[pl.BlockSpec()] * 2 + [pl.BlockSpec(memory_space=pl.ANY)],
-        out_shape=jax.ShapeDtypeStruct((1, gathered.shape[0], weight.shape[1]), bf16),
-        compiler_params=pltpu.CompilerParams(vmem_limit_bytes=VMEM),
+        in_specs=[pl.BlockSpec(memory_space=pltpu.SMEM)]
+        + [pl.BlockSpec()] * 3
+        + [pl.BlockSpec(memory_space=pl.ANY)],
+        out_shape=jax.ShapeDtypeStruct((1, rows, cols), bf16),
+        scratch_shapes=[pltpu.VMEM((PEERS * SHARD, cols), f32)],
+        compiler_params=pltpu.CompilerParams(vmem_limit_bytes=24 * MIB),
         name="project",
-    )(gathered, weight, after)
+    )(core, gathered, mine, other, after)
 
 
 def weight_sum_kernel(parts_ref, weight_ref, totals_ref):
@@ -413,14 +428,28 @@
             jax.ShapeDtypeStruct((SHARD, cols), f32),
             jax.ShapeDtypeStruct((extra, cols), f32),
         ),
-        compiler_params=pltpu.CompilerParams(vmem_limit_bytes=VMEM),
+        compiler_params=pltpu.CompilerParams(vmem_limit_bytes=8 * MIB),
         name="weight_sum",
     )(parts)
 
 
-def spread(shard, axis, count):
-    copies = jnp.broadcast_to(shard[None], (count,) + shard.shape)
-    return lax.all_to_all(copies, axis, split_axis=0, concat_axis=0, tiled=True)
+def shard_copies_kernel(tile_ref, weight_ref, out_ref):
+    cols = weight_ref.shape[1]
+    tile = jnp.full((SHARD_PAD - SHARD, cols), tile_ref[0], i32).astype(f32)
+    block = jnp.concatenate([weight_ref[...].astype(f32), tile], axis=0).astype(bf16)
+    for n in range(NZ * NX):
+        out_ref[n] = block
+
+
+def shard_copies(tile, weight):
+    cols = weight.shape[1]
+    return pl.pallas_call(
+        shard_copies_kernel,
+        in_specs=[pl.BlockSpec(memory_space=pltpu.SMEM), pl.BlockSpec()],
+        out_shape=jax.ShapeDtypeStruct((NZ * NX, SHARD_PAD, cols), bf16),
+        compiler_params=pltpu.CompilerParams(vmem_limit_bytes=8 * MIB),
+        name="shard_copies",
+    )(tile, weight)
 
 
 def shards(hidden, norm_gain, norm_bias, slot_tile, block_owner, proj_weight, proj_grad):
@@ -432,16 +461,13 @@
     peers = jnp.pad(table >> 4, ((0, 0), (0, BLOCKS_PAD - BLOCKS)), constant_values=-1)
     outgoing, stats = pool_tokens(slot_tile, peers, peers.T, hidden)
 
-    tile_row = jnp.broadcast_to(slot_tile.astype(bf16)[:, None], (1, cols))
-    shard = jnp.concatenate(
-        [proj_weight, tile_row, jnp.zeros((SHARD_PAD - SHARD - 1, cols), bf16)], axis=0
-    )
-    mine = spread(shard, ("z", "x"), NZ * NX)
+    copies = shard_copies(slot_tile, proj_weight)
+    mine = lax.all_to_all(copies, ("z", "x"), split_axis=0, concat_axis=0, tiled=True)
     mine, outgoing = lax.optimization_barrier((mine, outgoing))
     arrived = lax.all_to_all(outgoing, ("z", "x", "c"), 0, 0, tiled=True)
     other = lax.ppermute(mine, "c", [(0, 1), (1, 0)])
 
-    weight, row_part, tiles = row_grad_part(core.reshape(1), mine, other, proj_grad)
+    row_part, tiles = row_grad_part(core.reshape(1), mine, other, proj_grad)
     own_grad = lax.psum_scatter(row_part, "dp", scatter_dimension=0, tiled=True)
 
     held = (table >> 4) == me
@@ -465,18 +491,18 @@
     code = jnp.where(found >= 0, scale[:, None] * OWN + found, -1).reshape(1, SEND)
 
     gain = norm_gain.reshape(1, WIDTH)
+    returning, done = returning_blocks(code, own_grad)
     features, unit_sums = owned_features(
-        code, named, gain, norm_bias.reshape(1, WIDTH), arrived
+        code, named, gain, norm_bias.reshape(1, WIDTH), arrived, done
     )
-
-    returning, totals = returning_blocks(code, named, unit_sums, own_grad)
     gathered = lax.all_gather(features, "dp", axis=0, tiled=True)
+    totals = gain_and_bias(named, unit_sums, own_grad)
     returned = lax.all_to_all(returning, ("z", "x", "c"), 0, 0, tiled=True)
 
     totals = lax.psum(totals, "dp").reshape(-1, cols)
     extra = totals.shape[0]
     kept, sent, done = weight_terms(core.reshape(1), gathered, proj_grad, totals)
-    projected = project(gathered, weight, done)
+    projected = project(core.reshape(1), gathered, mine, other, done)
     got = lax.ppermute(sent, "c", [(0, 1), (1, 0)])
     terms = (kept.astype(f32) + got.astype(f32)).astype(bf16)
     terms, returned = lax.optimization_barrier((terms, returned))

time: 208 us -> 207 us (level)
  starting transfers between devices: 46.3 us -> 48.5 us
    all_to_all x1, waiting for transfers between devices: 41.4 us -> 6.52 us  [shards(): arrived = lax.all_to_all(outgoing, ('z', 'x', 'c'), 0, 0, tiled=True)]
    reduce_scatter x1, waiting for transfers between devices: 0.02 us -> 31.9 us  [shards(): own_grad = lax.psum_scatter(row_part, 'dp', scatter_dimension=0, tiled=True)]
    all_gather x1, waiting for transfers between devices: 3.48 us -> 6.75 us  [shards(): gathered = lax.all_gather(features, 'dp', axis=0, tiled=True)]
    unnamed x23 -> x33, local copies, waits for them, and re-layouts: 5.54 us -> 7.45 us
  transfers between devices with their start and end apart: 8 -> 8, of which waited for: 7 -> 7; matrix products, arithmetic and copies ran while one was open for 2% -> 2% of each run, Pallas kernels for 11% -> 10%
where the time goes in v4:
time: 207 us; the launch traced here: 205 us
  waiting for transfers between devices  79.1 us (38%)
  starting transfers between devices  48.5 us (23%)
  Pallas kernels  25.9 us (13%)
  blocking collectives  24.7 us (12%)
  between operations  15.1 us (7%)
  local copies, waits for them, and re-layouts  9.07 us (4%)
    reduce_scatter x1, waiting for transfers between devices, shards(): own_grad = lax.psum_scatter(row_part, 'dp', scatter_dimension=0, tiled=True)  31.9 us
    psum x1, blocking collectives, shards(): totals = lax.psum(totals, 'dp').reshape(-1, cols)  24.7 us
    all_to_all x1, waiting for transfers between devices, shards(): lax.all_to_all(terms, ('z', 'x'), split_axis=0, concat_axis=0, tiled=True)  15 us
    all_to_all x1, waiting for transfers between devices, shards(): lax.all_to_all(copies, ('z', 'x'), split_axis=0, concat_axis=0, tiled=True)  14.6 us
    all_to_all x1, starting transfers between devices, shards(): lax.all_to_all(copies, ('z', 'x'), split_axis=0, concat_axis=0, tiled=True)  13.7 us
    all_to_all x1, starting transfers between devices, shards(): lax.all_to_all(terms, ('z', 'x'), split_axis=0, concat_axis=0, tiled=True)  10.2 us
    all_to_all x1, starting transfers between devices, shards(): returned = lax.all_to_all(returning, ('z', 'x', 'c'), 0, 0, tiled=True)  8.75 us
    pallas_call x1, Pallas kernels, pool_tokens(): pl.pallas_call(pool_kernel, grid=(STEPS,), in_specs=[pl.BlockSpec(memory_...  8.31 us
  transfers between devices with their start and end apart: 8, of which 7 were waited for; matrix products, arithmetic and copies ran while one was open for 2% of the time, Pallas kernels for 10%

profile of v4, /device:TPU:1, one launch (start us, length us, event | category | flops | bytes accessed | tf_op | source)
XLA Modules:
  0.0 204.5 jit_solution(14667678717995621781)
XLA Ops:
  8.0 0.7 copy-done.12
  8.7 1.0 shard_copies.1
  9.7 13.7 %all-to-all-start = ((bf16[32,56,256]{2,1,0:T(8,128)(2,1)}), bf16[32,56,256]{2,1,0:T(8,128)(2,1)S(1)}, u32[]{:S(2)}, u32[]{:S(2)}) async-start(bf16[32,56,256]{2,1,0:T(8,128)(2,1)} %shard_copies.1), calls=%async_computation | async-start | bytes 1835008 | tf_op jit(solution)/shard_map/all_to_all | solution.py:465
  24.0 8.3 %pool_tokens.1 = (bf16[64,4,3456]{2,1,0:T(4,128)(2,1)}, f32[768,128]{1,0:T(8,128)S(1)}) custom-call(s32[1]{0:T(128)S(6)} %copy.35.tile_ref, s32[4,256]{1,0:T(4,128)S(1)} %pad.4.clone.peer_row_ref, s32[256,4]{1,0:T(8,128)S(1)} %pad_bitcast_fusion.peer_col_ref, bf16[1,729,1152]{2,1,0:T(8,128)(2,1)S(1)} %copy-done.5), custom_call_target="tpu_custom_call" | custom-call | flops 8000000000 | bytes 24000000 | tf_op jit(solution)/shard_map/pool_tokens/pallas_call | solution.py:147
  32.3 14.6 %all-to-all-done.mine_ref = bf16[32,56,256]{2,1,0:T(8,128)(2,1)S(1)} async-done(((bf16[32,56,256]{2,1,0:T(8,128)(2,1)}), bf16[32,56,256]{2,1,0:T(8,128)(2,1)S(1)}, u32[]{:S(2)}, u32[]{:S(2)}) %all-to-all-start) | async-done | bytes 917536 | tf_op jit(solution)/shard_map/all_to_all | solution.py:465
  46.9 5.0 %collective-permute-start = (bf16[32,56,256]{2,1,0:T(8,128)(2,1)S(1)}, bf16[32,56,256]{2,1,0:T(8,128)(2,1)S(1)}, u32[]{:S(2)}, u32[]{:S(2)}) collective-permute-start(bf16[32,56,256]{2,1,0:T(8,128)(2,1)S(1)} %all-to-all-done.mine_ref), channel_id=1, source_target_pairs={{0,1},{1,0},{2,3},{3,2},{4,5},{5,4},{6,7},{7,6},{8,9},{9,8},{10,11... | collective-permute-start | bytes 2752520 | tf_op jit(solution)/shard_map/ppermute | solution.py:468
  51.9 2.1 %collective-permute-done.other_ref = bf16[32,56,256]{2,1,0:T(8,128)(2,1)S(1)} collective-permute-done((bf16[32,56,256]{2,1,0:T(8,128)(2,1)S(1)}, bf16[32,56,256]{2,1,0:T(8,128)(2,1)S(1)}, u32[]{:S(2)}, u32[]{:S(2)}) %collective-permute-start) | collective-permute-done | bytes 917536 | tf_op jit(solution)/shard_map/ppermute | solution.py:468
  53.9 1.1 row_grad_part.1
  55.1 1.5 copy-done.4
  56.6 5.8 %all-to-all-start.1 = ((bf16[64,4,3456]{2,1,0:T(4,128)(2,1)}), bf16[64,4,3456]{2,1,0:T(4,128)(2,1)S(1)}, u32[]{:S(2)}, u32[]{:S(2)}) async-start(bf16[64,4,3456]{2,1,0:T(4,128)(2,1)} %get-tuple-element.25), calls=%async_computation.1 | async-start | bytes 3538944 | tf_op jit(solution)/shard_map/all_to_all | solution.py:467
  63.9 31.9 %reduce-scatter.2.cloned.1.call-done.grad_ref = bf16[48,3456]{1,0:T(8,128)(2,1)} async-done(((bf16[384,3456]{1,0:T(8,128)(2,1)}), bf16[48,3456]{1,0:T(8,128)(2,1)}) %reduce-scatter.2.cloned.1.call-update) | async-done | bytes 331792 | tf_op jit(solution)/shard_map/reduce_scatter | solution.py:471
  95.9 1.0 copy-done.7
  96.8 2.0 returning_blocks.1
  98.8 6.5 %all-to-all-done.1.arrived_ref = bf16[64,4,3456]{2,1,0:T(4,128)(2,1)S(1)} async-done(((bf16[64,4,3456]{2,1,0:T(4,128)(2,1)}), bf16[64,4,3456]{2,1,0:T(4,128)(2,1)S(1)}, u32[]{:S(2)}, u32[]{:S(2)}) %all-to-all-start.1) | async-done | bytes 1769504 | tf_op jit(solution)/shard_map/all_to_all | solution.py:467
  105.4 1.2 owned_features.1
  106.6 8.8 %all-to-all-start.2 = ((bf16[64,4,3456]{2,1,0:T(4,128)(2,1)}), bf16[64,4,3456]{2,1,0:T(4,128)(2,1)}, u32[]{:S(2)}, u32[]{:S(2)}) async-start(bf16[64,4,3456]{2,1,0:T(4,128)(2,1)} %get-tuple-element.33), calls=%async_computation.3 | async-start | bytes 3538944 | tf_op jit(solution)/shard_map/all_to_all | solution.py:500
  115.4 0.2 gain_and_bias.1
  115.6 24.7 %psum.7.totals_ref = f32[9,256]{1,0:T(8,128)S(1)} all-reduce(f32[9,256]{1,0:T(8,128)S(1)} %reshape.136), channel_id=1, replica_groups=mesh['dp'=8,'z'=8,'x'=4,'c'=2] {'dp'}, use_global_device_ids=true, to_apply=%region_4.5 | all-reduce | flops 2304 | bytes 18432 | tf_op jit(solution)/shard_map/psum | solution.py:502
  140.3 6.7 %all-gather.2.cloned.1.call-done.gathered_ref = bf16[384,3456]{1,0:T(8,128)(2,1)} async-done(((bf16[48,3456]{1,0:T(8,128)(2,1)}), bf16[384,3456]{1,0:T(8,128)(2,1)}) %all-gather.2.cloned.1.call-update) | async-done | bytes 2654224 | tf_op jit(solution)/shard_map/all_gather | solution.py:498
  147.1 1.7 copy-done
  148.8 1.2 weight_terms.1
  150.1 5.0 %collective-permute-start.1 = (bf16[32,64,256]{2,1,0:T(8,128)(2,1)S(1)}, bf16[32,64,256]{2,1,0:T(8,128)(2,1)S(1)}, u32[]{:S(2)}, u32[]{:S(2)}) collective-permute-start(bf16[32,64,256]{2,1,0:T(8,128)(2,1)S(1)} %get-tuple-element.32), channel_id=1, source_target_pairs={{0,1},{1,0},{2,3},{3,2},{4,5},{5,4},{6,7},{7,6},{8,9},{9,8},{10,11... | collective-permute-start | bytes 3145736 | tf_op jit(solution)/shard_map/ppermute | solution.py:506
  155.1 2.3 %collective-permute-done.1 = bf16[32,64,256]{2,1,0:T(8,128)(2,1)S(1)} collective-permute-done((bf16[32,64,256]{2,1,0:T(8,128)(2,1)S(1)}, bf16[32,64,256]{2,1,0:T(8,128)(2,1)S(1)}, u32[]{:S(2)}, u32[]{:S(2)}) %collective-permute-start.1) | collective-permute-done | bytes 1048608 | tf_op jit(solution)/shard_map/ppermute | solution.py:506
  157.4 1.4 add_convert_fusion
  158.7 10.2 %all-to-all-start.3 = ((bf16[32,64,256]{2,1,0:T(8,128)(2,1)}), bf16[32,64,256]{2,1,0:T(8,128)(2,1)}, u32[]{:S(2)}, u32[]{:S(2)}) async-start(bf16[32,64,256]{2,1,0:T(8,128)(2,1)} %add_convert_fusion), calls=%async_computation.4 | async-start | bytes 2097152 | tf_op jit(solution)/shard_map/all_to_all | solution.py:510
  168.9 1.2 copy-done.3
  170.1 1.2 copy-done.10
  171.3 1.7 project.1
  173.0 7.1 %hidden_gradient.1 = bf16[1,729,1152]{2,1,0:T(8,128)(2,1)} custom-call(s32[1]{0:T(128)S(6)} %copy.35.tile_ref, s32[4,256]{1,0:T(4,128)S(1)} %pad.4.clone.peer_row_ref, s32[256,4]{1,0:T(8,128)S(1)} %pad_bitcast_fusion.peer_col_ref, f32[1,1152]{1,0:T(1,128)S(1)} %reshape.134.gain_ref, bf16[1,729,1152]{2,1,0:T(8,128)(2,1)S(1)} %copy-done.6, ...), custom_call_target="tpu_custom_call" | custom-call | tf_op jit(solution)/shard_map/hidden_gradient/pallas_call | solution.py:341
  180.1 15.0 %all-to-all-done.3.parts_ref = bf16[32,64,256]{2,1,0:T(8,128)(2,1)} async-done(((bf16[32,64,256]{2,1,0:T(8,128)(2,1)}), bf16[32,64,256]{2,1,0:T(8,128)(2,1)}, u32[]{:S(2)}, u32[]{:S(2)}) %all-to-all-start.3) | async-done | bytes 1048608 | tf_op jit(solution)/shard_map/all_to_all | solution.py:510
  195.1 2.0 weight_sum.1
  197.1 0.6 slice_reduce_fusion
  (58 shorter events, 2.1 us)
Async XLA Ops:
  7.2 16.8 %copy-start.5 = (bf16[1,729,1152]{2,1,0:T(8,128)(2,1)S(1)}, bf16[1,729,1152]{2,1,0:T(8,128)(2,1)}, u32[]{:S(2)}) copy-start(bf16[1,729,1152]{2,1,0:T(8,128)(2,1)} %hidden_ref.3) | copy-start | bytes 5038852
  7.9 0.7 copy-start.12
  8.7 14.8 %copy-start.13 = (s32[1,4,27,9]{2,1,3,0:T(4,128)S(1)}, s32[1,4,27,9]{2,1,3,0:T(4,128)}, u32[]{:S(2)}) copy-start(s32[1,4,27,9]{2,1,3,0:T(4,128)} %param.11) | copy-start | bytes 11668
  9.7 37.2 %all-to-all-start = ((bf16[32,56,256]{2,1,0:T(8,128)(2,1)}), bf16[32,56,256]{2,1,0:T(8,128)(2,1)S(1)}, u32[]{:S(2)}, u32[]{:S(2)}) async-start(bf16[32,56,256]{2,1,0:T(8,128)(2,1)} %shard_copies.1), calls=%async_computation | async-start | bytes 1835008 | tf_op jit(solution)/shard_map/all_to_all | solution.py:465
  23.4 72.4 %reduce-scatter.2.cloned.1.call-start = ((), (), s32[]{:S(2)}) async-start(), calls=%async_computation.5 | async-start | bytes 2985984 | tf_op jit(solution)/shard_map/reduce_scatter | solution.py:471
  24.0 30.0 %copy-start.11 = (bf16[1,384,256]{2,1,0:T(8,128)(2,1)S(1)}, bf16[1,384,256]{2,1,0:T(8,128)(2,1)}, u32[]{:S(2)}) copy-start(bf16[1,384,256]{2,1,0:T(8,128)(2,1)} %grad_ref.3) | copy-start | bytes 589828
  46.9 8.2 %copy-start.2 = (bf16[32,56,256]{2,1,0:T(8,128)(2,1)}, bf16[32,56,256]{2,1,0:T(8,128)(2,1)S(1)}, u32[]{:S(2)}) copy-start(bf16[32,56,256]{2,1,0:T(8,128)(2,1)S(1)} %all-to-all-done.mine_ref) | copy-start | bytes 2752516
  46.9 7.1 %collective-permute-start = (bf16[32,56,256]{2,1,0:T(8,128)(2,1)S(1)}, bf16[32,56,256]{2,1,0:T(8,128)(2,1)S(1)}, u32[]{:S(2)}, u32[]{:S(2)}) collective-permute-start(bf16[32,56,256]{2,1,0:T(8,128)(2,1)S(1)} %all-to-all-done.mine_ref), channel_id=1, source_target_pairs={{0,1},{1,0},{2,3},{3,2},{4,5},{5,4},{6,7},{7,6},{8,9},{9,8},{10,11... | collective-permute-start | bytes 2752520 | tf_op jit(solution)/shard_map/ppermute | solution.py:468
  53.9 1.1 copy-start.9
  55.1 1.5 copy-start.4
  56.6 5.9 %copy-start.14 = (f32[1152]{0:T(1024)S(1)}, f32[1152]{0:T(1024)}, u32[]{:S(2)}) copy-start(f32[1152]{0:T(1024)} %param.8) | copy-start | bytes 13828
  56.6 5.9 %copy-start.15 = (f32[1152]{0:T(1024)S(1)}, f32[1152]{0:T(1024)}, u32[]{:S(2)}) copy-start(f32[1152]{0:T(1024)} %param.9) | copy-start | bytes 13828
  56.6 48.7 %all-to-all-start.1 = ((bf16[64,4,3456]{2,1,0:T(4,128)(2,1)}), bf16[64,4,3456]{2,1,0:T(4,128)(2,1)S(1)}, u32[]{:S(2)}, u32[]{:S(2)}) async-start(bf16[64,4,3456]{2,1,0:T(4,128)(2,1)} %get-tuple-element.25), calls=%async_computation.1 | async-start | bytes 3538944 | tf_op jit(solution)/shard_map/all_to_all | solution.py:467
  62.4 84.7 %all-gather.2.cloned.1.call-start = ((), (), s32[]{:S(2)}) async-start(), calls=%async_computation.6 | async-start | bytes 2985984 | tf_op jit(solution)/shard_map/all_gather | solution.py:498
  95.9 1.0 copy-start.7
  106.6 8.8 %copy-start.8 = (bf16[48,3456]{1,0:T(8,128)(2,1)S(1)}, bf16[48,3456]{1,0:T(8,128)(2,1)}, u32[]{:S(2)}) copy-start(bf16[48,3456]{1,0:T(8,128)(2,1)} %reduce-scatter.2.cloned.1.call-done.grad_ref) | copy-start | bytes 995332
  106.6 52.1 %all-to-all-start.2 = ((bf16[64,4,3456]{2,1,0:T(4,128)(2,1)}), bf16[64,4,3456]{2,1,0:T(4,128)(2,1)}, u32[]{:S(2)}, u32[]{:S(2)}) async-start(bf16[64,4,3456]{2,1,0:T(4,128)(2,1)} %get-tuple-element.33), calls=%async_computation.3 | async-start | bytes 3538944 | tf_op jit(solution)/shard_map/all_to_all | solution.py:500
  147.1 1.7 copy-start
  150.1 7.3 %collective-permute-start.1 = (bf16[32,64,256]{2,1,0:T(8,128)(2,1)S(1)}, bf16[32,64,256]{2,1,0:T(8,128)(2,1)S(1)}, u32[]{:S(2)}, u32[]{:S(2)}) collective-permute-start(bf16[32,64,256]{2,1,0:T(8,128)(2,1)S(1)} %get-tuple-element.32), channel_id=1, source_target_pairs={{0,1},{1,0},{2,3},{3,2},{4,5},{5,4},{6,7},{7,6},{8,9},{9,8},{10,11... | collective-permute-start | bytes 3145736 | tf_op jit(solution)/shard_map/ppermute | solution.py:506
  157.4 11.5 %copy-start.1 = (bf16[384,3456]{1,0:T(8,128)(2,1)S(1)}, bf16[384,3456]{1,0:T(8,128)(2,1)}, u32[]{:S(2)}) copy-start(bf16[384,3456]{1,0:T(8,128)(2,1)} %all-gather.2.cloned.1.call-done.gathered_ref) | copy-start | bytes 7962628
  158.7 36.3 %all-to-all-start.3 = ((bf16[32,64,256]{2,1,0:T(8,128)(2,1)}), bf16[32,64,256]{2,1,0:T(8,128)(2,1)}, u32[]{:S(2)}, u32[]{:S(2)}) async-start(bf16[32,64,256]{2,1,0:T(8,128)(2,1)} %add_convert_fusion), calls=%async_computation.4 | async-start | bytes 2097152 | tf_op jit(solution)/shard_map/all_to_all | solution.py:510
  168.9 1.2 copy-start.3
  170.1 1.2 copy-start.10
  171.3 1.7 copy-start.6
Sparse Core Ops, SparseCore 0:
  56.7 39.0 reduce-scatter.1
  106.7 40.3 all-gather.1

commit v5 on v4

--- a/solution.py
+++ b/solution.py
@@ -22,6 +22,7 @@
 SHARD = 54
 SHARD_PAD = 56
 TERM_PAD = 64
+LANES = 128
 CHUNK = 192
 STEPS = 4
 ROWS = 32
@@ -276,13 +277,16 @@
         unit = unit_ref[s * OWN_ROWS : (s + 1) * OWN_ROWS, :]
         gain_sum = gain_sum + jnp.sum(rows * unit, axis=0, keepdims=True)
         bias_sum = bias_sum + jnp.sum(rows, axis=0, keepdims=True)
-    totals_ref[...] = jnp.concatenate([gain_sum, bias_sum], axis=0)
+    for n in range(WIDTH // LANES):
+        part = slice(n * LANES, (n + 1) * LANES)
+        totals_ref[n : n + 1, :LANES] = gain_sum[:, part]
+        totals_ref[n : n + 1, LANES:] = bias_sum[:, part]
 
 
 def gain_and_bias(named, unit_sums, grad):
     return pl.pallas_call(
         gain_and_bias_kernel,
-        out_shape=jax.ShapeDtypeStruct((2, WIDTH), f32),
+        out_shape=jax.ShapeDtypeStruct((WIDTH // LANES, 2 * LANES), f32),
         compiler_params=pltpu.CompilerParams(vmem_limit_bytes=8 * MIB),
         name="gain_and_bias",
     )(named, unit_sums, grad)
@@ -412,21 +416,25 @@
     )(core, gathered, mine, other, after)
 
 
-def weight_sum_kernel(parts_ref, weight_ref, totals_ref):
+def weight_sum_kernel(parts_ref, weight_ref, gain_ref, bias_ref):
     total = parts_ref[0].astype(f32)
     for n in range(1, parts_ref.shape[0]):
         total = total + parts_ref[n].astype(f32)
     weight_ref[...] = total[:SHARD]
-    totals_ref[...] = total[SHARD : SHARD + totals_ref.shape[0]]
-
-
-def weight_sum(parts, extra):
+    for n in range(WIDTH // LANES):
+        part = slice(n * LANES, (n + 1) * LANES)
+        gain_ref[part] = total[SHARD + n, :LANES]
+        bias_ref[part] = total[SHARD + n, LANES:]
+
+
+def weight_sum(parts):
     cols = parts.shape[2]
     return pl.pallas_call(
         weight_sum_kernel,
         out_shape=(
             jax.ShapeDtypeStruct((SHARD, cols), f32),
-            jax.ShapeDtypeStruct((extra, cols), f32),
+            jax.ShapeDtypeStruct((WIDTH,), f32),
+            jax.ShapeDtypeStruct((WIDTH,), f32),
         ),
         compiler_params=pltpu.CompilerParams(vmem_limit_bytes=8 * MIB),
         name="weight_sum",
@@ -499,8 +507,7 @@
     totals = gain_and_bias(named, unit_sums, own_grad)
     returned = lax.all_to_all(returning, ("z", "x", "c"), 0, 0, tiled=True)
 
-    totals = lax.psum(totals, "dp").reshape(-1, cols)
-    extra = totals.shape[0]
+    totals = lax.psum(totals, "dp")
     kept, sent, done = weight_terms(core.reshape(1), gathered, proj_grad, totals)
     projected = project(core.reshape(1), gathered, mine, other, done)
     got = lax.ppermute(sent, "c", [(0, 1), (1, 0)])
@@ -508,9 +515,8 @@
     terms, returned = lax.optimization_barrier((terms, returned))
     hidden_grad = hidden_gradient(slot_tile, peers, peers.T, gain, hidden, stats, returned)
     parts = lax.all_to_all(terms, ("z", "x"), split_axis=0, concat_axis=0, tiled=True)
-    weight_grad, totals = weight_sum(parts, extra)
-    totals = totals.reshape(2, WIDTH)
-    return projected, weight_grad, hidden_grad, totals[0], totals[1]
+    weight_grad, gain_grad, bias_grad = weight_sum(parts)
+    return projected, weight_grad, hidden_grad, gain_grad, bias_grad
 
 
 def solution(mesh):

time: 207 us -> 206 us (level)
  no operation moved by 1% of the time
where the time goes in v5:
time: 206 us; the launch traced here: 204 us
  waiting for transfers between devices  79.1 us (38%)
  starting transfers between devices  48.3 us (23%)
  Pallas kernels  25.9 us (13%)
  blocking collectives  24.8 us (12%)
  between operations  15.1 us (7%)
  local copies, waits for them, and re-layouts  8.41 us (4%)
  other arithmetic  2.06 us (1%)
    reduce_scatter x1, waiting for transfers between devices, shards(): own_grad = lax.psum_scatter(row_part, 'dp', scatter_dimension=0, tiled=True)  32.2 us
    psum x1, blocking collectives, shards(): totals = lax.psum(totals, 'dp')  24.8 us
    all_to_all x1, waiting for transfers between devices, shards(): lax.all_to_all(terms, ('z', 'x'), split_axis=0, concat_axis=0, tiled=True)  15 us
    all_to_all x1, waiting for transfers between devices, shards(): lax.all_to_all(copies, ('z', 'x'), split_axis=0, concat_axis=0, tiled=True)  14.6 us
    all_to_all x1, starting transfers between devices, shards(): lax.all_to_all(copies, ('z', 'x'), split_axis=0, concat_axis=0, tiled=True)  13.7 us
    all_to_all x1, starting transfers between devices, shards(): lax.all_to_all(terms, ('z', 'x'), split_axis=0, concat_axis=0, tiled=True)  10.1 us
    all_to_all x1, starting transfers between devices, shards(): returned = lax.all_to_all(returning, ('z', 'x', 'c'), 0, 0, tiled=True)  8.58 us
    pallas_call x1, Pallas kernels, pool_tokens(): pl.pallas_call(pool_kernel, grid=(STEPS,), in_specs=[pl.BlockSpec(memory_...  8.3 us
  transfers between devices with their start and end apart: 8, of which 7 were waited for; matrix products, arithmetic and copies ran while one was open for 2% of the time, Pallas kernels for 10%

profile of v5, /device:TPU:1, one launch (start us, length us, event | category | flops | bytes accessed | tf_op | source)
XLA Modules:
  0.0 203.8 jit_solution(6710589059091100214)
XLA Ops:
  8.0 0.7 copy-done.12
  8.7 1.0 shard_copies.1
  9.7 13.7 %all-to-all-start = ((bf16[32,56,256]{2,1,0:T(8,128)(2,1)}), bf16[32,56,256]{2,1,0:T(8,128)(2,1)S(1)}, u32[]{:S(2)}, u32[]{:S(2)}) async-start(bf16[32,56,256]{2,1,0:T(8,128)(2,1)} %shard_copies.1), calls=%async_computation | async-start | bytes 1835008 | tf_op jit(solution)/shard_map/all_to_all | solution.py:473
  24.0 8.3 %pool_tokens.1 = (bf16[64,4,3456]{2,1,0:T(4,128)(2,1)}, f32[768,128]{1,0:T(8,128)S(1)}) custom-call(s32[1]{0:T(128)S(6)} %copy.35.tile_ref, s32[4,256]{1,0:T(4,128)S(1)} %pad.4.clone.peer_row_ref, s32[256,4]{1,0:T(8,128)S(1)} %pad_bitcast_fusion.peer_col_ref, bf16[1,729,1152]{2,1,0:T(8,128)(2,1)S(1)} %copy-done.5), custom_call_target="tpu_custom_call" | custom-call | flops 8000000000 | bytes 24000000 | tf_op jit(solution)/shard_map/pool_tokens/pallas_call | solution.py:148
  32.3 14.6 %all-to-all-done.mine_ref = bf16[32,56,256]{2,1,0:T(8,128)(2,1)S(1)} async-done(((bf16[32,56,256]{2,1,0:T(8,128)(2,1)}), bf16[32,56,256]{2,1,0:T(8,128)(2,1)S(1)}, u32[]{:S(2)}, u32[]{:S(2)}) %all-to-all-start) | async-done | bytes 917536 | tf_op jit(solution)/shard_map/all_to_all | solution.py:473
  46.9 5.0 %collective-permute-start = (bf16[32,56,256]{2,1,0:T(8,128)(2,1)S(1)}, bf16[32,56,256]{2,1,0:T(8,128)(2,1)S(1)}, u32[]{:S(2)}, u32[]{:S(2)}) collective-permute-start(bf16[32,56,256]{2,1,0:T(8,128)(2,1)S(1)} %all-to-all-done.mine_ref), channel_id=1, source_target_pairs={{0,1},{1,0},{2,3},{3,2},{4,5},{5,4},{6,7},{7,6},{8,9},{9,8},{10,11... | collective-permute-start | bytes 2752520 | tf_op jit(solution)/shard_map/ppermute | solution.py:476
  51.9 2.1 %collective-permute-done.other_ref = bf16[32,56,256]{2,1,0:T(8,128)(2,1)S(1)} collective-permute-done((bf16[32,56,256]{2,1,0:T(8,128)(2,1)S(1)}, bf16[32,56,256]{2,1,0:T(8,128)(2,1)S(1)}, u32[]{:S(2)}, u32[]{:S(2)}) %collective-permute-start) | collective-permute-done | bytes 917536 | tf_op jit(solution)/shard_map/ppermute | solution.py:476
  53.9 1.0 row_grad_part.1
  55.0 1.5 copy-done.4
  56.6 5.8 %all-to-all-start.1 = ((bf16[64,4,3456]{2,1,0:T(4,128)(2,1)}), bf16[64,4,3456]{2,1,0:T(4,128)(2,1)S(1)}, u32[]{:S(2)}, u32[]{:S(2)}) async-start(bf16[64,4,3456]{2,1,0:T(4,128)(2,1)} %get-tuple-element.26), calls=%async_computation.1 | async-start | bytes 3538944 | tf_op jit(solution)/shard_map/all_to_all | solution.py:475
  63.1 0.2 select_reduce_fusion
  63.9 32.2 %reduce-scatter.2.cloned.1.call-done.grad_ref = bf16[48,3456]{1,0:T(8,128)(2,1)} async-done(((bf16[384,3456]{1,0:T(8,128)(2,1)}), bf16[48,3456]{1,0:T(8,128)(2,1)}) %reduce-scatter.2.cloned.1.call-update) | async-done | bytes 331792 | tf_op jit(solution)/shard_map/reduce_scatter | solution.py:479
  96.1 1.0 copy-done.7
  97.1 2.0 returning_blocks.1
  99.1 6.2 %all-to-all-done.1.arrived_ref = bf16[64,4,3456]{2,1,0:T(4,128)(2,1)S(1)} async-done(((bf16[64,4,3456]{2,1,0:T(4,128)(2,1)}), bf16[64,4,3456]{2,1,0:T(4,128)(2,1)S(1)}, u32[]{:S(2)}, u32[]{:S(2)}) %all-to-all-start.1) | async-done | bytes 1769504 | tf_op jit(solution)/shard_map/all_to_all | solution.py:475
  105.3 1.2 owned_features.1
  106.6 8.6 %all-to-all-start.2 = ((bf16[64,4,3456]{2,1,0:T(4,128)(2,1)}), bf16[64,4,3456]{2,1,0:T(4,128)(2,1)}, u32[]{:S(2)}, u32[]{:S(2)}) async-start(bf16[64,4,3456]{2,1,0:T(4,128)(2,1)} %get-tuple-element.34), calls=%async_computation.3 | async-start | bytes 3538944 | tf_op jit(solution)/shard_map/all_to_all | solution.py:508
  115.2 0.2 gain_and_bias.1
  115.4 24.8 %psum.7.totals_ref = f32[9,256]{1,0:T(8,128)S(1)} all-reduce(f32[9,256]{1,0:T(8,128)S(1)} %gain_and_bias.1), channel_id=1, replica_groups=mesh['dp'=8,'z'=8,'x'=4,'c'=2] {'dp'}, use_global_device_ids=true, to_apply=%region_4.5 | all-reduce | flops 2304 | bytes 18432 | tf_op jit(solution)/shard_map/psum | solution.py:510
  140.2 6.8 %all-gather.2.cloned.1.call-done.gathered_ref = bf16[384,3456]{1,0:T(8,128)(2,1)} async-done(((bf16[48,3456]{1,0:T(8,128)(2,1)}), bf16[384,3456]{1,0:T(8,128)(2,1)}) %all-gather.2.cloned.1.call-update) | async-done | bytes 2654224 | tf_op jit(solution)/shard_map/all_gather | solution.py:506
  147.0 1.7 copy-done
  148.8 1.2 weight_terms.1
  150.0 5.0 %collective-permute-start.1 = (bf16[32,64,256]{2,1,0:T(8,128)(2,1)S(1)}, bf16[32,64,256]{2,1,0:T(8,128)(2,1)S(1)}, u32[]{:S(2)}, u32[]{:S(2)}) collective-permute-start(bf16[32,64,256]{2,1,0:T(8,128)(2,1)S(1)} %get-tuple-element.33), channel_id=1, source_target_pairs={{0,1},{1,0},{2,3},{3,2},{4,5},{5,4},{6,7},{7,6},{8,9},{9,8},{10,11... | collective-permute-start | bytes 3145736 | tf_op jit(solution)/shard_map/ppermute | solution.py:513
  155.1 2.3 %collective-permute-done.1 = bf16[32,64,256]{2,1,0:T(8,128)(2,1)S(1)} collective-permute-done((bf16[32,64,256]{2,1,0:T(8,128)(2,1)S(1)}, bf16[32,64,256]{2,1,0:T(8,128)(2,1)S(1)}, u32[]{:S(2)}, u32[]{:S(2)}) %collective-permute-start.1) | collective-permute-done | bytes 1048608 | tf_op jit(solution)/shard_map/ppermute | solution.py:513
  157.3 1.4 add_convert_fusion
  158.7 10.1 %all-to-all-start.3 = ((bf16[32,64,256]{2,1,0:T(8,128)(2,1)}), bf16[32,64,256]{2,1,0:T(8,128)(2,1)}, u32[]{:S(2)}, u32[]{:S(2)}) async-start(bf16[32,64,256]{2,1,0:T(8,128)(2,1)} %add_convert_fusion), calls=%async_computation.4 | async-start | bytes 2097152 | tf_op jit(solution)/shard_map/all_to_all | solution.py:517
  168.8 1.2 copy-done.3
  170.0 1.2 copy-done.10
  171.2 1.7 project.1
  172.9 7.1 %hidden_gradient.1 = bf16[1,729,1152]{2,1,0:T(8,128)(2,1)} custom-call(s32[1]{0:T(128)S(6)} %copy.35.tile_ref, s32[4,256]{1,0:T(4,128)S(1)} %pad.4.clone.peer_row_ref, s32[256,4]{1,0:T(8,128)S(1)} %pad_bitcast_fusion.peer_col_ref, f32[1,1152]{1,0:T(1,128)S(1)} %reshape.128.gain_ref, bf16[1,729,1152]{2,1,0:T(8,128)(2,1)S(1)} %copy-done.6, ...), custom_call_target="tpu_custom_call" | custom-call | tf_op jit(solution)/shard_map/hidden_gradient/pallas_call | solution.py:345
  180.0 15.0 %all-to-all-done.3.parts_ref = bf16[32,64,256]{2,1,0:T(8,128)(2,1)} async-done(((bf16[32,64,256]{2,1,0:T(8,128)(2,1)}), bf16[32,64,256]{2,1,0:T(8,128)(2,1)}, u32[]{:S(2)}, u32[]{:S(2)}) %all-to-all-start.3) | async-done | bytes 1048608 | tf_op jit(solution)/shard_map/all_to_all | solution.py:517
  195.0 2.0 weight_sum.1
  (55 shorter events, 1.9 us)
Async XLA Ops:
  7.2 16.8 %copy-start.5 = (bf16[1,729,1152]{2,1,0:T(8,128)(2,1)S(1)}, bf16[1,729,1152]{2,1,0:T(8,128)(2,1)}, u32[]{:S(2)}) copy-start(bf16[1,729,1152]{2,1,0:T(8,128)(2,1)} %hidden_ref.3) | copy-start | bytes 5038852
  7.9 0.7 copy-start.12
  8.7 14.8 %copy-start.13 = (s32[1,4,27,9]{2,1,3,0:T(4,128)S(1)}, s32[1,4,27,9]{2,1,3,0:T(4,128)}, u32[]{:S(2)}) copy-start(s32[1,4,27,9]{2,1,3,0:T(4,128)} %param.11) | copy-start | bytes 11668
  9.7 37.2 %all-to-all-start = ((bf16[32,56,256]{2,1,0:T(8,128)(2,1)}), bf16[32,56,256]{2,1,0:T(8,128)(2,1)S(1)}, u32[]{:S(2)}, u32[]{:S(2)}) async-start(bf16[32,56,256]{2,1,0:T(8,128)(2,1)} %shard_copies.1), calls=%async_computation | async-start | bytes 1835008 | tf_op jit(solution)/shard_map/all_to_all | solution.py:473
  23.4 72.7 %reduce-scatter.2.cloned.1.call-start = ((), (), s32[]{:S(2)}) async-start(), calls=%async_computation.5 | async-start | bytes 2985984 | tf_op jit(solution)/shard_map/reduce_scatter | solution.py:479
  24.0 30.0 %copy-start.11 = (bf16[1,384,256]{2,1,0:T(8,128)(2,1)S(1)}, bf16[1,384,256]{2,1,0:T(8,128)(2,1)}, u32[]{:S(2)}) copy-start(bf16[1,384,256]{2,1,0:T(8,128)(2,1)} %grad_ref.3) | copy-start | bytes 589828
  46.9 8.1 %copy-start.2 = (bf16[32,56,256]{2,1,0:T(8,128)(2,1)}, bf16[32,56,256]{2,1,0:T(8,128)(2,1)S(1)}, u32[]{:S(2)}) copy-start(bf16[32,56,256]{2,1,0:T(8,128)(2,1)S(1)} %all-to-all-done.mine_ref) | copy-start | bytes 2752516
  46.9 7.1 %collective-permute-start = (bf16[32,56,256]{2,1,0:T(8,128)(2,1)S(1)}, bf16[32,56,256]{2,1,0:T(8,128)(2,1)S(1)}, u32[]{:S(2)}, u32[]{:S(2)}) collective-permute-start(bf16[32,56,256]{2,1,0:T(8,128)(2,1)S(1)} %all-to-all-done.mine_ref), channel_id=1, source_target_pairs={{0,1},{1,0},{2,3},{3,2},{4,5},{5,4},{6,7},{7,6},{8,9},{9,8},{10,11... | collective-permute-start | bytes 2752520 | tf_op jit(solution)/shard_map/ppermute | solution.py:476
  53.9 1.1 copy-start.9
  55.0 1.5 copy-start.4
  56.5 5.9 %copy-start.14 = (f32[1152]{0:T(1024)S(1)}, f32[1152]{0:T(1024)}, u32[]{:S(2)}) copy-start(f32[1152]{0:T(1024)} %param.8) | copy-start | bytes 13828
  56.6 5.9 %copy-start.15 = (f32[1152]{0:T(1024)S(1)}, f32[1152]{0:T(1024)}, u32[]{:S(2)}) copy-start(f32[1152]{0:T(1024)} %param.9) | copy-start | bytes 13828
  56.6 48.7 %all-to-all-start.1 = ((bf16[64,4,3456]{2,1,0:T(4,128)(2,1)}), bf16[64,4,3456]{2,1,0:T(4,128)(2,1)S(1)}, u32[]{:S(2)}, u32[]{:S(2)}) async-start(bf16[64,4,3456]{2,1,0:T(4,128)(2,1)} %get-tuple-element.26), calls=%async_computation.1 | async-start | bytes 3538944 | tf_op jit(solution)/shard_map/all_to_all | solution.py:475
  62.4 84.7 %all-gather.2.cloned.1.call-start = ((), (), s32[]{:S(2)}) async-start(), calls=%async_computation.6 | async-start | bytes 2985984 | tf_op jit(solution)/shard_map/all_gather | solution.py:506
  96.1 1.0 copy-start.7
  106.6 8.6 %copy-start.8 = (bf16[48,3456]{1,0:T(8,128)(2,1)S(1)}, bf16[48,3456]{1,0:T(8,128)(2,1)}, u32[]{:S(2)}) copy-start(bf16[48,3456]{1,0:T(8,128)(2,1)} %reduce-scatter.2.cloned.1.call-done.grad_ref) | copy-start | bytes 995332
  106.6 52.1 %all-to-all-start.2 = ((bf16[64,4,3456]{2,1,0:T(4,128)(2,1)}), bf16[64,4,3456]{2,1,0:T(4,128)(2,1)}, u32[]{:S(2)}, u32[]{:S(2)}) async-start(bf16[64,4,3456]{2,1,0:T(4,128)(2,1)} %get-tuple-element.34), calls=%async_computation.3 | async-start | bytes 3538944 | tf_op jit(solution)/shard_map/all_to_all | solution.py:508
  147.0 1.7 copy-start
  150.0 7.3 %collective-permute-start.1 = (bf16[32,64,256]{2,1,0:T(8,128)(2,1)S(1)}, bf16[32,64,256]{2,1,0:T(8,128)(2,1)S(1)}, u32[]{:S(2)}, u32[]{:S(2)}) collective-permute-start(bf16[32,64,256]{2,1,0:T(8,128)(2,1)S(1)} %get-tuple-element.33), channel_id=1, source_target_pairs={{0,1},{1,0},{2,3},{3,2},{4,5},{5,4},{6,7},{7,6},{8,9},{9,8},{10,11... | collective-permute-start | bytes 3145736 | tf_op jit(solution)/shard_map/ppermute | solution.py:513
  157.3 11.5 %copy-start.1 = (bf16[384,3456]{1,0:T(8,128)(2,1)S(1)}, bf16[384,3456]{1,0:T(8,128)(2,1)}, u32[]{:S(2)}) copy-start(bf16[384,3456]{1,0:T(8,128)(2,1)} %all-gather.2.cloned.1.call-done.gathered_ref) | copy-start | bytes 7962628
  158.7 36.3 %all-to-all-start.3 = ((bf16[32,64,256]{2,1,0:T(8,128)(2,1)}), bf16[32,64,256]{2,1,0:T(8,128)(2,1)}, u32[]{:S(2)}, u32[]{:S(2)}) async-start(bf16[32,64,256]{2,1,0:T(8,128)(2,1)} %add_convert_fusion), calls=%async_computation.4 | async-start | bytes 2097152 | tf_op jit(solution)/shard_map/all_to_all | solution.py:517
  168.8 1.2 copy-start.3
  170.0 1.2 copy-start.10
  171.2 1.7 copy-start.6
Sparse Core Ops, SparseCore 0:
  56.7 39.3 reduce-scatter.1
  106.7 40.3 all-gather.1
